TPU v7x, 32 devices: a whole 2x2x4 slice. The times are simulated.
32 devices in a mesh: dp: 8 (over z, y), tensor: 4 (over x, core).
Axes of the slice: x: 2, y: 2, z: 4, core: 2. Of those that a mesh axis runs over, the one named last changes fastest.
Arguments:
- tokens_in: bfloat16 [6144, 2048], P(('dp', 'tensor')), may hold values from -6 to 6
- lengths: int32 [8, 2], P('dp'), may hold values from 64 to 640, as said below
- norm_gain: bfloat16 [2, 2048], P(None, ('dp', 'tensor')), may hold values from 0.5 to 1.5
- norm_bias: bfloat16 [2, 2048], P(None, ('dp', 'tensor')), may hold values from -2 to 2
- proj_weight: bfloat16 [2, 2048, 3, 2048], P(None, 'dp', None, 'tensor'), may hold values from -0.125 to 0.125
- proj_bias: bfloat16 [2, 3, 4, 512], P(None, None, 'tensor', 'dp'), may hold values from -3 to 3
- dense_weight: bfloat16 [2, 2048, 2048], P(None, 'tensor', 'dp'), may hold values from -2 to 2
- dense_bias: bfloat16 [2, 2048], P(None, ('dp', 'tensor')), may hold values from -3 to 3
- up_weight: bfloat16 [2, 2048, 8192], P(None, 'dp', 'tensor'), may hold values from -0.125 to 0.125
- up_bias: bfloat16 [2, 4, 2048], P(None, 'tensor', 'dp'), may hold values from -3 to 3
- down_weight: bfloat16 [2, 8192, 2048], P(None, 'tensor', 'dp'), may hold values from -0.0625 to 0.0625
- down_bias: bfloat16 [2, 2048], P(None, ('dp', 'tensor')), may hold values from -3 to 3
- cotangent: bfloat16 [6144, 2048], P(('dp', 'tensor')), may hold values from -6 to 6
Outputs:
- activations: float32 [6144, 2048], P(('dp', 'tensor'))
- input_grad: float32 [6144, 2048], P(('dp', 'tensor'))
- grad_norm_gain: float32 [2, 2048], P(None, ('dp', 'tensor'))
- grad_norm_bias: float32 [2, 2048], P(None, ('dp', 'tensor'))
- grad_proj_weight: float32 [2, 2048, 3, 2048], P(None, 'dp', None, 'tensor')
- grad_proj_bias: float32 [2, 3, 4, 512], P(None, None, 'tensor', 'dp')
- grad_dense_weight: float32 [2, 2048, 2048], P(None, 'tensor', 'dp')
- grad_dense_bias: float32 [2, 2048], P(None, ('dp', 'tensor'))
- grad_up_weight: float32 [2, 2048, 8192], P(None, 'dp', 'tensor')
- grad_up_bias: float32 [2, 4, 2048], P(None, 'tensor', 'dp')
- grad_down_weight: float32 [2, 8192, 2048], P(None, 'tensor', 'dp')
- grad_down_bias: float32 [2, 2048], P(None, ('dp', 'tensor'))
Inputs may be any that keep to these rules, and one draw needn't show every extreme that they name: lengths[g] are the lengths of the two sequences of data group g in the order in which they are packed, each padded to whole blocks of 128 tokens; the two fit in 6 blocks.
All inputs are finite; a program needn't handle non-finite values.
Results may differ from a plain program's by a relative error of at most 0.018.
Values may be sent and summed in bfloat16 or wider, within the bound.
No kernel may reach another device: no remote copies, remote signals or barrier semaphores. Data moves between devices by JAX's collectives and lax.ppermute only.
A program may use at most 256 MiB of HBM per device.

v0:
```python
from functools import partial
import math

import jax
import jax.numpy as jnp
from jax import lax
from jax.sharding import PartitionSpec as P

HEAD_DIM = 64
ROT = 32
BLOCK = 128


neg_large = -1e30


def norm_rows(rows, scale, shift):
    centre = rows - jnp.mean(rows, axis=-1, keepdims=True)
    spread = jnp.mean(centre * centre, axis=-1, keepdims=True)
    return centre * lax.rsqrt(spread + 1e-05) * scale + shift


def layout(lens, total, block):
    steps_index = jnp.arange(total, dtype=jnp.int32)
    blocks_first = (lens[0] + block - 1) // block
    second_start = blocks_first * block
    in_first = steps_index < lens[0]
    in_second = (steps_index >= second_start) & (steps_index < second_start + lens[1])
    segment = jnp.where(in_first, 0, jnp.where(in_second, 1, steps_index + 2))
    position = jnp.where(in_first, steps_index, jnp.where(in_second, steps_index - second_start, 0))
    return (segment, position)


def rotary_tables(position):
    half_rot = ROT // 2
    freqs = 10000.0 ** (-(jnp.arange(half_rot).astype(jnp.float32) * 2.0) / ROT)
    angles = position.astype(jnp.float32)[:, None] * freqs[None, :]
    return (jnp.cos(angles)[:, None, :], jnp.sin(angles)[:, None, :])


def rotate(field, cosine, sine):
    half_rot = cosine.shape[-1]
    first = field[..., :half_rot]
    second = field[..., half_rot : 2 * half_rot]
    remain = field[..., 2 * half_rot :]
    return jnp.concatenate(
        [first * cosine - second * sine, second * cosine + first * sine, remain], axis=-1
    )


def rotate_back(field, cosine, sine):
    half_rot = cosine.shape[-1]
    first = field[..., :half_rot]
    second = field[..., half_rot : 2 * half_rot]
    remain = field[..., 2 * half_rot :]
    return jnp.concatenate(
        [first * cosine + second * sine, second * cosine - first * sine, remain], axis=-1
    )


def rows_product(left, right):
    return lax.dot_general(
        left, right, (((0,), (0,)), ((), ())), preferred_element_type=jnp.float32
    )


def cols_product(left, right):
    return lax.dot_general(
        left, right, (((1,), (1,)), ((), ())), preferred_element_type=jnp.float32
    )


def heads_first(field):
    return jnp.transpose(field, (1, 0, 2))


def attention_forward(query16, key16, value16, allowed, scale):

    def one_head(pieces):
        query_head, key_head, value_head = pieces
        scores = cols_product(query_head, key_head) * scale
        masked = jnp.where(allowed, scores, neg_large)
        top = jnp.max(masked, axis=1, keepdims=True)
        expo = jnp.exp(masked - top)
        total = jnp.sum(expo, axis=1, keepdims=True)
        probs16 = (expo / total).astype(jnp.bfloat16)
        result = jnp.dot(probs16, value_head, preferred_element_type=jnp.float32)
        return (result.astype(jnp.bfloat16), top[:, 0] + jnp.log(total[:, 0]))

    attended, log_sums = lax.map(
        one_head, (heads_first(query16), heads_first(key16), heads_first(value16))
    )
    return (heads_first(attended), log_sums)


def attention_backward(query16, key16, value16, grad16, log_sums, allowed, scale):

    def one_head(pieces):
        query_head, key_head, value_head, grad_head, sums_head = pieces
        scores = cols_product(query_head, key_head) * scale
        masked = jnp.where(allowed, scores, neg_large)
        probs = jnp.exp(masked - sums_head[:, None])
        value_grad = rows_product(probs.astype(jnp.bfloat16), grad_head)
        prob_grad = cols_product(grad_head, value_head)
        score_grad = (
            probs * (prob_grad - jnp.sum(probs * prob_grad, axis=1, keepdims=True))
        ).astype(jnp.bfloat16)
        query_grad = jnp.dot(score_grad, key_head, preferred_element_type=jnp.float32) * scale
        key_grad = rows_product(score_grad, query_head) * scale
        return (query_grad, key_grad, value_grad)

    query_grad, key_grad, value_grad = lax.map(
        one_head,
        (
            heads_first(query16),
            heads_first(key16),
            heads_first(value16),
            heads_first(grad16),
            log_sums,
        ),
    )
    return (heads_first(query_grad), heads_first(key_grad), heads_first(value_grad))


def fetch_forward(
    proj_weight, proj_bias, dense_weight, up_weight, up_bias, down_weight, layer_index
):
    return (
        lax.all_gather(proj_weight[layer_index], "dp", axis=0, tiled=True),
        lax.all_gather(proj_bias[layer_index], "dp", axis=2, tiled=True),
        lax.all_gather(dense_weight[layer_index], "dp", axis=1, tiled=True),
        lax.all_gather(up_weight[layer_index], "dp", axis=0, tiled=True),
        lax.all_gather(up_bias[layer_index], "dp", axis=1, tiled=True),
        lax.all_gather(down_weight[layer_index], "dp", axis=1, tiled=True),
    )


def fetch_again(proj_weight, proj_bias, dense_weight, up_weight, up_bias, down_weight, layer_index):
    return (
        lax.all_gather(proj_weight[layer_index], "dp", axis=0, tiled=True),
        lax.all_gather(proj_bias[layer_index], "dp", axis=2, tiled=True),
        lax.all_gather(dense_weight[layer_index], "dp", axis=1, tiled=True),
        lax.all_gather(up_weight[layer_index], "dp", axis=0, tiled=True),
        lax.all_gather(up_bias[layer_index], "dp", axis=1, tiled=True),
        lax.all_gather(down_weight[layer_index], "dp", axis=1, tiled=True),
    )


def layer_forward(
    stream, scale_row, shift_row, dense_shift, down_shift, fetched, allowed, cosine, sine, scale
):
    proj_full, proj_shift, dense_full, up_full, up_shift, down_full = fetched
    width = stream.shape[1]
    normed = norm_rows(stream, scale_row, shift_row).astype(jnp.bfloat16)
    gathered = lax.all_gather(normed, "tensor", axis=0, tiled=True)
    group_tokens = gathered.shape[0]
    local_heads = proj_full.shape[2] // HEAD_DIM
    mixed = jnp.dot(
        gathered, proj_full.reshape(width, -1), preferred_element_type=jnp.float32
    ) + proj_shift.reshape(-1).astype(jnp.float32)
    mixed = mixed.reshape(group_tokens, 3, local_heads, HEAD_DIM)
    query16 = rotate(mixed[:, 0], cosine, sine).astype(jnp.bfloat16)
    key16 = rotate(mixed[:, 1], cosine, sine).astype(jnp.bfloat16)
    value16 = mixed[:, 2].astype(jnp.bfloat16)
    attended, log_sums = attention_forward(query16, key16, value16, allowed, scale)
    attended = attended.reshape(group_tokens, -1)
    hidden_pre = jnp.dot(gathered, up_full, preferred_element_type=jnp.float32) + up_shift.reshape(
        -1
    ).astype(jnp.float32)
    hidden16 = jax.nn.gelu(hidden_pre, approximate=True).astype(jnp.bfloat16)
    branch = lax.psum_scatter(
        (
            jnp.dot(attended, dense_full, preferred_element_type=jnp.float32)
            + jnp.dot(hidden16, down_full, preferred_element_type=jnp.float32)
        ).astype(jnp.bfloat16),
        "tensor",
        scatter_dimension=0,
        tiled=True,
    ).astype(jnp.float32)
    result = stream + branch + dense_shift + down_shift
    kept = (gathered, query16, key16, value16, attended, log_sums, hidden_pre, hidden16)
    return (result, kept)


def layer_backward(
    grad_in, stream_in, scale_row, shift_row, fetched, kept, allowed, cosine, sine, scale
):
    proj_full, proj_shift, dense_full, up_full, up_shift, down_full = fetched
    gathered, query16, key16, value16, attended, log_sums, hidden_pre, hidden16 = kept
    width = stream_in.shape[1]
    group_tokens = gathered.shape[0]
    local_heads = proj_full.shape[2] // HEAD_DIM
    bias_grad = jnp.sum(grad_in, axis=0)
    gathered_grad = lax.all_gather(grad_in.astype(jnp.bfloat16), "tensor", axis=0, tiled=True)
    dense_wgrad = rows_product(attended, gathered_grad)
    down_wgrad = rows_product(hidden16, gathered_grad)
    attended_grad = cols_product(gathered_grad, dense_full).astype(jnp.bfloat16)
    hidden_grad = cols_product(gathered_grad, down_full)
    unused, gelu_pull = jax.vjp(partial(jax.nn.gelu, approximate=True), hidden_pre)
    pre_grad = gelu_pull(hidden_grad)[0].astype(jnp.bfloat16)
    attended_heads = attended_grad.reshape(group_tokens, local_heads, HEAD_DIM)
    query_grad, key_grad, value_grad = attention_backward(
        query16, key16, value16, attended_heads, log_sums, allowed, scale
    )
    query_grad = rotate_back(query_grad, cosine, sine)
    key_grad = rotate_back(key_grad, cosine, sine)
    mixed_grad = (
        jnp.stack([query_grad, key_grad, value_grad], axis=1)
        .astype(jnp.bfloat16)
        .reshape(group_tokens, -1)
    )
    proj_wgrad = rows_product(gathered, mixed_grad).reshape(width, 3, -1)
    proj_bgrad = jnp.sum(mixed_grad, axis=0, dtype=jnp.float32).reshape(3, 1, -1)
    up_wgrad = rows_product(gathered, pre_grad)
    up_bgrad = jnp.sum(pre_grad, axis=0, dtype=jnp.float32)[None, :]
    proj_flat = proj_full.reshape(width, -1)
    normed_grad = lax.psum_scatter(
        (cols_product(mixed_grad, proj_flat) + cols_product(pre_grad, up_full)).astype(
            jnp.bfloat16
        ),
        "tensor",
        scatter_dimension=0,
        tiled=True,
    ).astype(jnp.float32)
    unused_norm, norm_pull = jax.vjp(norm_rows, stream_in, scale_row, shift_row)
    stream_grad, scale_grad, shift_grad = norm_pull(normed_grad)
    layer_wgrads = (proj_wgrad, proj_bgrad, dense_wgrad, up_wgrad, up_bgrad, down_wgrad)
    return (grad_in + stream_grad, layer_wgrads, (scale_grad, shift_grad, bias_grad))


def shards(
    tokens_in,
    lengths,
    norm_gain,
    norm_bias,
    proj_weight,
    proj_bias,
    dense_weight,
    dense_bias,
    up_weight,
    up_bias,
    down_weight,
    down_bias,
    cotangent,
):
    rows_dev = tokens_in.shape[0]
    group_tokens = rows_dev * lax.axis_size("tensor")
    layer_count = proj_weight.shape[0]
    scale = 1.0 / math.sqrt(HEAD_DIM)
    segment, position = layout(lengths[0], group_tokens, BLOCK)
    token_index = jnp.arange(group_tokens, dtype=jnp.int32)
    allowed = (segment[:, None] == segment[None, :]) & (
        token_index[None, :] <= token_index[:, None]
    )
    cosine, sine = rotary_tables(position)
    gain_full, shift_full, dense_full_bias, down_full_bias = (
        lax.all_gather(norm_gain, ("dp", "tensor"), axis=1, tiled=True),
        lax.all_gather(norm_bias, ("dp", "tensor"), axis=1, tiled=True),
        lax.all_gather(dense_bias, ("dp", "tensor"), axis=1, tiled=True),
        lax.all_gather(down_bias, ("dp", "tensor"), axis=1, tiled=True),
    )
    gain_full = gain_full.astype(jnp.float32)
    shift_full = shift_full.astype(jnp.float32)
    dense_full_bias = dense_full_bias.astype(jnp.float32)
    down_full_bias = down_full_bias.astype(jnp.float32)
    stream = tokens_in.astype(jnp.float32)
    saved = []
    for layer_index in range(layer_count):
        fetched = fetch_forward(
            proj_weight, proj_bias, dense_weight, up_weight, up_bias, down_weight, layer_index
        )
        stream_in = stream
        stream, kept = layer_forward(
            stream,
            gain_full[layer_index],
            shift_full[layer_index],
            dense_full_bias[layer_index],
            down_full_bias[layer_index],
            fetched,
            allowed,
            cosine,
            sine,
            scale,
        )
        saved.append((stream_in, fetched, kept))
    grad_stream = cotangent.astype(jnp.float32)
    weight_grads = [None] * layer_count
    small_grads = [None] * layer_count
    for layer_index in reversed(range(layer_count)):
        stream_in, fetched_fwd, kept = saved[layer_index]
        fetched = fetch_again(
            proj_weight, proj_bias, dense_weight, up_weight, up_bias, down_weight, layer_index
        )
        grad_stream, layer_wgrads, layer_sgrads = layer_backward(
            grad_stream,
            stream_in,
            gain_full[layer_index],
            shift_full[layer_index],
            fetched,
            kept,
            allowed,
            cosine,
            sine,
            scale,
        )
        proj_wg, proj_bg, dense_wg, up_wg, up_bg, down_wg = layer_wgrads
        weight_grads[layer_index] = (
            lax.psum_scatter(
                proj_wg.astype(jnp.bfloat16), "dp", scatter_dimension=0, tiled=True
            ).astype(jnp.float32),
            lax.psum_scatter(
                proj_bg.astype(jnp.bfloat16), "dp", scatter_dimension=2, tiled=True
            ).astype(jnp.float32),
            lax.psum_scatter(
                dense_wg.astype(jnp.bfloat16), "dp", scatter_dimension=1, tiled=True
            ).astype(jnp.float32),
            lax.psum_scatter(
                up_wg.astype(jnp.bfloat16), "dp", scatter_dimension=0, tiled=True
            ).astype(jnp.float32),
            lax.psum_scatter(
                up_bg.astype(jnp.bfloat16), "dp", scatter_dimension=1, tiled=True
            ).astype(jnp.float32),
            lax.psum_scatter(
                down_wg.astype(jnp.bfloat16), "dp", scatter_dimension=1, tiled=True
            ).astype(jnp.float32),
        )
        small_grads[layer_index] = layer_sgrads
    proj_wstack = jnp.stack([weight_grads[index_at][0] for index_at in range(layer_count)])
    proj_bstack = jnp.stack([weight_grads[index_at][1] for index_at in range(layer_count)])
    dense_wstack = jnp.stack([weight_grads[index_at][2] for index_at in range(layer_count)])
    up_wstack = jnp.stack([weight_grads[index_at][3] for index_at in range(layer_count)])
    up_bstack = jnp.stack([weight_grads[index_at][4] for index_at in range(layer_count)])
    down_wstack = jnp.stack([weight_grads[index_at][5] for index_at in range(layer_count)])
    scale_stack = jnp.stack([small_grads[index_at][0] for index_at in range(layer_count)])
    shift_stack = jnp.stack([small_grads[index_at][1] for index_at in range(layer_count)])
    bias_stack = jnp.stack([small_grads[index_at][2] for index_at in range(layer_count)])
    scale_owned, shift_owned, bias_owned = (
        lax.psum_scatter(scale_stack, ("dp", "tensor"), scatter_dimension=1, tiled=True),
        lax.psum_scatter(shift_stack, ("dp", "tensor"), scatter_dimension=1, tiled=True),
        lax.psum_scatter(bias_stack, ("dp", "tensor"), scatter_dimension=1, tiled=True),
    )
    return (
        stream,
        grad_stream,
        scale_owned,
        shift_owned,
        proj_wstack,
        proj_bstack,
        dense_wstack,
        bias_owned,
        up_wstack,
        up_bstack,
        down_wstack,
        bias_owned,
    )


def solution(mesh):
    in_specs = (
        P(("dp", "tensor"), None),
        P("dp", None),
        P(None, ("dp", "tensor")),
        P(None, ("dp", "tensor")),
        P(None, "dp", None, "tensor"),
        P(None, None, "tensor", "dp"),
        P(None, "tensor", "dp"),
        P(None, ("dp", "tensor")),
        P(None, "dp", "tensor"),
        P(None, "tensor", "dp"),
        P(None, "tensor", "dp"),
        P(None, ("dp", "tensor")),
        P(("dp", "tensor"), None),
    )
    out_specs = (
        P(("dp", "tensor"), None),
        P(("dp", "tensor"), None),
        P(None, ("dp", "tensor")),
        P(None, ("dp", "tensor")),
        P(None, "dp", None, "tensor"),
        P(None, None, "tensor", "dp"),
        P(None, "tensor", "dp"),
        P(None, ("dp", "tensor")),
        P(None, "dp", "tensor"),
        P(None, "tensor", "dp"),
        P(None, "tensor", "dp"),
        P(None, ("dp", "tensor")),
    )
    return jax.shard_map(shards, mesh=mesh, in_specs=in_specs, out_specs=out_specs, check_vma=False)
```

profile of v0, /device:TPU:0, one launch (start us, length us, event | category | flops | bytes accessed | tf_op | source)
XLA Modules:
  0.0 2997.1 jit_solution(7094105584548354432)
XLA Ops:
  7.2 43.3 %all-gather.13 = bf16[32,64,2]{1,2,0:T(2,128)(2,1)S(1)} all-gather(bf16[1,64,2]{1,2,0:T(2,128)(2,1)} %bitcast.485), channel_id=1, replica_groups=mesh['dp'=8,'tensor'=4] {'dp','tensor'}, dimensions={0}, use_global_device_ids=true | all-gather | bytes 8448 | tf_op jit(solution)/shard_map/all_gather | solution.py:258
  50.7 36.6 %all-gather.12 = bf16[32,64,2]{1,2,0:T(2,128)(2,1)S(1)} all-gather(bf16[1,64,2]{1,2,0:T(2,128)(2,1)} %bitcast.486), channel_id=1, replica_groups=mesh['dp'=8,'tensor'=4] {'dp','tensor'}, dimensions={0}, use_global_device_ids=true | all-gather | bytes 8448 | tf_op jit(solution)/shard_map/all_gather | solution.py:257
  120.1 31.8 %all-gather.1 = bf16[1,3,1,512]{1,2,0,3:T(2,128)(2,1)S(1)} all-gather(bf16[1,3,1,64]{1,2,0,3:T(2,128)(2,1)S(1)} %copy.134), channel_id=3, replica_groups=mesh['dp'=8,'tensor'=4] {'dp'}, dimensions={3}, use_global_device_ids=true | all-gather | bytes 3456 | tf_op jit(solution)/shard_map/all_gather | solution.py:130
  153.8 69.5 %all-gather.37.cloned.1.call-done = bf16[1,2048,3,512]{1,3,2,0:T(8,128)(2,1)} async-done(((bf16[1,256,3,512]{1,3,2,0:T(8,128)(2,1)}), bf16[1,2048,3,512]{1,3,2,0:T(8,128)(2,1)}) %all-gather.37.cloned.1.call-update) | async-done | bytes 6291472 | tf_op jit(solution)/shard_map/all_gather | solution.py:129
  277.2 72.0 %all-gather.41.cloned.1.call-done = bf16[1,2048,2048]{2,1,0:T(8,128)(2,1)} async-done(((bf16[1,256,2048]{2,1,0:T(8,128)(2,1)}), bf16[1,2048,2048]{2,1,0:T(8,128)(2,1)}) %all-gather.41.cloned.1.call-update) | async-done | bytes 8388624 | tf_op jit(solution)/shard_map/all_gather | solution.py:132
  360.8 114.4 %all-gather.43.cloned.1.call-done = bf16[1,2048,2048]{2,1,0:T(8,128)(2,1)} async-done(((bf16[1,2048,256]{2,1,0:T(8,128)(2,1)}), bf16[1,2048,2048]{2,1,0:T(8,128)(2,1)}) %all-gather.43.cloned.1.call-update) | async-done | bytes 8388624 | tf_op jit(solution)/shard_map/all_gather | solution.py:134
  489.1 37.9 %all-gather.39.cloned.1.call-done = bf16[1,512,2048]{2,1,0:T(8,128)(2,1)} async-done(((bf16[1,512,256]{2,1,0:T(8,128)(2,1)}), bf16[1,512,2048]{2,1,0:T(8,128)(2,1)}) %all-gather.39.cloned.1.call-update) | async-done | bytes 2097168 | tf_op jit(solution)/shard_map/all_gather | solution.py:131
  536.8 38.4 %all-gather.15 = bf16[32,64,2]{1,2,0:T(2,128)(2,1)S(1)} all-gather(bf16[1,64,2]{1,2,0:T(2,128)(2,1)S(1)} %bitcast.487), channel_id=1, replica_groups=mesh['dp'=8,'tensor'=4] {'dp','tensor'}, dimensions={0}, use_global_device_ids=true | all-gather | bytes 8448 | tf_op jit(solution)/shard_map/all_gather | solution.py:260
  575.3 36.5 %all-gather.14 = bf16[32,64,2]{1,2,0:T(2,128)(2,1)S(1)} all-gather(bf16[1,64,2]{1,2,0:T(2,128)(2,1)S(1)} %bitcast.488), channel_id=1, replica_groups=mesh['dp'=8,'tensor'=4] {'dp','tensor'}, dimensions={0}, use_global_device_ids=true | all-gather | bytes 8448 | tf_op jit(solution)/shard_map/all_gather | solution.py:259
  619.6 30.7 %all-gather.7 = bf16[1,3,1,512]{1,2,0,3:T(2,128)(2,1)S(1)} all-gather(bf16[1,3,1,64]{1,2,0,3:T(2,128)(2,1)S(1)} %copy.136), channel_id=9, replica_groups=mesh['dp'=8,'tensor'=4] {'dp'}, dimensions={3}, use_global_device_ids=true | all-gather | bytes 3456 | tf_op jit(solution)/shard_map/all_gather | solution.py:130
  672.6 83.3 %all-gather.45.cloned.1.call-done = bf16[1,2048,3,512]{1,3,2,0:T(8,128)(2,1)} async-done(((bf16[1,256,3,512]{1,3,2,0:T(8,128)(2,1)}), bf16[1,2048,3,512]{1,3,2,0:T(8,128)(2,1)}) %all-gather.45.cloned.1.call-update) | async-done | bytes 6291472 | tf_op jit(solution)/shard_map/all_gather | solution.py:129
  755.8 28.8 all-gather.31.cloned.1.call-done
  811.1 28.9 while.57
  842.7 66.0 %while.58 = (s32[]{:T(128)}, f32[8,768,64]{1,2,0:T(8,128)}, f32[8,768,64]{1,2,0:T(8,128)}, bf16[8,768,64]{1,2,0:T(8,128)(2,1)S(1)}, bf16[8,768,64]{2,1,0:T(8,128...) while((s32[]{:T(128)}, f32[8,768,64]{1,2,0:T(8,128)}, ...), condition=%wide.region_16.17_spmd.clone, body=%wide.region_14.16_spmd.clone.sunk | while | flops 384662784 | bytes 19690616 | solution.py:112
  936.7 100.9 %all-gather.51.cloned.1.call-done = bf16[1,2048,2048]{2,1,0:T(8,128)(2,1)} async-done(((bf16[1,2048,256]{2,1,0:T(8,128)(2,1)}), bf16[1,2048,2048]{2,1,0:T(8,128)(2,1)}) %all-gather.51.cloned.1.call-update) | async-done | bytes 8388624 | tf_op jit(solution)/shard_map/all_gather | solution.py:134
  1102.4 38.7 %reduce-scatter.36.cloned.1.call-done = bf16[192,2048]{1,0:T(8,128)(2,1)} async-done(((bf16[768,2048]{1,0:T(8,128)(2,1)}), bf16[192,2048]{1,0:T(8,128)(2,1)}) %reduce-scatter.36.cloned.1.call-update) | async-done | bytes 786448 | tf_op jit(solution)/shard_map/reduce_scatter | solution.py:171
  1146.9 28.6 all-gather.35.cloned.1.call-done
  1184.9 71.8 %while.59 = (s32[]{:T(128)}, f32[8,768,64]{1,2,0:T(8,128)}, f32[8,768,64]{1,2,0:T(8,128)}, bf16[8,768,64]{1,2,0:T(8,128)(2,1)S(1)}, bf16[8,768,64]{2,1,0:T(8,128...) while((s32[]{:T(128)}, f32[8,768,64]{1,2,0:T(8,128)}, ...), condition=%wide.region_22.23_spmd.clone, body=%wide.region_20.22_spmd.clone.sunk | while | flops 384662784 | bytes 19690616 | solution.py:112
  1413.2 51.7 %reduce-scatter.70.cloned.1.call-done = bf16[256,1]{1,0:T(8,128)(2,1)} async-done(((bf16[2048,1]{1,0:T(8,128)(2,1)}), bf16[256,1]{1,0:T(8,128)(2,1)}) %reduce-scatter.70.cloned.1.call-update) | async-done | bytes 528
  1465.8 135.8 %reduce-scatter.66.cloned.1.call-done = f32[64,2]{1,0:T(8,128)} async-done(((f32[2048,2]{1,0:T(8,128)}), f32[64,2]{1,0:T(8,128)}) %reduce-scatter.66.cloned.1.call-update) | async-done | bytes 528
  1602.5 59.1 %reduce-scatter.62.cloned.1.call-done = bf16[64,3]{1,0:T(8,128)(2,1)} async-done(((bf16[512,3]{1,0:T(8,128)(2,1)}), bf16[64,3]{1,0:T(8,128)(2,1)}) %reduce-scatter.62.cloned.1.call-update) | async-done | bytes 400
  1663.0 62.9 %reduce-scatter.68.cloned.1.call-done = bf16[256,1]{1,0:T(8,128)(2,1)} async-done(((bf16[2048,1]{1,0:T(8,128)(2,1)}), bf16[256,1]{1,0:T(8,128)(2,1)}) %reduce-scatter.68.cloned.1.call-update) | async-done | bytes 528
  1727.5 69.5 %reduce-scatter.48.cloned.1.call-done = bf16[512,256]{1,0:T(8,128)(2,1)} async-done(((bf16[512,2048]{1,0:T(8,128)(2,1)}), bf16[512,256]{1,0:T(8,128)(2,1)}) %reduce-scatter.48.cloned.1.call-update) | async-done | bytes 262160 | tf_op jit(solution)/shard_map/reduce_scatter | solution.py:314
  1797.0 71.0 %reduce-scatter.46.cloned.1.call-done = bf16[512,256]{1,0:T(8,128)(2,1)} async-done(((bf16[512,2048]{1,0:T(8,128)(2,1)}), bf16[512,256]{1,0:T(8,128)(2,1)}) %reduce-scatter.46.cloned.1.call-update) | async-done | bytes 262160 | tf_op jit(solution)/shard_map/reduce_scatter | solution.py:314
  1873.2 131.4 %reduce-scatter.58.cloned.1.call-done = f32[64,2]{1,0:T(8,128)} async-done(((f32[2048,2]{1,0:T(8,128)}), f32[64,2]{1,0:T(8,128)}) %reduce-scatter.58.cloned.1.call-update) | async-done | bytes 528
  2006.0 131.5 %reduce-scatter.60.cloned.1.call-done = f32[64,2]{1,0:T(8,128)} async-done(((f32[2048,2]{1,0:T(8,128)}), f32[64,2]{1,0:T(8,128)}) %reduce-scatter.60.cloned.1.call-update) | async-done | bytes 528
  2138.9 116.8 %reduce-scatter.44.cloned.1.call-done = bf16[256,3,512]{2,0,1:T(8,128)(2,1)} async-done(((bf16[2048,3,512]{2,0,1:T(8,128)(2,1)}), bf16[256,3,512]{2,0,1:T(8,128)(2,1)}) %reduce-scatter.44.cloned.1.call-update) | async-done | bytes 786448 | tf_op jit(solution)/shard_map/reduce_scatter | solution.py:308
  2255.7 121.4 %reduce-scatter.42.cloned.1.call-done = bf16[256,3,512]{2,0,1:T(8,128)(2,1)} async-done(((bf16[2048,3,512]{2,0,1:T(8,128)(2,1)}), bf16[256,3,512]{2,0,1:T(8,128)(2,1)}) %reduce-scatter.42.cloned.1.call-update) | async-done | bytes 786448 | tf_op jit(solution)/shard_map/reduce_scatter | solution.py:308
  2380.3 149.0 %reduce-scatter.52.cloned.1.call-done = bf16[256,2048]{1,0:T(8,128)(2,1)} async-done(((bf16[2048,2048]{1,0:T(8,128)(2,1)}), bf16[256,2048]{1,0:T(8,128)(2,1)}) %reduce-scatter.52.cloned.1.call-update) | async-done | bytes 1048592 | tf_op jit(solution)/shard_map/reduce_scatter | solution.py:317
  2529.4 151.7 %reduce-scatter.50.cloned.1.call-done = bf16[256,2048]{1,0:T(8,128)(2,1)} async-done(((bf16[2048,2048]{1,0:T(8,128)(2,1)}), bf16[256,2048]{1,0:T(8,128)(2,1)}) %reduce-scatter.50.cloned.1.call-update) | async-done | bytes 1048592 | tf_op jit(solution)/shard_map/reduce_scatter | solution.py:317
  2684.9 148.6 %reduce-scatter.56.cloned.1.call-done = bf16[2048,256]{1,0:T(8,128)(2,1)} async-done(((bf16[2048,2048]{1,0:T(8,128)(2,1)}), bf16[2048,256]{1,0:T(8,128)(2,1)}) %reduce-scatter.56.cloned.1.call-update) | async-done | bytes 1048592 | tf_op jit(solution)/shard_map/reduce_scatter | solution.py:323
  2833.5 152.1 %reduce-scatter.54.cloned.1.call-done = bf16[2048,256]{1,0:T(8,128)(2,1)} async-done(((bf16[2048,2048]{1,0:T(8,128)(2,1)}), bf16[2048,256]{1,0:T(8,128)(2,1)}) %reduce-scatter.54.cloned.1.call-update) | async-done | bytes 1048592 | tf_op jit(solution)/shard_map/reduce_scatter | solution.py:323
  (583 shorter events, 660.7 us)
Async XLA Ops:
  7.2 146.6 %all-gather.29.cloned.1.call-start = ((), (), s32[]{:S(2)}) async-start(), calls=%async_computation.19 | async-start | bytes 3932160 | tf_op jit(solution)/shard_map/all_gather | solution.py:155
  92.2 131.2 %all-gather.37.cloned.1.call-start = ((), (), s32[]{:S(2)}) async-start(), calls=%async_computation.35 | async-start | bytes 7077888 | tf_op jit(solution)/shard_map/all_gather | solution.py:129
  94.9 254.3 %all-gather.41.cloned.1.call-start = ((), (), s32[]{:S(2)}) async-start(), calls=%async_computation.37 | async-start | bytes 9437184 | tf_op jit(solution)/shard_map/all_gather | solution.py:132
  98.2 377.0 %all-gather.43.cloned.1.call-start = ((), (), s32[]{:S(2)}) async-start(), calls=%async_computation.38 | async-start | bytes 9437184 | tf_op jit(solution)/shard_map/all_gather | solution.py:134
  101.5 425.6 %all-gather.39.cloned.1.call-start = ((), (), s32[]{:S(2)}) async-start(), calls=%async_computation.36 | async-start | bytes 2359296 | tf_op jit(solution)/shard_map/all_gather | solution.py:131
  102.4 510.8 %reduce-scatter.34.cloned.1.call-start = ((), (), s32[]{:S(2)}) async-start(), calls=%async_computation.20 | async-start | bytes 3932160 | tf_op jit(solution)/shard_map/reduce_scatter | solution.py:171
  534.0 132.9 %all-gather.47.cloned.1.call-start = ((), (), s32[]{:S(2)}) async-start(), calls=%async_computation.40 | async-start | bytes 2359296 | tf_op jit(solution)/shard_map/all_gather | solution.py:131
  534.8 132.1 %all-gather.33.cloned.1.call-start = ((), (), s32[]{:S(2)}) async-start(), calls=%async_computation.23 | async-start | bytes 3932160 | tf_op jit(solution)/shard_map/all_gather | solution.py:194
  535.5 220.3 %all-gather.45.cloned.1.call-start = ((), (), s32[]{:S(2)}) async-start(), calls=%async_computation.39 | async-start | bytes 7077888 | tf_op jit(solution)/shard_map/all_gather | solution.py:129
  536.7 247.9 %all-gather.31.cloned.1.call-start = ((), (), s32[]{:S(2)}) async-start(), calls=%async_computation.21 | async-start | bytes 3932160 | tf_op jit(solution)/shard_map/all_gather | solution.py:155
  618.0 307.0 %all-gather.49.cloned.1.call-start = ((), (), s32[]{:S(2)}) async-start(), calls=%async_computation.41 | async-start | bytes 9437184 | tf_op jit(solution)/shard_map/all_gather | solution.py:132
  618.7 419.0 %all-gather.51.cloned.1.call-start = ((), (), s32[]{:S(2)}) async-start(), calls=%async_computation.42 | async-start | bytes 9437184 | tf_op jit(solution)/shard_map/all_gather | solution.py:134
  619.3 480.9 %reduce-scatter.38.cloned.1.call-start = ((), (), s32[]{:S(2)}) async-start(), calls=%async_computation.24 | async-start | bytes 3932160 | tf_op jit(solution)/shard_map/reduce_scatter | solution.py:217
  1063.9 77.3 %reduce-scatter.36.cloned.1.call-start = ((), (), s32[]{:S(2)}) async-start(), calls=%async_computation.22 | async-start | bytes 3932160 | tf_op jit(solution)/shard_map/reduce_scatter | solution.py:171
  1080.9 94.7 %all-gather.35.cloned.1.call-start = ((), (), s32[]{:S(2)}) async-start(), calls=%async_computation.25 | async-start | bytes 3932160 | tf_op jit(solution)/shard_map/all_gather | solution.py:194
  1146.9 189.2 %reduce-scatter.40.cloned.1.call-start = ((), (), s32[]{:S(2)}) async-start(), calls=%async_computation.26 | async-start | bytes 3932160 | tf_op jit(solution)/shard_map/reduce_scatter | solution.py:217
  1297.9 114.2 %reduce-scatter.64.cloned.1.call-start = ((), (), s32[]{:S(2)}) async-start(), calls=%async_computation.46 | async-start | bytes 147456
  1299.6 165.3 %reduce-scatter.70.cloned.1.call-start = ((), (), s32[]{:S(2)}) async-start(), calls=%async_computation.49 | async-start | bytes 589824
  1300.8 300.8 %reduce-scatter.66.cloned.1.call-start = ((), (), s32[]{:S(2)}) async-start(), calls=%async_computation.47 | async-start | bytes 1081344
  1302.3 359.4 %reduce-scatter.62.cloned.1.call-start = ((), (), s32[]{:S(2)}) async-start(), calls=%async_computation.45 | async-start | bytes 147456
  1303.3 422.7 %reduce-scatter.68.cloned.1.call-start = ((), (), s32[]{:S(2)}) async-start(), calls=%async_computation.48 | async-start | bytes 589824
  1304.5 492.5 %reduce-scatter.48.cloned.1.call-start = ((), (), s32[]{:S(2)}) async-start(), calls=%async_computation.30 | async-start | bytes 2359296 | tf_op jit(solution)/shard_map/reduce_scatter | solution.py:314
  1310.4 557.7 %reduce-scatter.46.cloned.1.call-start = ((), (), s32[]{:S(2)}) async-start(), calls=%async_computation.29 | async-start | bytes 2359296 | tf_op jit(solution)/shard_map/reduce_scatter | solution.py:314
  1315.5 689.1 %reduce-scatter.58.cloned.1.call-start = ((), (), s32[]{:S(2)}) async-start(), calls=%async_computation.43 | async-start | bytes 1081344
  1341.2 796.3 %reduce-scatter.60.cloned.1.call-start = ((), (), s32[]{:S(2)}) async-start(), calls=%async_computation.44 | async-start | bytes 1081344
  1342.7 913.0 %reduce-scatter.44.cloned.1.call-start = ((), (), s32[]{:S(2)}) async-start(), calls=%async_computation.28 | async-start | bytes 7077888 | tf_op jit(solution)/shard_map/reduce_scatter | solution.py:308
  1351.8 1025.3 %reduce-scatter.42.cloned.1.call-start = ((), (), s32[]{:S(2)}) async-start(), calls=%async_computation.27 | async-start | bytes 7077888 | tf_op jit(solution)/shard_map/reduce_scatter | solution.py:308
  1362.7 1166.7 %reduce-scatter.52.cloned.1.call-start = ((), (), s32[]{:S(2)}) async-start(), calls=%async_computation.32 | async-start | bytes 9437184 | tf_op jit(solution)/shard_map/reduce_scatter | solution.py:317
  1374.3 1306.8 %reduce-scatter.50.cloned.1.call-start = ((), (), s32[]{:S(2)}) async-start(), calls=%async_computation.31 | async-start | bytes 9437184 | tf_op jit(solution)/shard_map/reduce_scatter | solution.py:317
  1385.8 1447.7 %reduce-scatter.56.cloned.1.call-start = ((), (), s32[]{:S(2)}) async-start(), calls=%async_computation.34 | async-start | bytes 9437184 | tf_op jit(solution)/shard_map/reduce_scatter | solution.py:323
  1399.4 1586.1 %reduce-scatter.54.cloned.1.call-start = ((), (), s32[]{:S(2)}) async-start(), calls=%async_computation.33 | async-start | bytes 9437184 | tf_op jit(solution)/shard_map/reduce_scatter | solution.py:323
  1602.5 1386.9 %copy-start.59 = (f32[2,64]{1,0:T(2,128)}, f32[2,64]{1,0:T(2,128)S(1)}, u32[]{:S(2)}) copy-start(f32[2,64]{1,0:T(2,128)S(1)} %copy.126) | copy-start | bytes 1540
  (72 other events, 5163.1 us)
Sparse Core Ops, SparseCore 0:
  92.3 25.9 all-gather.28
  120.9 102.3 all-gather.36
  226.0 123.1 all-gather.40
  351.7 123.5 all-gather.42
  477.7 49.2 all-gather.38
  534.1 36.2 reduce-scatter.33
  573.2 51.4 all-gather.46
  626.3 26.7 all-gather.32
  655.9 99.9 all-gather.44
  757.9 26.7 all-gather.30
  787.0 124.9 all-gather.48
  914.1 123.5 all-gather.50
  1064.0 36.1 reduce-scatter.37
  1103.1 37.9 reduce-scatter.35
  1147.0 28.5 all-gather.34
  1298.1 37.9 reduce-scatter.39
  1339.2 60.8 reduce-scatter.63
  1403.9 60.9 reduce-scatter.69
  1467.8 133.7 reduce-scatter.65
  1604.8 56.7 reduce-scatter.61
  1665.0 60.9 reduce-scatter.67
  1729.9 67.0 reduce-scatter.47
  1800.9 67.0 reduce-scatter.45
  1870.8 133.7 reduce-scatter.57
  2006.8 130.6 reduce-scatter.59
  2141.4 114.2 reduce-scatter.43
  2259.6 117.4 reduce-scatter.41
  2381.2 148.1 reduce-scatter.51
  2533.0 148.0 reduce-scatter.49
  2685.0 148.4 reduce-scatter.55
  2837.1 148.4 reduce-scatter.53
where the time goes:
time: 3000 us
  waiting for transfers between devices  2170 us (72%)
  matrix products  409 us (14%)
  blocking collectives  250 us (8%)
  local copies, waits for them, and re-layouts  92.1 us (3%)
  other arithmetic  56.5 us (2%)
    unnamed x38, waiting for transfers between devices  576 us
    reduce_scatter x2, waiting for transfers between devices, shards(): lax.psum_scatter(up_wg.astype(jnp.bfloat16), 'dp', scatter_dimension=0, t...  301 us
    reduce_scatter x2, waiting for transfers between devices, shards(): lax.psum_scatter(down_wg.astype(jnp.bfloat16), 'dp', scatter_dimension=1,...  301 us
    reduce_scatter x2, waiting for transfers between devices, shards(): lax.psum_scatter(proj_wg.astype(jnp.bfloat16), 'dp', scatter_dimension=0,...  238 us
    all_gather x2, waiting for transfers between devices, fetch_forward(): lax.all_gather(down_weight[layer_index], 'dp', axis=1, tiled=True)  215 us
    dot_general x56, matrix products, cols_product(): lax.dot_general(left, right, (((1,), (1,)), ((), ())), preferred_element_...  156 us
    all_gather x2, waiting for transfers between devices, fetch_forward(): lax.all_gather(proj_weight[layer_index], 'dp', axis=0, tiled=True)  153 us
    reduce_scatter x2, waiting for transfers between devices, shards(): lax.psum_scatter(dense_wg.astype(jnp.bfloat16), 'dp', scatter_dimension=1...  141 us
  transfers between devices with their start and end apart: 31, of which 25 were waited for; matrix products, arithmetic and copies ran while one was open for 13% of the time, Pallas kernels for 0%

commit v1 on v0

v1 whole, which is shorter than its diff:
```python
from functools import partial
import math

import jax
import jax.numpy as jnp
from jax import lax
from jax.experimental import pallas as pl
from jax.experimental.pallas import tpu as pltpu
from jax.sharding import PartitionSpec as P

HEAD_DIM = 64
ROT = 32
BLOCK = 128
LANES = 128
TILE = 256
MID = 1

neg_large = -1e30
f32 = jnp.float32
bf16 = jnp.bfloat16


def swap(value, axis, bit):
    size = lax.axis_size(axis)
    return lax.ppermute(value, axis, [(i, i ^ (1 << bit)) for i in range(size)])


def side_bits():
    count = (lax.axis_size("dp") - 1).bit_length()
    return [bit for bit in range(count - 1, MID, -1)] + [0]


def slice_order():
    sides = side_bits()
    me = lax.axis_index("dp")
    base = me - (((me >> MID) & 1) << MID)
    order = []
    for k in range(1 << len(sides)):
        mask = sum(((k >> s) & 1) << bit for s, bit in enumerate(sides))
        for mid in range(2):
            order.append((base ^ mask) | (mid << MID))
    return jnp.stack(order).astype(jnp.int32)


def pick(pair_first, pair_second, bit):
    return jnp.where(bit == 0, pair_first, pair_second)


def pair_up(keep, received, mid, axis):
    return jnp.concatenate(
        [pick(keep, received, mid), pick(received, keep, mid)], axis=axis
    )


def spread(block, axis):
    blocks = [block]
    for bit in side_bits():
        blocks = blocks + [swap(value, "dp", bit) for value in blocks]
    return jnp.concatenate(blocks, axis=axis)


def spread_sum(product):
    sides = side_bits()
    arrived = [[] for _ in range(1 << len(sides))]

    def total(k):
        part = product(k)
        for value in arrived[k]:
            part = part + value.astype(f32)
        return part.astype(bf16)

    for s in reversed(range(len(sides))):
        for k in reversed(range(1 << s, 2 << s)):
            arrived[k - (1 << s)].append(swap(total(k), "dp", sides[s]))
    return total(0)


def gather_rows(own):
    chunks = [own]
    chunks = chunks + [swap(value, "dp", MID) for value in chunks]
    chunks = chunks + [swap(value, "tensor", 1) for value in chunks]
    chunks = chunks + [swap(value, "tensor", 0) for value in chunks]
    return jnp.concatenate(chunks, axis=0)


def scatter_rows(product, rows):
    high = product(6 * rows, 8 * rows).astype(bf16)
    core_high = swap(high, "tensor", 0)
    low = product(4 * rows, 6 * rows).astype(bf16)
    core_low = swap(low, "tensor", 0)

    def chunk(k, *others):
        source = core_high if k >= 2 else core_low
        at = (k % 2) * rows
        part = product(k * rows, (k + 1) * rows) + source[at : at + rows].astype(f32)
        for value in others:
            part = part + value.astype(f32)
        return part

    x_high = swap(chunk(3).astype(bf16), "tensor", 1)
    x_low = swap(chunk(2).astype(bf16), "tensor", 1)
    mid = swap(chunk(1, x_high).astype(bf16), "dp", MID)
    return chunk(0, x_low, mid)


def copy_kernel(order_ref, in_ref, out_ref):
    out_ref[...] = in_ref[...].astype(out_ref.dtype)


def reorder(value, order, dtype, back=False):
    rows, width = value.shape
    count = order.shape[0]
    part = width // count
    if part % LANES:
        blocks = value.reshape(rows, count, part)
        index = jnp.argsort(order) if back else order
        return jnp.take(blocks, index, axis=1).reshape(rows, width).astype(dtype)
    there = pl.BlockSpec((rows, part), lambda i, order_ref: (0, order_ref[i]))
    here = pl.BlockSpec((rows, part), lambda i, order_ref: (0, i))
    return pl.pallas_call(
        copy_kernel,
        grid_spec=pltpu.PrefetchScalarGridSpec(
            num_scalar_prefetch=1,
            grid=(count,),
            in_specs=[here if back else there],
            out_specs=there if back else here,
        ),
        out_shape=jax.ShapeDtypeStruct((rows, width), dtype),
    )(order, value)


def layout(lens, total, block):
    steps_index = jnp.arange(total, dtype=jnp.int32)
    blocks_first = (lens[0] + block - 1) // block
    second_start = blocks_first * block
    in_first = steps_index < lens[0]
    in_second = (steps_index >= second_start) & (steps_index < second_start + lens[1])
    return jnp.where(in_first, steps_index, jnp.where(in_second, steps_index - second_start, 0))


def rotary_tables(position):
    half_rot = ROT // 2
    freqs = 10000.0 ** (-(jnp.arange(half_rot).astype(f32) * 2.0) / ROT)
    angles = position.astype(f32)[..., None] * freqs
    cosine, sine = jnp.cos(angles), jnp.sin(angles)
    rest = position.shape + (HEAD_DIM - ROT,)
    ones, zeros, none = jnp.ones(rest, f32), jnp.zeros(rest, f32), jnp.zeros_like(sine)
    heads = LANES // HEAD_DIM
    tables = (
        jnp.concatenate([cosine, cosine, ones] * heads, axis=-1),
        jnp.concatenate([-sine, none, zeros] * heads, axis=-1),
        jnp.concatenate([none, sine, zeros] * heads, axis=-1),
    )
    return tables


def turn(field, cos, above, below, back=False):
    up = pltpu.roll(field, LANES - ROT // 2, 1) * above
    down = pltpu.roll(field, ROT // 2, 1) * below
    return field * cos - (up + down) if back else field * cos + (up + down)


def allowed_bias(scalars, group, first_row, rows, cols):
    first_len, second_len = scalars[2 * group], scalars[2 * group + 1]
    second_start = ((first_len + BLOCK - 1) // BLOCK) * BLOCK
    row = first_row + lax.broadcasted_iota(jnp.int32, (rows, 1), 0)
    in_second = (row >= second_start) & (row < second_start + second_len)
    start = jnp.where(row < first_len, 0, jnp.where(in_second, second_start, row))
    col = lax.broadcasted_iota(jnp.int32, (rows, cols), 1)
    return jnp.where((col >= start) & (col <= row), 0.0, neg_large)


def chunk_places(scalars, rows):
    me = scalars[4]
    return [pl.multiple_of((me ^ ((r % 2) * 2 + r // 2)) * rows, 64) for r in range(4)]


def head_mask(head):
    lane = lax.broadcasted_iota(jnp.int32, (1, LANES), 1)
    return jnp.where(lane // HEAD_DIM == head, 1.0, 0.0).astype(bf16)


def nt(left, right):
    return lax.dot_general(left, right, (((1,), (1,)), ((), ())), preferred_element_type=f32)


def nn(left, right):
    return jnp.dot(left, right, preferred_element_type=f32)


def tn(left, right):
    return lax.dot_general(left, right, (((0,), (0,)), ((), ())), preferred_element_type=f32)


def attention_kernel(
    scalars, mixed_ref, cos_ref, above_ref, below_ref, out_ref, kept_ref, sums_ref, held
):
    group = pl.program_id(0)
    rows = mixed_ref.shape[2]
    width = mixed_ref.shape[3] // 3
    total = 4 * rows
    places = chunk_places(scalars, rows)
    for r in range(4):
        at = pl.ds(places[r], rows)
        cos, above, below = cos_ref[0, at, :], above_ref[0, at, :], below_ref[0, at, :]
        for part in range(0, 2 * width, LANES):
            turned = turn(mixed_ref[r, 0, :, part : part + LANES], cos, above, below)
            if part < width:
                turned = turned.astype(bf16) * HEAD_DIM**-0.5
            kept_ref[0, at, part : part + LANES] = turned.astype(bf16)
        kept_ref[0, at, 2 * width :] = mixed_ref[r, 0, :, 2 * width :].astype(bf16)
    for first in range(0, total, TILE):
        cols = first + TILE
        bias = allowed_bias(scalars, group, first, TILE, cols)
        for pair in range(0, width, LANES):
            query = kept_ref[0, first:cols, pair : pair + LANES]
            key = kept_ref[0, :cols, width + pair : width + pair + LANES]
            value = kept_ref[0, :cols, 2 * width + pair : 2 * width + pair + LANES]
            result = None
            for head in range(LANES // HEAD_DIM):
                mask = head_mask(head)
                scores = nt(query * mask, key) + bias
                top = jnp.max(scores, axis=1, keepdims=True)
                expo = jnp.exp(scores - top)
                mass = jnp.sum(expo, axis=1, keepdims=True)
                probs16 = (expo * (1.0 / mass)).astype(bf16)
                mine = nn(probs16, value * mask)
                result = mine if result is None else result + mine
                at_head = pair // HEAD_DIM + head
                sums_ref[0, first:cols, at_head : at_head + 1] = top + jnp.log(mass)
            held[first:cols, pair : pair + LANES] = result.astype(bf16)
    for r in range(4):
        out_ref[r, 0] = held[pl.ds(places[r], rows), :]


def attention_back_kernel(
    scalars,
    kept_ref,
    sums_ref,
    grad_ref,
    cos_ref,
    above_ref,
    below_ref,
    out_ref,
    held,
    query_grad,
    key_grad,
    value_grad,
):
    group = pl.program_id(0)
    rows = grad_ref.shape[2]
    width = grad_ref.shape[3]
    total = 4 * rows
    places = chunk_places(scalars, rows)
    for r in range(4):
        held[pl.ds(places[r], rows), :] = grad_ref[r, 0]
    for first in reversed(range(0, total, TILE)):
        cols = first + TILE
        bias = allowed_bias(scalars, group, first, TILE, cols)
        for pair in range(0, width, LANES):
            lanes = slice(pair, pair + LANES)
            query = kept_ref[0, first:cols, pair : pair + LANES]
            key = kept_ref[0, :cols, width + pair : width + pair + LANES]
            value = kept_ref[0, :cols, 2 * width + pair : 2 * width + pair + LANES]
            grad = held[first:cols, lanes]
            grads = [None, None, None]
            for head in range(LANES // HEAD_DIM):
                mask = head_mask(head)
                at_head = pair // HEAD_DIM + head
                query_head, grad_head = query * mask, grad * mask
                scores = nt(query_head, key) + bias
                probs = jnp.exp(scores - sums_ref[0, first:cols, at_head : at_head + 1])
                prob_grad = nt(grad_head, value)
                mean = jnp.sum(probs * prob_grad, axis=1, keepdims=True)
                score_grad = (probs * (prob_grad - mean)).astype(bf16)
                mine = (
                    nn(score_grad, key * mask),
                    tn(score_grad, query_head),
                    tn(probs.astype(bf16), grad_head),
                )
                grads = [m if g is None else g + m for g, m in zip(grads, mine)]
            query_grad[first:cols, lanes] = grads[0]
            if cols == total:
                key_grad[:, lanes] = grads[1]
                value_grad[:, lanes] = grads[2]
            else:
                key_grad[:cols, lanes] += grads[1]
                value_grad[:cols, lanes] += grads[2]
    for r in range(4):
        at = pl.ds(places[r], rows)
        cos, above, below = cos_ref[0, at, :], above_ref[0, at, :], below_ref[0, at, :]
        for pair in range(0, width, LANES):
            query = turn(query_grad[at, pair : pair + LANES] * HEAD_DIM**-0.5, cos, above, below, True)
            key = turn(key_grad[at, pair : pair + LANES], cos, above, below, True)
            out_ref[r, 0, :, pair : pair + LANES] = query.astype(bf16)
            out_ref[r, 0, :, width + pair : width + pair + LANES] = key.astype(bf16)
        out_ref[r, 0, :, 2 * width :] = value_grad[at, :].astype(bf16)


def chunk_spec(rows, width):
    return pl.BlockSpec((4, 1, rows, width), lambda g, scalars: (0, g, 0, 0))


def group_spec(total, width):
    return pl.BlockSpec((1, total, width), lambda g, scalars: (g, 0, 0))


def attention_forward(mixed, tables, scalars, rows):
    width = mixed.shape[1] // 3
    total = 4 * rows
    attended, kept, sums = pl.pallas_call(
        attention_kernel,
        grid_spec=pltpu.PrefetchScalarGridSpec(
            num_scalar_prefetch=1,
            grid=(2,),
            in_specs=[chunk_spec(rows, 3 * width)] + [group_spec(total, LANES)] * 3,
            out_specs=[
                chunk_spec(rows, width),
                group_spec(total, 3 * width),
                group_spec(total, LANES),
            ],
            scratch_shapes=[pltpu.VMEM((total, width), bf16)],
        ),
        out_shape=[
            jax.ShapeDtypeStruct((4, 2, rows, width), bf16),
            jax.ShapeDtypeStruct((2, total, 3 * width), bf16),
            jax.ShapeDtypeStruct((2, total, LANES), f32),
        ],
        compiler_params=pltpu.CompilerParams(vmem_limit_bytes=40 << 20),
        cost_estimate=pl.CostEstimate(
            flops=16 * total * total * width, bytes_accessed=40 * total * width, transcendentals=0
        ),
    )(scalars, mixed.reshape(4, 2, rows, 3 * width), *tables)
    return attended.reshape(8 * rows, width), kept, sums


def attention_backward(kept, sums, grad16, tables, scalars, rows):
    width = grad16.shape[1]
    total = 4 * rows
    mixed_grad = pl.pallas_call(
        attention_back_kernel,
        grid_spec=pltpu.PrefetchScalarGridSpec(
            num_scalar_prefetch=1,
            grid=(2,),
            in_specs=[
                group_spec(total, 3 * width),
                group_spec(total, LANES),
                chunk_spec(rows, width),
            ]
            + [group_spec(total, LANES)] * 3,
            out_specs=chunk_spec(rows, 3 * width),
            scratch_shapes=[pltpu.VMEM((total, width), bf16)]
            + [pltpu.VMEM((total, width), f32)] * 3,
        ),
        out_shape=jax.ShapeDtypeStruct((4, 2, rows, 3 * width), bf16),
        compiler_params=pltpu.CompilerParams(vmem_limit_bytes=40 << 20),
        cost_estimate=pl.CostEstimate(
            flops=40 * total * total * width, bytes_accessed=40 * total * width, transcendentals=0
        ),
    )(scalars, kept, sums, grad16.reshape(4, 2, rows, width), *tables)
    return mixed_grad.reshape(8 * rows, 3 * width)


def norm_rows(rows, scale, shift):
    centre = rows - jnp.mean(rows, axis=-1, keepdims=True)
    spread_of = jnp.mean(centre * centre, axis=-1, keepdims=True)
    return centre * lax.rsqrt(spread_of + 1e-05) * scale + shift


def halves(value, half, axis):
    size = value.shape[axis] // 2
    return lax.dynamic_slice_in_dim(value, half * size, size, axis)


def fetch(take, mid, axis):
    keep, received = take(mid), swap(take(1 - mid), "dp", MID)
    return spread(pair_up(keep, received, mid, axis), axis)


def owned(product, mid, axis):
    total = spread_sum(product)
    keep = halves(total, mid, axis)
    received = swap(halves(total, 1 - mid, axis), "dp", MID)
    return pick(keep, received, mid).astype(f32), pick(received, keep, mid).astype(f32)


def layer_forward(stream, scale_row, shift_row, out_shift, weights, in_shift, tables, scalars, last):
    proj_full, up_full, out_full = weights
    proj_shift, up_shift = in_shift
    rows = stream.shape[0]
    normed = norm_rows(stream, scale_row, shift_row).astype(bf16)
    gathered = gather_rows(normed)
    mixed = nn(gathered, proj_full) + proj_shift
    attended, kept, sums = attention_forward(mixed, tables, scalars, rows)
    hidden_pre = nn(gathered, up_full) + up_shift
    hidden16 = jax.nn.gelu(hidden_pre, approximate=True).astype(bf16)
    features = jnp.concatenate([attended, hidden16], axis=1)
    branch = scatter_rows(lambda lo, hi: nn(features[lo:hi], out_full), rows)
    return stream + branch + out_shift, (gathered, kept, sums, features, hidden_pre)


def layer_backward(grad_in, stream_in, scale_row, shift_row, weights, saved, tables, scalars, mid):
    proj_full, up_full, out_full = weights
    gathered, kept, sums, features, hidden_pre = saved
    rows, width = stream_in.shape
    parts = 1 << len(side_bits())
    part = width // parts
    heads_width = proj_full.shape[1] // 3
    bias_grad = jnp.sum(grad_in, axis=0)
    grad16 = gather_rows(grad_in.astype(bf16))
    out_grads = owned(
        lambda k: tn(features, grad16[:, k * part : (k + 1) * part]), mid, 1
    )
    attended_grad = nt(grad16, out_full[:heads_width]).astype(bf16)
    mixed_grad = attention_backward(kept, sums, attended_grad, tables, scalars, rows)
    hidden_grad = nt(grad16, out_full[heads_width:])
    unused, gelu_pull = jax.vjp(partial(jax.nn.gelu, approximate=True), hidden_pre)
    pre_grad = gelu_pull(hidden_grad)[0].astype(bf16)
    up_grads = owned(
        lambda k: tn(gathered[:, k * part : (k + 1) * part], pre_grad), mid, 0
    )
    proj_grads = owned(
        lambda k: tn(gathered[:, k * part : (k + 1) * part], mixed_grad), mid, 0
    )
    in_bgrad = (
        jnp.sum(mixed_grad, axis=0, dtype=f32),
        jnp.sum(pre_grad, axis=0, dtype=f32),
    )
    both = jnp.concatenate([mixed_grad, pre_grad], axis=1)
    both_full = jnp.concatenate([proj_full, up_full], axis=1)
    normed_grad = scatter_rows(lambda lo, hi: nt(both[lo:hi], both_full), rows)
    unused_norm, norm_pull = jax.vjp(norm_rows, stream_in, scale_row, shift_row)
    stream_grad, scale_grad, shift_grad = norm_pull(normed_grad)
    norm_grads = jnp.stack([scale_grad, shift_grad, bias_grad])
    return grad_in + stream_grad, (proj_grads, up_grads, out_grads), in_bgrad, norm_grads


def small_sums(norm_grads, in_bgrads, mid):
    sides = side_bits()
    tensor = lax.axis_index("tensor")
    layers, kinds, width = norm_grads.shape
    sums = norm_grads.reshape(layers * kinds, -1)
    biases = in_bgrads
    split = biases.shape[0]
    for s in reversed(range(len(sides))):
        half = sums.shape[1] // 2
        sent = jnp.concatenate([biases, sums[:, half:].reshape(-1)])
        received = swap(sent, "dp", sides[s])
        biases = biases + received[:split]
        sums = sums[:, :half] + received[split:].reshape(-1, half)
    half = sums.shape[1] // 2
    sent = jnp.concatenate([biases, halves(sums, 1 - mid, 1).reshape(-1)])
    received = swap(sent, "dp", MID)
    both = jnp.stack([pick(biases, received[:split], mid), pick(received[:split], biases, mid)])
    sums = halves(sums, mid, 1) + received[split:].reshape(-1, half)
    for bit in (1, 0):
        mine = (tensor >> bit) & 1
        sums = halves(sums, mine, 1) + swap(halves(sums, 1 - mine, 1), "tensor", bit)
    return sums.reshape(layers, kinds, -1), both


def shards(
    tokens_in,
    lengths,
    norm_gain,
    norm_bias,
    proj_weight,
    proj_bias,
    dense_weight,
    dense_bias,
    up_weight,
    up_bias,
    down_weight,
    down_bias,
    cotangent,
):
    rows, width = tokens_in.shape
    layer_count = proj_weight.shape[0]
    n_dp = lax.axis_size("dp")
    dp = lax.axis_index("dp")
    tensor = lax.axis_index("tensor")
    mid = (dp >> MID) & 1
    order = slice_order()

    def weights_of(l):
        def take_proj(half):
            return halves(proj_weight[l], half, 2).reshape(proj_weight.shape[1], -1)

        def take_up(half):
            return halves(up_weight[l], half, 1)

        def take_out(half):
            return jnp.concatenate(
                [halves(dense_weight[l], half, 0), halves(down_weight[l], half, 0)], axis=0
            )

        return (fetch(take_proj, mid, 0), fetch(take_up, mid, 0), fetch(take_out, mid, 1))

    weights = [weights_of(l) for l in range(layer_count)]

    owners = n_dp * lax.axis_size("tensor")
    small = jnp.concatenate(
        [
            value.reshape(-1)
            for value in (norm_gain, norm_bias, dense_bias, down_bias, proj_bias, up_bias)
        ]
    )
    everyone = lax.all_gather(small, ("dp", "tensor"), axis=0)
    each = norm_gain.shape[1]
    rows_count = 4 * layer_count
    at = rows_count * each
    norm_parts = everyone[:, :at].reshape(n_dp, -1, rows_count, each)[order]
    norm_parts = jnp.transpose(norm_parts, (2, 0, 1, 3)).reshape(4, layer_count, width).astype(f32)
    same_heads = lax.dynamic_index_in_dim(
        everyone[:, at:].reshape(n_dp, -1, everyone.shape[1] - at), tensor, 1, keepdims=False
    )
    same_heads = halves(same_heads, mid, 0).astype(f32)
    proj_each, up_each = proj_bias.shape[3], up_bias.shape[2]
    proj_at = layer_count * 3 * proj_each
    proj_shift = jnp.transpose(
        same_heads[:, :proj_at].reshape(-1, layer_count * 3, proj_each), (1, 0, 2)
    ).reshape(layer_count, -1)
    up_shift = jnp.transpose(
        same_heads[:, proj_at:].reshape(-1, layer_count, up_each), (1, 0, 2)
    ).reshape(layer_count, -1)

    lens = jnp.concatenate([lengths, swap(lengths, "dp", MID)], axis=0)
    scalars = jnp.concatenate([lens.reshape(-1), tensor[None].astype(jnp.int32)]).astype(jnp.int32)
    tables = rotary_tables(jax.vmap(partial(layout, total=4 * rows, block=BLOCK))(lens))

    stream = reorder(tokens_in, order, f32)
    grad_stream = reorder(cotangent, order, f32)
    saved = []
    for l in range(layer_count):
        stream_in = stream
        stream, kept = layer_forward(
            stream,
            norm_parts[0, l],
            norm_parts[1, l],
            norm_parts[2, l] + norm_parts[3, l],
            weights[l],
            (proj_shift[l], up_shift[l]),
            tables,
            scalars,
            l == layer_count - 1,
        )
        saved.append((stream_in, kept))
    weight_grads = [None] * layer_count
    in_bgrads = [None] * layer_count
    norm_grads = [None] * layer_count
    for l in reversed(range(layer_count)):
        stream_in, kept = saved[l]
        grad_stream, weight_grads[l], in_bgrads[l], norm_grads[l] = layer_backward(
            grad_stream,
            stream_in,
            norm_parts[0, l],
            norm_parts[1, l],
            weights[l],
            kept,
            tables,
            scalars,
            mid,
        )
    heads_width = weights[0][0].shape[1] // 3
    proj_out, up_out, dense_out, down_out = [], [], [], []
    for l in range(layer_count):
        proj_grads, up_grads, out_grads = weight_grads[l]
        proj_out.append(
            jnp.concatenate([g.reshape(g.shape[0], 3, -1) for g in proj_grads], axis=2)
        )
        up_out.append(jnp.concatenate(up_grads, axis=1))
        dense_out.append(jnp.concatenate([g[:heads_width] for g in out_grads], axis=0))
        down_out.append(jnp.concatenate([g[heads_width:] for g in out_grads], axis=0))

    flat = jnp.concatenate([value for pair in in_bgrads for value in pair])
    norm_owned, bias_both = small_sums(jnp.stack(norm_grads), flat, mid)
    per_layer = flat.shape[0] // layer_count
    bias_both = bias_both.reshape(2, layer_count, per_layer)
    proj_b = jnp.transpose(
        bias_both[:, :, : 3 * heads_width].reshape(2, layer_count, 3, heads_width), (1, 2, 0, 3)
    ).reshape(layer_count, 3, 1, 2 * heads_width)
    up_b = jnp.transpose(bias_both[:, :, 3 * heads_width :], (1, 0, 2)).reshape(layer_count, 1, -1)
    return (
        reorder(stream, order, f32, True),
        reorder(grad_stream, order, f32, True),
        norm_owned[:, 0],
        norm_owned[:, 1],
        jnp.stack(proj_out),
        lax.dynamic_slice_in_dim(proj_b, dp * proj_each, proj_each, 3),
        jnp.stack(dense_out),
        norm_owned[:, 2],
        jnp.stack(up_out),
        lax.dynamic_slice_in_dim(up_b, dp * up_each, up_each, 2),
        jnp.stack(down_out),
        norm_owned[:, 2],
    )


def solution(mesh):
    in_specs = (
        P(("dp", "tensor"), None),
        P("dp", None),
        P(None, ("dp", "tensor")),
        P(None, ("dp", "tensor")),
        P(None, "dp", None, "tensor"),
        P(None, None, "tensor", "dp"),
        P(None, "tensor", "dp"),
        P(None, ("dp", "tensor")),
        P(None, "dp", "tensor"),
        P(None, "tensor", "dp"),
        P(None, "tensor", "dp"),
        P(None, ("dp", "tensor")),
        P(("dp", "tensor"), None),
    )
    out_specs = (
        P(("dp", "tensor"), None),
        P(("dp", "tensor"), None),
        P(None, ("dp", "tensor")),
        P(None, ("dp", "tensor")),
        P(None, "dp", None, "tensor"),
        P(None, None, "tensor", "dp"),
        P(None, "tensor", "dp"),
        P(None, ("dp", "tensor")),
        P(None, "dp", "tensor"),
        P(None, "tensor", "dp"),
        P(None, "tensor", "dp"),
        P(None, ("dp", "tensor")),
    )
    return jax.shard_map(shards, mesh=mesh, in_specs=in_specs, out_specs=out_specs, check_vma=False)
```

time: 3000 us -> 1420 us (0.47)
  waiting for transfers between devices: 2170 us -> 751 us
  blocking collectives: 250 us -> 43.7 us
  matrix products: 409 us -> 271 us
  starting transfers between devices: 1.28 us -> 99.4 us
  Pallas kernels: 0 us -> 79.4 us
    reduce_scatter x12 -> x0, waiting for transfers between devices: 1060 us -> none  [the longest x2 301 us: shards(): lax.psum_scatter(up_wg.astype(jnp.bfloat16), 'dp', scatter_dimension=0, t...]
    ppermute x0 -> x102, waiting for transfers between devices: none -> 751 us  [swap(): return lax.ppermute(value, axis, [(i, i ^ 1 << bit) for i in range(size)])]
    unnamed x38 -> x0, waiting for transfers between devices: 576 us -> none
    all_gather x12 -> x0, waiting for transfers between devices: 536 us -> none  [the longest x2 215 us: fetch_forward(): lax.all_gather(down_weight[layer_index], 'dp', axis=1, tiled=True)]
    all_gather x8 -> x1, blocking collectives: 250 us -> 43.7 us  [shards(): everyone = lax.all_gather(small, ('dp', 'tensor'), axis=0)]
    dot_general x136 -> x56, matrix products: 409 us -> 271 us  [the longest x16 99.8 us: nt(): lax.dot_general(left, right, (((1,), (1,)), ((), ())), preferred_element_...]
    ppermute x0 -> x102, starting transfers between devices: none -> 99.4 us  [swap(): return lax.ppermute(value, axis, [(i, i ^ 1 << bit) for i in range(size)])]
    pallas_call x0 -> x8, Pallas kernels: none -> 79.4 us  [the longest x2 32.4 us: attention_backward(): pl.pallas_call(attention_back_kernel, grid_spec=pltpu.PrefetchScalarGridS...]
  transfers between devices with their start and end apart: 31 -> 102, of which waited for: 25 -> 39; matrix products, arithmetic and copies ran while one was open for 13% -> 18% of each run, Pallas kernels for 0% -> 2%
where the time goes in v1:
time: 1420 us; the launch traced here: 1410 us
  waiting for transfers between devices  751 us (53%)
  matrix products  271 us (19%)
  local copies, waits for them, and re-layouts  104 us (7%)
  starting transfers between devices  99.4 us (7%)
  Pallas kernels  79.4 us (6%)
  other arithmetic  55.5 us (4%)
  blocking collectives  43.7 us (3%)
    ppermute x102, waiting for transfers between devices, swap(): return lax.ppermute(value, axis, [(i, i ^ 1 << bit) for i in range(size)])  751 us
    dot_general x16, matrix products, nt(): lax.dot_general(left, right, (((1,), (1,)), ((), ())), preferred_element_...  99.8 us
    ppermute x102, starting transfers between devices, swap(): return lax.ppermute(value, axis, [(i, i ^ 1 << bit) for i in range(size)])  99.4 us
    dot_general x24, matrix products, tn(): lax.dot_general(left, right, (((0,), (0,)), ((), ())), preferred_element_...  92.2 us
    dot_general x16, matrix products, nn(): return jnp.dot(left, right, preferred_element_type=f32)  79.1 us
    unnamed x339, local copies, waits for them, and re-layouts  57.3 us
    all_gather x1, blocking collectives, shards(): everyone = lax.all_gather(small, ('dp', 'tensor'), axis=0)  43.7 us
    pallas_call x2, Pallas kernels, attention_backward(): pl.pallas_call(attention_back_kernel, grid_spec=pltpu.PrefetchScalarGridS...  32.4 us
  transfers between devices with their start and end apart: 102, of which 39 were waited for; matrix products, arithmetic and copies ran while one was open for 18% of the time, Pallas kernels for 2%

profile of v1, /device:TPU:0, one launch (start us, length us, event | category | flops | bytes accessed | tf_op | source)
XLA Modules:
  0.0 1408.1 jit_solution(14177696471513281879)
XLA Ops:
  6.5 43.7 %all-gather.1 = bf16[32,1,1408]{2,1,0:T(2,128)(2,1)S(1)} all-gather(bf16[1,1,1408]{2,1,0:T(2,128)(2,1)S(1)} %reshape.802), channel_id=2, replica_groups=mesh['dp'=8,'tensor'=4] {'dp','tensor'}, dimensions={0}, use_global_device_ids=true | all-gather | bytes 92928 | tf_op jit(solution)/shard_map/all_gather | solution.py:508
  132.0 21.4 %collective-permute-done.40 = bf16[1280,256]{1,0:T(8,128)(2,1)S(1)} collective-permute-done((bf16[1280,256]{1,0:T(8,128)(2,1)S(1)}, bf16[1280,256]{1,0:T(8,128)(2,1)S(1)}, u32[]{:S(2)}, u32[]{:S(2)}) %collective-permute-start.40) | collective-permute-done | bytes 655392 | tf_op jit(solution)/shard_map/ppermute | solution.py:25
  179.2 34.9 %collective-permute-done.9 = bf16[512,768]{1,0:T(8,128)(2,1)S(1)} collective-permute-done((bf16[512,768]{1,0:T(8,128)(2,1)S(1)}, bf16[512,768]{1,0:T(8,128)(2,1)S(1)}, u32[]{:S(2)}, u32[]{:S(2)}) %collective-permute-start.9) | collective-permute-done | bytes 786464 | tf_op jit(solution)/shard_map/ppermute | solution.py:25
  223.8 24.9 %collective-permute-done.13 = bf16[512,1024]{1,0:T(8,128)(2,1)} collective-permute-done((bf16[512,1024]{1,0:T(8,128)(2,1)S(1)}, bf16[512,1024]{1,0:T(8,128)(2,1)}, u32[]{:S(2)}, u32[]{:S(2)}) %collective-permute-start.13) | collective-permute-done | bytes 1048608 | tf_op jit(solution)/shard_map/ppermute | solution.py:25
  258.2 40.1 %collective-permute-done.11 = bf16[512,768]{1,0:T(8,128)(2,1)S(1)} collective-permute-done((bf16[512,768]{1,0:T(8,128)(2,1)S(1)}, bf16[512,768]{1,0:T(8,128)(2,1)S(1)}, u32[]{:S(2)}, u32[]{:S(2)}) %collective-permute-start.11) | collective-permute-done | bytes 786464 | tf_op jit(solution)/shard_map/ppermute | solution.py:25
  325.7 37.0 %collective-permute-done.15 = bf16[512,1024]{1,0:T(8,128)(2,1)} collective-permute-done((bf16[512,1024]{1,0:T(8,128)(2,1)}, bf16[512,1024]{1,0:T(8,128)(2,1)}, u32[]{:S(2)}, u32[]{:S(2)}) %collective-permute-start.15) | collective-permute-done | bytes 1048608 | tf_op jit(solution)/shard_map/ppermute | solution.py:25
  365.5 13.4 multiply_convert_fusion.1
  379.0 13.5 collective-permute-done.19
  406.8 31.8 %collective-permute-done.37 = bf16[512,1024]{1,0:T(8,128)(2,1)S(1)} collective-permute-done((bf16[512,1024]{1,0:T(8,128)(2,1)}, bf16[512,1024]{1,0:T(8,128)(2,1)S(1)}, u32[]{:S(2)}, u32[]{:S(2)}) %collective-permute-start.37) | collective-permute-done | bytes 1048608 | tf_op jit(solution)/shard_map/ppermute | solution.py:25
  448.3 13.9 collective-permute-done.51
  468.2 15.6 %collective-permute-done.23 = bf16[192,2048]{1,0:T(8,128)(2,1)S(1)} collective-permute-done((bf16[192,2048]{1,0:T(8,128)(2,1)S(1)}, bf16[192,2048]{1,0:T(8,128)(2,1)S(1)}, u32[]{:S(2)}, u32[]{:S(2)}) %collective-permute-start.23) | collective-permute-done | bytes 786464 | tf_op jit(solution)/shard_map/ppermute | solution.py:25
  487.1 30.5 %collective-permute-done.41 = bf16[1280,512]{1,0:T(8,128)(2,1)S(1)} collective-permute-done((bf16[1280,512]{1,0:T(8,128)(2,1)S(1)}, bf16[1280,512]{1,0:T(8,128)(2,1)S(1)}, u32[]{:S(2)}, u32[]{:S(2)}) %collective-permute-start.41) | collective-permute-done | bytes 1310752 | tf_op jit(solution)/shard_map/ppermute | solution.py:25
  545.5 25.2 %collective-permute-done.43 = bf16[1280,512]{1,0:T(8,128)(2,1)S(1)} collective-permute-done((bf16[1280,512]{1,0:T(8,128)(2,1)S(1)}, bf16[1280,512]{1,0:T(8,128)(2,1)S(1)}, u32[]{:S(2)}, u32[]{:S(2)}) %collective-permute-start.43) | collective-permute-done | bytes 1310752 | tf_op jit(solution)/shard_map/ppermute | solution.py:25
  579.6 12.5 collective-permute-done.27
  617.6 16.3 %shard_map.225 = bf16[4,2,192,768]{3,2,1,0:T(8,128)(2,1)S(1)} custom-call(s32[5]{0:T(128)S(1)} %pad_add_fusion.1.scalars, bf16[2,768,768]{2,1,0:T(8,128)(2,1)S(1)} %get-tuple-element.20.kept_ref, f32[2,768,128]{2,1,0:T(8,128)S(1)} %get-tuple-element.21.sums_ref, bf16[4,2,192,256]{3,2,1,0:T(8,128)(2,1)S(1)} %bitcast.178, f32[2,768,128]{2,1,0:T(8,128)S(1)} %copy-done.7, ...), custom_call_target="tpu_custom_call" | custom-call | flops 6039797760 | bytes 7864320 | tf_op jit(solution)/shard_map/pallas_call | solution.py:340
  664.1 12.1 convert_reduce_fusion
  729.2 18.7 %collective-permute-done.99 = bf16[512,1024]{1,0:T(8,128)(2,1)S(1)} collective-permute-done((bf16[512,1024]{1,0:T(8,128)(2,1)S(1)}, bf16[512,1024]{1,0:T(8,128)(2,1)S(1)}, u32[]{:S(2)}, u32[]{:S(2)}) %collective-permute-start.99) | collective-permute-done | bytes 1048608 | tf_op jit(solution)/shard_map/ppermute | solution.py:25
  752.1 23.9 %collective-permute-done.91 = bf16[1280,512]{1,0:T(8,128)(2,1)S(1)} collective-permute-done((bf16[1280,512]{1,0:T(8,128)(2,1)S(1)}, bf16[1280,512]{1,0:T(8,128)(2,1)S(1)}, u32[]{:S(2)}, u32[]{:S(2)}) %collective-permute-start.91) | collective-permute-done | bytes 1310752 | tf_op jit(solution)/shard_map/ppermute | solution.py:25
  798.1 48.2 %collective-permute-done.84 = bf16[512,768]{1,0:T(8,128)(2,1)S(1)} collective-permute-done((bf16[512,768]{1,0:T(8,128)(2,1)S(1)}, bf16[512,768]{1,0:T(8,128)(2,1)S(1)}, u32[]{:S(2)}, u32[]{:S(2)}) %collective-permute-start.84) | collective-permute-done | bytes 786464 | tf_op jit(solution)/shard_map/ppermute | solution.py:25
  854.0 23.1 %collective-permute-done.85 = bf16[256,768]{1,0:T(8,128)(2,1)S(1)} collective-permute-done((bf16[256,768]{1,0:T(8,128)(2,1)S(1)}, bf16[256,768]{1,0:T(8,128)(2,1)S(1)}, u32[]{:S(2)}, u32[]{:S(2)}) %collective-permute-start.85) | collective-permute-done | bytes 393248 | tf_op jit(solution)/shard_map/ppermute | solution.py:25
  922.3 22.5 %collective-permute-done.92 = bf16[1280,512]{1,0:T(8,128)(2,1)S(1)} collective-permute-done((bf16[1280,512]{1,0:T(8,128)(2,1)S(1)}, bf16[1280,512]{1,0:T(8,128)(2,1)S(1)}, u32[]{:S(2)}, u32[]{:S(2)}) %collective-permute-start.92) | collective-permute-done | bytes 1310752 | tf_op jit(solution)/shard_map/ppermute | solution.py:25
  957.4 32.3 %collective-permute-done.60 = bf16[192,2048]{1,0:T(8,128)(2,1)S(1)} collective-permute-done((bf16[192,2048]{1,0:T(8,128)(2,1)}, bf16[192,2048]{1,0:T(8,128)(2,1)S(1)}, u32[]{:S(2)}, u32[]{:S(2)}) %collective-permute-start.60) | collective-permute-done | bytes 786464 | tf_op jit(solution)/shard_map/ppermute | solution.py:25
  1027.0 12.7 collective-permute-done.63
  1050.7 16.1 %shard_map.226 = bf16[4,2,192,768]{3,2,1,0:T(8,128)(2,1)S(1)} custom-call(s32[5]{0:T(128)S(1)} %pad_add_fusion.1.scalars, bf16[2,768,768]{2,1,0:T(8,128)(2,1)S(1)} %copy-done.10, f32[2,768,128]{2,1,0:T(8,128)S(1)} %copy-done.12, bf16[4,2,192,256]{3,2,1,0:T(8,128)(2,1)S(1)} %bitcast.179, f32[2,768,128]{2,1,0:T(8,128)S(1)} %copy-done.8, ...), custom_call_target="tpu_custom_call" | custom-call | flops 6039797760 | bytes 7864320 | tf_op jit(solution)/shard_map/pallas_call | solution.py:340
  1073.1 14.4 %convert_reduce_fusion.1 = (f32[1024]{0:T(1024)S(1)}, bf16[1536,1024]{0,1:T(8,128)(2,1)S(1)}) fusion(f32[1536,1024]{0,1:T(8,128)} %get-tuple-element.159, f32[1024]{0:T(1024)S(1)} %bitcast.225, bf16[1536,2048]{1,0:T(8,128)(2,1)} %constant_dynamic-update-slice_fusion.54, bf16[1280,2048]{1,0:T(8,128)(2,1)} %copy-done.14), kind=kOutput, calls=%fused_computation.56 | convolution fusion | flops 6478625792 | bytes 19931136 | tf_op jit(solution)/shard_map/dot_general | solution.py:184
  1127.2 13.4 collective-permute-done.79
  1142.1 60.3 %collective-permute-done.95 = bf16[512,1024]{1,0:T(8,128)(2,1)S(1)} collective-permute-done((bf16[512,1024]{1,0:T(8,128)(2,1)S(1)}, bf16[512,1024]{1,0:T(8,128)(2,1)S(1)}, u32[]{:S(2)}, u32[]{:S(2)}) %collective-permute-start.95) | collective-permute-done | bytes 1048608 | tf_op jit(solution)/shard_map/ppermute | solution.py:25
  1206.4 23.7 %collective-permute-done.87 = bf16[1280,512]{1,0:T(8,128)(2,1)S(1)} collective-permute-done((bf16[1280,512]{1,0:T(8,128)(2,1)S(1)}, bf16[1280,512]{1,0:T(8,128)(2,1)S(1)}, u32[]{:S(2)}, u32[]{:S(2)}) %collective-permute-start.87) | collective-permute-done | bytes 1310752 | tf_op jit(solution)/shard_map/ppermute | solution.py:25
  1253.9 16.4 %collective-permute-done.81 = bf16[256,768]{1,0:T(8,128)(2,1)S(1)} collective-permute-done((bf16[256,768]{1,0:T(8,128)(2,1)S(1)}, bf16[256,768]{1,0:T(8,128)(2,1)S(1)}, u32[]{:S(2)}, u32[]{:S(2)}) %collective-permute-start.81) | collective-permute-done | bytes 393248 | tf_op jit(solution)/shard_map/ppermute | solution.py:25
  1280.1 34.9 %collective-permute-done.96 = bf16[512,1024]{1,0:T(8,128)(2,1)} collective-permute-done((bf16[512,1024]{1,0:T(8,128)(2,1)}, bf16[512,1024]{1,0:T(8,128)(2,1)}, u32[]{:S(2)}, u32[]{:S(2)}) %collective-permute-start.96) | collective-permute-done | bytes 1048608 | tf_op jit(solution)/shard_map/ppermute | solution.py:25
  1327.1 16.0 %collective-permute-done.88 = bf16[1280,512]{1,0:T(8,128)(2,1)S(1)} collective-permute-done((bf16[1280,512]{1,0:T(8,128)(2,1)S(1)}, bf16[1280,512]{1,0:T(8,128)(2,1)S(1)}, u32[]{:S(2)}, u32[]{:S(2)}) %collective-permute-start.88) | collective-permute-done | bytes 1310752 | tf_op jit(solution)/shard_map/ppermute | solution.py:25
  1357.0 14.1 %collective-permute-done.72 = bf16[192,2048]{1,0:T(8,128)(2,1)S(1)} collective-permute-done((bf16[192,2048]{1,0:T(8,128)(2,1)S(1)}, bf16[192,2048]{1,0:T(8,128)(2,1)S(1)}, u32[]{:S(2)}, u32[]{:S(2)}) %collective-permute-start.72) | collective-permute-done | bytes 786464 | tf_op jit(solution)/shard_map/ppermute | solution.py:25
  (776 shorter events, 626.7 us)
Async XLA Ops:
  63.4 96.9 %collective-permute-start.2 = (bf16[192,2048]{1,0:T(8,128)(2,1)}, bf16[192,2048]{1,0:T(8,128)(2,1)}, u32[]{:S(2)}, u32[]{:S(2)}) collective-permute-start(bf16[192,2048]{1,0:T(8,128)(2,1)} %get-tuple-element.102), channel_id=1, source_target_pairs={{0,2},{1,3},{2,0},{3,1},{4,6},{5,7},{6,4},{7,5},{8,10},{9,11},{10,... | collective-permute-start | bytes 2359304 | tf_op jit(solution)/shard_map/ppermute | solution.py:25
  63.4 107.7 %collective-permute-start.1 = (bf16[192,2048]{1,0:T(8,128)(2,1)}, bf16[192,2048]{1,0:T(8,128)(2,1)}, u32[]{:S(2)}, u32[]{:S(2)}) collective-permute-start(bf16[192,2048]{1,0:T(8,128)(2,1)} %get-tuple-element.102), channel_id=1, source_target_pairs={{0,8},{4,12},{8,0},{12,4},{16,24},{20,28},{24,16},{28,20},{1,9},{5... | collective-permute-start | bytes 2359304 | tf_op jit(solution)/shard_map/ppermute | solution.py:25
  153.4 60.7 %collective-permute-start.9 = (bf16[512,768]{1,0:T(8,128)(2,1)S(1)}, bf16[512,768]{1,0:T(8,128)(2,1)S(1)}, u32[]{:S(2)}, u32[]{:S(2)}) collective-permute-start(bf16[512,768]{1,0:T(8,128)(2,1)S(1)} %pad_maximum_fusion.14), channel_id=1, source_target_pairs={{0,16},{4,20},{8,24},{12,28},{16,0},{20,4},{24,8},{28,12},{1,17},{... | collective-permute-start | bytes 2359304 | tf_op jit(solution)/shard_map/ppermute | solution.py:25
  155.6 93.1 %collective-permute-start.13 = (bf16[512,1024]{1,0:T(8,128)(2,1)S(1)}, bf16[512,1024]{1,0:T(8,128)(2,1)}, u32[]{:S(2)}, u32[]{:S(2)}) collective-permute-start(bf16[512,1024]{1,0:T(8,128)(2,1)S(1)} %pad_maximum_fusion.7), channel_id=1, source_target_pairs={{0,16},{4,20},{8,24},{12,28},{16,0},{20,4},{24,8},{28,12},{1,17},{... | collective-permute-start | bytes 3145736 | tf_op jit(solution)/shard_map/ppermute | solution.py:25
  160.2 63.5 %collective-permute-start.10 = (bf16[512,768]{1,0:T(8,128)(2,1)S(1)}, bf16[512,768]{1,0:T(8,128)(2,1)S(1)}, u32[]{:S(2)}, u32[]{:S(2)}) collective-permute-start(bf16[512,768]{1,0:T(8,128)(2,1)S(1)} %pad_maximum_fusion.14), channel_id=1, source_target_pairs={{0,4},{4,0},{8,12},{12,8},{16,20},{20,16},{24,28},{28,24},{1,5},{5... | collective-permute-start | bytes 2359304 | tf_op jit(solution)/shard_map/ppermute | solution.py:25
  171.0 79.0 %collective-permute-start.14 = (bf16[512,1024]{1,0:T(8,128)(2,1)S(1)}, bf16[512,1024]{1,0:T(8,128)(2,1)S(1)}, u32[]{:S(2)}, u32[]{:S(2)}) collective-permute-start(bf16[512,1024]{1,0:T(8,128)(2,1)S(1)} %pad_maximum_fusion.7), channel_id=1, source_target_pairs={{0,4},{4,0},{8,12},{12,8},{16,20},{20,16},{24,28},{28,24},{1,5},{5... | collective-permute-start | bytes 3145736 | tf_op jit(solution)/shard_map/ppermute | solution.py:25
  179.2 71.0 %collective-permute-start.4 = (bf16[192,2048]{1,0:T(8,128)(2,1)}, bf16[192,2048]{1,0:T(8,128)(2,1)S(1)}, u32[]{:S(2)}, u32[]{:S(2)}) collective-permute-start(bf16[192,2048]{1,0:T(8,128)(2,1)} %get-tuple-element.102), channel_id=1, source_target_pairs={{0,1},{1,0},{2,3},{3,2},{4,5},{5,4},{6,7},{7,6},{8,9},{9,8},{10,11... | collective-permute-start | bytes 2359304 | tf_op jit(solution)/shard_map/ppermute | solution.py:25
  252.5 145.5 %collective-permute-start.50 = (bf16[192,2048]{1,0:T(8,128)(2,1)}, bf16[192,2048]{1,0:T(8,128)(2,1)}, u32[]{:S(2)}, u32[]{:S(2)}) collective-permute-start(bf16[192,2048]{1,0:T(8,128)(2,1)} %get-tuple-element.78), channel_id=1, source_target_pairs={{0,2},{1,3},{2,0},{3,1},{4,6},{5,7},{6,4},{7,5},{8,10},{9,11},{10,... | collective-permute-start | bytes 2359304 | tf_op jit(solution)/shard_map/ppermute | solution.py:25
  298.3 106.0 %collective-permute-start.34 = (bf16[512,768]{1,0:T(8,128)(2,1)}, bf16[512,768]{1,0:T(8,128)(2,1)}, u32[]{:S(2)}, u32[]{:S(2)}) collective-permute-start(bf16[512,768]{1,0:T(8,128)(2,1)} %pad_maximum_fusion.15), channel_id=1, source_target_pairs={{0,4},{4,0},{8,12},{12,8},{16,20},{20,16},{24,28},{28,24},{1,5},{5... | collective-permute-start | bytes 2359304 | tf_op jit(solution)/shard_map/ppermute | solution.py:25
  298.7 103.5 %collective-permute-start.33 = (bf16[512,768]{1,0:T(8,128)(2,1)}, bf16[512,768]{1,0:T(8,128)(2,1)}, u32[]{:S(2)}, u32[]{:S(2)}) collective-permute-start(bf16[512,768]{1,0:T(8,128)(2,1)} %pad_maximum_fusion.15), channel_id=1, source_target_pairs={{0,16},{4,20},{8,24},{12,28},{16,0},{20,4},{24,8},{28,12},{1,17},{... | collective-permute-start | bytes 2359304 | tf_op jit(solution)/shard_map/ppermute | solution.py:25
  301.9 142.8 %collective-permute-start.38 = (bf16[512,1024]{1,0:T(8,128)(2,1)}, bf16[512,1024]{1,0:T(8,128)(2,1)}, u32[]{:S(2)}, u32[]{:S(2)}) collective-permute-start(bf16[512,1024]{1,0:T(8,128)(2,1)} %pad_maximum_fusion.8), channel_id=1, source_target_pairs={{0,4},{4,0},{8,12},{12,8},{16,20},{20,16},{24,28},{28,24},{1,5},{5... | collective-permute-start | bytes 3145736 | tf_op jit(solution)/shard_map/ppermute | solution.py:25
  397.9 64.4 %collective-permute-start.21 = (bf16[384,2048]{1,0:T(8,128)(2,1)S(1)}, bf16[384,2048]{1,0:T(8,128)(2,1)S(1)}, u32[]{:S(2)}, u32[]{:S(2)}) collective-permute-start(bf16[384,2048]{1,0:T(8,128)(2,1)S(1)} %convolution_convert_fusion.6), channel_id=1, source_target_pairs={{0,1},{1,0},{2,3},{3,2},{4,5},{5,4},{6,7},{7,6},{8,9},{9,8},{10,11... | collective-permute-start | bytes 4718600 | tf_op jit(solution)/shard_map/ppermute | solution.py:25
  402.1 61.6 %collective-permute-start.52 = (bf16[192,2048]{1,0:T(8,128)(2,1)}, bf16[192,2048]{1,0:T(8,128)(2,1)S(1)}, u32[]{:S(2)}, u32[]{:S(2)}) collective-permute-start(bf16[192,2048]{1,0:T(8,128)(2,1)} %get-tuple-element.78), channel_id=1, source_target_pairs={{0,1},{1,0},{2,3},{3,2},{4,5},{5,4},{6,7},{7,6},{8,9},{9,8},{10,11... | collective-permute-start | bytes 2359304 | tf_op jit(solution)/shard_map/ppermute | solution.py:25
  404.3 115.6 %collective-permute-start.42 = (bf16[1280,512]{1,0:T(8,128)(2,1)S(1)}, bf16[1280,512]{1,0:T(8,128)(2,1)S(1)}, u32[]{:S(2)}, u32[]{:S(2)}) collective-permute-start(bf16[1280,512]{1,0:T(8,128)(2,1)S(1)} %copy-done.50), channel_id=1, source_target_pairs={{0,4},{4,0},{8,12},{12,8},{16,20},{20,16},{24,28},{28,24},{1,5},{5... | collective-permute-start | bytes 3932168 | tf_op jit(solution)/shard_map/ppermute | solution.py:25
  467.3 70.1 %collective-permute-start.35 = (bf16[512,768]{1,0:T(8,128)(2,1)}, bf16[512,768]{1,0:T(8,128)(2,1)S(1)}, u32[]{:S(2)}, u32[]{:S(2)}) collective-permute-start(bf16[512,768]{1,0:T(8,128)(2,1)} %collective-permute-done.33), channel_id=1, source_target_pairs={{0,4},{4,0},{8,12},{12,8},{16,20},{20,16},{24,28},{28,24},{1,5},{5... | collective-permute-start | bytes 2359304 | tf_op jit(solution)/shard_map/ppermute | solution.py:25
  711.8 64.2 %collective-permute-start.91 = (bf16[1280,512]{1,0:T(8,128)(2,1)S(1)}, bf16[1280,512]{1,0:T(8,128)(2,1)S(1)}, u32[]{:S(2)}, u32[]{:S(2)}) collective-permute-start(bf16[1280,512]{1,0:T(8,128)(2,1)S(1)} %copy-done.115), channel_id=1, source_target_pairs={{0,4},{4,0},{8,12},{12,8},{16,20},{20,16},{24,28},{28,24},{1,5},{5... | collective-permute-start | bytes 3932168 | tf_op jit(solution)/shard_map/ppermute | solution.py:25
  716.6 78.7 %collective-permute-start.82 = (bf16[512,768]{1,0:T(8,128)(2,1)}, bf16[512,768]{1,0:T(8,128)(2,1)S(1)}, u32[]{:S(2)}, u32[]{:S(2)}) collective-permute-start(bf16[512,768]{1,0:T(8,128)(2,1)} %convolution_convert_fusion.19), channel_id=1, source_target_pairs={{0,4},{4,0},{8,12},{12,8},{16,20},{20,16},{24,28},{28,24},{1,5},{5... | collective-permute-start | bytes 2359304 | tf_op jit(solution)/shard_map/ppermute | solution.py:25
  717.6 162.8 %collective-permute-start.98 = (bf16[512,1024]{1,0:T(8,128)(2,1)}, bf16[512,1024]{1,0:T(8,128)(2,1)}, u32[]{:S(2)}, u32[]{:S(2)}) collective-permute-start(bf16[512,1024]{1,0:T(8,128)(2,1)} %convolution_convert_fusion.15), channel_id=1, source_target_pairs={{0,4},{4,0},{8,12},{12,8},{16,20},{20,16},{24,28},{28,24},{1,5},{5... | collective-permute-start | bytes 3145736 | tf_op jit(solution)/shard_map/ppermute | solution.py:25
  776.0 110.8 %collective-permute-start.44 = (bf16[384,2048]{1,0:T(8,128)(2,1)}, bf16[384,2048]{1,0:T(8,128)(2,1)}, u32[]{:S(2)}, u32[]{:S(2)}) collective-permute-start(bf16[384,2048]{1,0:T(8,128)(2,1)} %convolution_convert_fusion.5), channel_id=1, source_target_pairs={{0,1},{1,0},{2,3},{3,2},{4,5},{5,4},{6,7},{7,6},{8,9},{9,8},{10,11... | collective-permute-start | bytes 4718600 | tf_op jit(solution)/shard_map/ppermute | solution.py:25
  780.5 123.3 %collective-permute-start.56 = (bf16[384,2048]{1,0:T(8,128)(2,1)}, bf16[384,2048]{1,0:T(8,128)(2,1)}, u32[]{:S(2)}, u32[]{:S(2)}) collective-permute-start(bf16[384,2048]{1,0:T(8,128)(2,1)} %convolution_convert_fusion.11), channel_id=1, source_target_pairs={{0,1},{1,0},{2,3},{3,2},{4,5},{5,4},{6,7},{7,6},{8,9},{9,8},{10,11... | collective-permute-start | bytes 4718600 | tf_op jit(solution)/shard_map/ppermute | solution.py:25
  795.4 86.1 %collective-permute-start.100 = (bf16[512,1024]{1,0:T(8,128)(2,1)}, bf16[512,1024]{1,0:T(8,128)(2,1)}, u32[]{:S(2)}, u32[]{:S(2)}) collective-permute-start(bf16[512,1024]{1,0:T(8,128)(2,1)} %add_convert_fusion.1), channel_id=1, source_target_pairs={{0,16},{4,20},{8,24},{12,28},{16,0},{20,4},{24,8},{28,12},{1,17},{... | collective-permute-start | bytes 3145736 | tf_op jit(solution)/shard_map/ppermute | solution.py:25
  897.9 102.7 %collective-permute-start.46 = (bf16[192,2048]{1,0:T(8,128)(2,1)S(1)}, bf16[192,2048]{1,0:T(8,128)(2,1)S(1)}, u32[]{:S(2)}, u32[]{:S(2)}) collective-permute-start(bf16[192,2048]{1,0:T(8,128)(2,1)S(1)} %copy-done.60), channel_id=1, source_target_pairs={{0,2},{1,3},{2,0},{3,1},{4,6},{5,7},{6,4},{7,5},{8,10},{9,11},{10,... | collective-permute-start | bytes 2359304 | tf_op jit(solution)/shard_map/ppermute | solution.py:25
  920.3 80.3 %collective-permute-start.48 = (bf16[192,2048]{1,0:T(8,128)(2,1)S(1)}, bf16[192,2048]{1,0:T(8,128)(2,1)S(1)}, u32[]{:S(2)}, u32[]{:S(2)}) collective-permute-start(bf16[192,2048]{1,0:T(8,128)(2,1)S(1)} %fusion.44), channel_id=1, source_target_pairs={{0,8},{4,12},{8,0},{12,4},{16,24},{20,28},{24,16},{28,20},{1,9},{5... | collective-permute-start | bytes 2359304 | tf_op jit(solution)/shard_map/ppermute | solution.py:25
  1122.5 111.8 %collective-permute-start.78 = (bf16[512,768]{1,0:T(8,128)(2,1)S(1)}, bf16[512,768]{1,0:T(8,128)(2,1)S(1)}, u32[]{:S(2)}, u32[]{:S(2)}) collective-permute-start(bf16[512,768]{1,0:T(8,128)(2,1)S(1)} %convolution_convert_fusion.21), channel_id=1, source_target_pairs={{0,4},{4,0},{8,12},{12,8},{16,20},{20,16},{24,28},{28,24},{1,5},{5... | collective-permute-start | bytes 2359304 | tf_op jit(solution)/shard_map/ppermute | solution.py:25
  1123.6 153.6 %collective-permute-start.94 = (bf16[512,1024]{1,0:T(8,128)(2,1)}, bf16[512,1024]{1,0:T(8,128)(2,1)}, u32[]{:S(2)}, u32[]{:S(2)}) collective-permute-start(bf16[512,1024]{1,0:T(8,128)(2,1)} %convolution_convert_fusion.17), channel_id=1, source_target_pairs={{0,4},{4,0},{8,12},{12,8},{16,20},{20,16},{24,28},{28,24},{1,5},{5... | collective-permute-start | bytes 3145736 | tf_op jit(solution)/shard_map/ppermute | solution.py:25
  1124.6 77.8 %collective-permute-start.95 = (bf16[512,1024]{1,0:T(8,128)(2,1)S(1)}, bf16[512,1024]{1,0:T(8,128)(2,1)S(1)}, u32[]{:S(2)}, u32[]{:S(2)}) collective-permute-start(bf16[512,1024]{1,0:T(8,128)(2,1)S(1)} %copy-done.117), channel_id=1, source_target_pairs={{0,4},{4,0},{8,12},{12,8},{16,20},{20,16},{24,28},{28,24},{1,5},{5... | collective-permute-start | bytes 3145736 | tf_op jit(solution)/shard_map/ppermute | solution.py:25
  1125.7 104.4 %collective-permute-start.87 = (bf16[1280,512]{1,0:T(8,128)(2,1)S(1)}, bf16[1280,512]{1,0:T(8,128)(2,1)S(1)}, u32[]{:S(2)}, u32[]{:S(2)}) collective-permute-start(bf16[1280,512]{1,0:T(8,128)(2,1)S(1)} %copy-done.114), channel_id=1, source_target_pairs={{0,4},{4,0},{8,12},{12,8},{16,20},{20,16},{24,28},{28,24},{1,5},{5... | collective-permute-start | bytes 3932168 | tf_op jit(solution)/shard_map/ppermute | solution.py:25
  1140.6 99.9 %collective-permute-start.69 = (bf16[384,2048]{1,0:T(8,128)(2,1)S(1)}, bf16[384,2048]{1,0:T(8,128)(2,1)S(1)}, u32[]{:S(2)}, u32[]{:S(2)}) collective-permute-start(bf16[384,2048]{1,0:T(8,128)(2,1)S(1)} %convolution_convert_fusion.8), channel_id=1, source_target_pairs={{0,1},{1,0},{2,3},{3,2},{4,5},{5,4},{6,7},{7,6},{8,9},{9,8},{10,11... | collective-permute-start | bytes 4718600 | tf_op jit(solution)/shard_map/ppermute | solution.py:25
  1230.1 97.0 %collective-permute-start.86 = (bf16[1280,512]{1,0:T(8,128)(2,1)}, bf16[1280,512]{1,0:T(8,128)(2,1)}, u32[]{:S(2)}, u32[]{:S(2)}) collective-permute-start(bf16[1280,512]{1,0:T(8,128)(2,1)} %convolution_convert_fusion.3), channel_id=1, source_target_pairs={{0,4},{4,0},{8,12},{12,8},{16,20},{20,16},{24,28},{28,24},{1,5},{5... | collective-permute-start | bytes 3932168 | tf_op jit(solution)/shard_map/ppermute | solution.py:25
  1234.4 85.9 %collective-permute-start.68 = (bf16[384,2048]{1,0:T(8,128)(2,1)}, bf16[384,2048]{1,0:T(8,128)(2,1)}, u32[]{:S(2)}, u32[]{:S(2)}) collective-permute-start(bf16[384,2048]{1,0:T(8,128)(2,1)} %convolution_convert_fusion.9), channel_id=1, source_target_pairs={{0,1},{1,0},{2,3},{3,2},{4,5},{5,4},{6,7},{7,6},{8,9},{9,8},{10,11... | collective-permute-start | bytes 4718600 | tf_op jit(solution)/shard_map/ppermute | solution.py:25
  1238.9 76.1 %collective-permute-start.96 = (bf16[512,1024]{1,0:T(8,128)(2,1)}, bf16[512,1024]{1,0:T(8,128)(2,1)}, u32[]{:S(2)}, u32[]{:S(2)}) collective-permute-start(bf16[512,1024]{1,0:T(8,128)(2,1)} %add_convert_fusion.3), channel_id=1, source_target_pairs={{0,16},{4,20},{8,24},{12,28},{16,0},{20,4},{24,8},{28,12},{1,17},{... | collective-permute-start | bytes 3145736 | tf_op jit(solution)/shard_map/ppermute | solution.py:25
  1277.3 65.8 %collective-permute-start.88 = (bf16[1280,512]{1,0:T(8,128)(2,1)S(1)}, bf16[1280,512]{1,0:T(8,128)(2,1)S(1)}, u32[]{:S(2)}, u32[]{:S(2)}) collective-permute-start(bf16[1280,512]{1,0:T(8,128)(2,1)S(1)} %copy-done.113), channel_id=1, source_target_pairs={{0,16},{4,20},{8,24},{12,28},{16,0},{20,4},{24,8},{28,12},{1,17},{... | collective-permute-start | bytes 3932168 | tf_op jit(solution)/shard_map/ppermute | solution.py:25
  (211 other events, 6415.1 us)

commit v2 on v1

v2 whole, which is shorter than its diff:
```python
from functools import partial
import math

import jax
import jax.numpy as jnp
from jax import lax
from jax.experimental import pallas as pl
from jax.experimental.pallas import tpu as pltpu
from jax.sharding import PartitionSpec as P

HEAD_DIM = 64
ROT = 32
BLOCK = 128
LANES = 128
TILE = 256
MID = 1

TICK = 1_200_000_000

neg_large = -1e30
f32 = jnp.float32
bf16 = jnp.bfloat16


def swap(value, axis, bit):
    size = lax.axis_size(axis)
    return lax.ppermute(value, axis, [(i, i ^ (1 << bit)) for i in range(size)])


def tick_kernel(in_ref, out_ref):
    out_ref[0, 0] = in_ref[0, 0]


def tick(scalar, count):
    spec = pl.BlockSpec(memory_space=pltpu.SMEM)
    result = pl.pallas_call(
        tick_kernel,
        in_specs=[spec],
        out_specs=spec,
        out_shape=jax.ShapeDtypeStruct((1, 1), f32),
        cost_estimate=pl.CostEstimate(flops=count * TICK, bytes_accessed=0, transcendentals=0),
    )(scalar.reshape(1, 1))
    return result[0, 0]


class Sequence:
    def __init__(self, scalar, always):
        self.scalar = scalar
        self.always = always

    def gate(self, *values):
        *values, self.scalar = lax.optimization_barrier((*values, self.scalar))
        return values

    def run(self, step, *values, apart=False):
        values = self.gate(*values)
        if apart:
            shapes = jax.eval_shape(step, *values)

            def never(*others):
                return jax.tree.map(lambda shape: jnp.zeros(shape.shape, shape.dtype), shapes)

            result = lax.cond(self.always, step, never, *values)
        else:
            result = step(*values)
        leaves, tree = jax.tree.flatten(result)
        return jax.tree.unflatten(tree, self.gate(*leaves))

    def start(self, value, axis, bit):
        (value,) = self.gate(value)
        return swap(value, axis, bit)

    def wait(self, value):
        (value,) = self.gate(value)
        return value

    def settle(self, step, *values, beside=None):
        def both(*moved):
            return (step(*moved), beside()) if beside else step(*moved)

        return self.run(both, *values, apart=True)

    def tick(self, count):
        self.scalar = tick(self.scalar, count)

    def swap(self, value, axis, bit):
        return self.settle(lambda moved: swap(moved, axis, bit), value)


def side_bits():
    count = (lax.axis_size("dp") - 1).bit_length()
    return [bit for bit in range(count - 1, MID, -1)] + [0]


def slice_order():
    sides = side_bits()
    me = lax.axis_index("dp")
    base = me - (((me >> MID) & 1) << MID)
    order = []
    for k in range(1 << len(sides)):
        mask = sum(((k >> s) & 1) << bit for s, bit in enumerate(sides))
        for mid in range(2):
            order.append((base ^ mask) | (mid << MID))
    return jnp.stack(order).astype(jnp.int32)


def slice_places():
    sides = side_bits()
    every = jnp.arange(lax.axis_size("dp"), dtype=jnp.int32)
    apart = every ^ lax.axis_index("dp")
    place = (every >> MID) & 1
    for s, bit in enumerate(sides):
        place = place + (((apart >> bit) & 1) << (s + 1))
    return place


def pick(pair_first, pair_second, bit):
    return jnp.where(bit == 0, pair_first, pair_second)


def pair_up(keep, received, bit, axis):
    return jnp.concatenate(
        [pick(keep, received, bit), pick(received, keep, bit)], axis=axis
    )


class Spread:
    def __init__(self, seq, block, axis):
        self.seq, self.axis = seq, axis
        self.sides = side_bits()
        self.far_count = 1 << (len(self.sides) - 1)
        self.blocks = {0: block}

    def move(self, ks):
        for k in ks:
            if k != ks[0]:
                self.arrived(ks)
            s = k.bit_length() - 1
            self.blocks[k] = self.seq.start(self.blocks[k - (1 << s)], "dp", self.sides[s])

    def arrived(self, ks):
        last = max(k for k in ks if k in self.blocks)
        self.blocks[last] = self.seq.wait(self.blocks[last])

    def far(self):
        self.move(range(1, self.far_count))

    def far_wait(self):
        self.arrived(range(1, self.far_count))

    def near(self):
        self.move([self.far_count])

    def near_wait(self):
        self.arrived([self.far_count])

    def last(self):
        self.move(range(self.far_count + 1, 2 * self.far_count))

    def last_wait(self):
        self.arrived(range(self.far_count + 1, 2 * self.far_count))

    def plain(self, window=None):
        parts = [self.blocks[k] for k in sorted(self.blocks)]
        return assemble(parts, self.axis, window)

    def whole(self, window=None):
        parts = [self.blocks[k] for k in sorted(self.blocks)]
        return self.seq.run(lambda *values: assemble(values, self.axis, window), *parts)


class Reduce:
    def __init__(self, seq, product, *operands):
        self.seq, self.product, self.operands = seq, product, operands
        self.sides = side_bits()
        self.count = 1 << len(self.sides)
        self.blocks = {}
        self.arrived = [[] for _ in range(self.count)]
        self.moving = {}

    def make(self, ks):
        for k in ks:
            values = (*self.operands, *self.arrived[k])
            self.blocks[k] = self.seq.run(partial(self.product, k), *values)

    def plain(self, ks):
        return [self.product(k, *self.operands, *self.arrived[k]) for k in ks]

    def take(self, ks, made):
        self.blocks.update(zip(ks, made))

    def send(self, ks):
        for i, k in enumerate(ks):
            if i:
                self.wait([ks[i - 1]])
            s = k.bit_length() - 1
            self.moving[k] = self.seq.start(self.blocks[k], "dp", self.sides[s])

    def wait(self, ks):
        k = ks[-1]
        s = k.bit_length() - 1
        self.arrived[k - (1 << s)].append(self.seq.wait(self.moving[k]))

    def near(self, half):
        whole = list(reversed(range(self.count // 2, self.count)))
        middle = len(whole) // 2
        return whole[middle:] if half else whole[:middle]

    def far(self):
        return list(reversed(range(1, self.count // 2)))

    def make_far(self, near_done=True):
        ks = self.far()
        if ks[-1] in self.blocks or not (near_done or len(ks) == 1):
            return
        for k in ks[:-1]:
            self.make([k])
            self.send([k])
            self.wait([k])
        self.make(ks[-1:])

    def send_far(self):
        self.send(self.far()[-1:])

    def wait_far(self):
        self.wait(self.far()[-1:])

    def finish(self):
        self.make([0])
        return self.blocks[0]


def gather_start(own):
    mid, across = swap(own, "dp", MID), swap(own, "tensor", 1)
    own, mid, across = lax.optimization_barrier((own, mid, across))
    return own, mid, across, swap(own, "tensor", 0), swap(across, "tensor", 0)


def gather_start_with(own, low, core, sent):
    mid, across = swap(own, "dp", MID), swap(own, "tensor", 1)
    low, core, across = lax.optimization_barrier((low, core, across))
    later, x_high = sent(low, core)
    own, mid, across, x_high = lax.optimization_barrier((own, mid, across, x_high))
    core_parts = swap(own, "tensor", 0), swap(across, "tensor", 0)
    return (later, x_high), (own, mid, across, *core_parts)


def gather_finish(own, mid, across, core_own, core_across):
    both, core_mid = swap(mid, "tensor", 1), swap(mid, "tensor", 0)
    core_both = swap(both, "tensor", 0)
    parts = (own, mid, across, both, core_own, core_mid, core_across, core_both)
    return assemble(parts, 0)


class Gather:
    def __init__(self, seq, own, beside=None):
        self.seq = seq
        self.parts = seq.settle(gather_start, own, beside=beside)
        if beside:
            self.parts, self.beside = self.parts

    def finish(self, beside=None):
        return self.seq.settle(gather_finish, *self.parts, beside=beside)


def gather_start_beside(mine, mid):
    own, near, across = mine, swap(mine, "dp", MID), swap(mine, "tensor", 1)
    across, mid = lax.optimization_barrier((across, mid))
    both = swap(mid, "tensor", 1)
    own, near, across, both = lax.optimization_barrier((own, near, across, both))
    return (own, near, across, swap(own, "tensor", 0), swap(across, "tensor", 0)), both


def gather_finish_beside(parts, other):
    own, mid, across, core_own, core_across = parts
    other_own, other_mid, other_across, other_both, other_core_own, other_core_across = other
    both, core_mid = swap(mid, "tensor", 1), swap(mid, "tensor", 0)
    core_mid, other_mid = lax.optimization_barrier((core_mid, other_mid))
    other_core_mid = swap(other_mid, "tensor", 0)
    other_core_mid, other_both = lax.optimization_barrier((other_core_mid, other_both))
    other_core_both = swap(other_both, "tensor", 0)
    both, other_core_both = lax.optimization_barrier((both, other_core_both))
    core_both = swap(both, "tensor", 0)
    mine = (own, mid, across, both, core_own, core_mid, core_across, core_both)
    others = (other_own, other_mid, other_across, other_both)
    others += (other_core_own, other_core_mid, other_core_across, other_core_both)
    return assemble(others, 0), assemble(mine, 0)


class Scatter:
    def __init__(self, seq, product, operands, rows):
        self.seq, self.product, self.operands, self.rows = seq, product, operands, rows

    def begin(self):
        high = self.seq.run(lambda *values: self.product(*values, 1, bf16), *self.operands)
        self.core, self.low_part = self.seq.settle(
            lambda high: swap(high, "tensor", 0),
            high,
            beside=lambda: self.product(*self.operands, 0, f32),
        )

    def plain(self):
        high = self.product(*self.operands, 1, bf16)
        return self.product(*self.operands, 0, f32), swap(high, "tensor", 0)

    def take(self, made):
        self.low_part, self.core = made

    def chunk(self, low, core, k, *others):
        at = slice(k * self.rows, (k + 1) * self.rows)
        part = low[at] + core[at].astype(f32)
        for value in others:
            part = part + value.astype(f32)
        return part

    def sent(self, low, core):
        return tuple(self.chunk(low, core, k).astype(bf16) for k in (2, 3))

    def next(self, low, core, other):
        return self.chunk(low, core, 1, other).astype(bf16)

    def second(self, beside=None):
        def step(low, core):
            later, first = self.sent(low, core)
            return later, swap(first, "tensor", 1)

        moved = self.seq.settle(step, self.low_part, self.core, beside=beside)
        if beside:
            moved, made = moved
        self.later, self.x_high = moved
        return made if beside else None

    def third_step(self, low, core, other, later):
        return swap(self.next(low, core, other), "dp", MID), swap(later, "tensor", 1)

    def third(self, beside=None):
        values = (self.low_part, self.core, self.x_high, self.later)
        moved = self.seq.settle(self.third_step, *values, beside=beside)
        if beside:
            moved, made = moved
        self.mid, self.x_low = moved
        return made if beside else None

    def sent_across(self, low, core):
        later, first = self.sent(low, core)
        return later, swap(first, "tensor", 1)

    def finish(self, step, *others):
        return self.seq.run(step, self.low_part, self.core, self.x_low, self.mid, *others)


def order_kernel(back, order_ref, in_ref, out_ref):
    count = order_ref.shape[0]
    part = in_ref.shape[1] // count
    for i in range(count):
        there = pl.ds(pl.multiple_of(order_ref[i] * part, LANES), part)
        here = slice(i * part, (i + 1) * part)
        if back:
            out_ref[:, there] = in_ref[:, here].astype(out_ref.dtype)
        else:
            out_ref[:, here] = in_ref[:, there].astype(out_ref.dtype)


def reorder(value, order, dtype, back=False):
    rows, width = value.shape
    count = order.shape[0]
    part = width // count
    if part % LANES:
        blocks = value.reshape(rows, count, part)
        index = slice_places() if back else order
        return jnp.take(blocks, index, axis=1).reshape(rows, width).astype(dtype)
    spec = pl.BlockSpec((rows, width), lambda i, order_ref: (0, 0))
    return pl.pallas_call(
        partial(order_kernel, back),
        grid_spec=pltpu.PrefetchScalarGridSpec(
            num_scalar_prefetch=1, grid=(1,), in_specs=[spec], out_specs=spec
        ),
        out_shape=jax.ShapeDtypeStruct((rows, width), dtype),
    )(order, value)


def assemble_kernel(axis, window, *refs):
    parts, out_ref, held, in_sems, out_sems = refs[:-4], refs[-4], refs[-3], refs[-2], refs[-1]
    copies, at = [], 0
    for i, part in enumerate(parts):
        size = window[1] if axis else part.shape[0]
        where = (pl.ds(at, size),) if axis == 0 else (slice(None), pl.ds(at, size))
        copies.append(
            (
                pltpu.make_async_copy(
                    part.at[:, pl.ds(*window)], held.at[where], in_sems.at[i]
                ),
                pltpu.make_async_copy(held.at[where], out_ref.at[where], out_sems.at[i]),
            )
        )
        at += size
    for come, go in copies:
        come.start()
    for come, go in copies:
        come.wait()
        go.start()
    for come, go in copies:
        go.wait()


def assemble(parts, axis, window=None):
    rows, width = parts[0].shape
    window = window or (0, width)
    count = len(parts)
    shape = (rows * count, window[1]) if axis == 0 else (rows, window[1] * count)
    if window[1] % LANES or window[0] % LANES:
        return jnp.concatenate(
            [part[:, window[0] : window[0] + window[1]] for part in parts], axis=axis
        )
    return pl.pallas_call(
        partial(assemble_kernel, axis, window),
        in_specs=[pl.BlockSpec(memory_space=pl.ANY)] * count,
        out_specs=pl.BlockSpec(memory_space=pl.ANY),
        out_shape=jax.ShapeDtypeStruct(shape, parts[0].dtype),
        scratch_shapes=[
            pltpu.VMEM(shape, parts[0].dtype),
            pltpu.SemaphoreType.DMA((count,)),
            pltpu.SemaphoreType.DMA((count,)),
        ],
        compiler_params=pltpu.CompilerParams(vmem_limit_bytes=16 << 20),
        cost_estimate=pl.CostEstimate(flops=0, bytes_accessed=0, transcendentals=0),
    )(*parts)


def norm_kernel(
    low_ref, core_ref, x_ref, mid_ref, old_ref, shift_ref, gain_ref, bias_ref, stream_ref, out_ref
):
    branch = low_ref[...] + core_ref[...].astype(f32) + x_ref[...].astype(f32)
    stream = old_ref[...] + (branch + mid_ref[...].astype(f32)) + shift_ref[...]
    stream_ref[...] = stream
    centre = stream - jnp.mean(stream, axis=1, keepdims=True)
    spread_of = jnp.mean(centre * centre, axis=1, keepdims=True)
    out_ref[...] = (
        centre * lax.rsqrt(spread_of + 1e-05) * gain_ref[...] + bias_ref[...]
    ).astype(bf16)


def norm_back_kernel(
    low_ref, core_ref, x_ref, mid_ref, grad_ref, old_ref, gain_ref, sums_ref, grad_out_ref, out_ref
):
    normed_grad = low_ref[...] + core_ref[...].astype(f32) + x_ref[...].astype(f32)
    normed_grad = normed_grad + mid_ref[...].astype(f32)
    grad, old = grad_ref[...].astype(f32), old_ref[...]
    centre = old - jnp.mean(old, axis=1, keepdims=True)
    root = lax.rsqrt(jnp.mean(centre * centre, axis=1, keepdims=True) + 1e-05)
    hat = centre * root
    scaled = normed_grad * gain_ref[...]
    back = scaled - jnp.mean(scaled, axis=1, keepdims=True)
    back = root * (back - hat * jnp.mean(scaled * hat, axis=1, keepdims=True))
    result = grad + back
    grad_out_ref[...] = result
    out_ref[...] = result.astype(bf16)

    @pl.when(pl.program_id(0) == 0)
    def clear():
        sums_ref[...] = jnp.zeros_like(sums_ref)

    sums_ref[0:1, :] += jnp.sum(normed_grad * hat, axis=0, keepdims=True)
    sums_ref[1:2, :] += jnp.sum(normed_grad, axis=0, keepdims=True)
    sums_ref[2:3, :] += jnp.sum(grad, axis=0, keepdims=True)


def norm_first_kernel(order_ref, in_ref, gain_ref, bias_ref, stream_ref, out_ref):
    order_kernel(False, order_ref, in_ref, stream_ref)
    stream = stream_ref[...]
    centre = stream - jnp.mean(stream, axis=1, keepdims=True)
    spread_of = jnp.mean(centre * centre, axis=1, keepdims=True)
    out_ref[...] = (
        centre * lax.rsqrt(spread_of + 1e-05) * gain_ref[...] + bias_ref[...]
    ).astype(bf16)


def norm_first(value, order, gain, bias):
    rows, width = value.shape
    if width // order.shape[0] % LANES:
        stream = reorder(value, order, f32)
        centre = stream - jnp.mean(stream, axis=1, keepdims=True)
        spread_of = jnp.mean(centre * centre, axis=1, keepdims=True)
        return stream, (centre * lax.rsqrt(spread_of + 1e-05) * gain + bias).astype(bf16)
    steps = row_steps(rows)
    row_spec = pl.BlockSpec((rows // steps, width), lambda i, order_ref: (i, 0))
    line_spec = pl.BlockSpec((1, width), lambda i, order_ref: (0, 0))
    return call(
        norm_first_kernel,
        (order, value, gain.reshape(1, width), bias.reshape(1, width)),
        (steps,),
        [row_spec, line_spec, line_spec],
        [row_spec, row_spec],
        [jax.ShapeDtypeStruct((rows, width), dtype) for dtype in (f32, bf16)],
        scalars=1,
    )


def row_steps(rows):
    return rows // 48 if rows % 48 == 0 else 1


def norm_call(kernel, rows, width, row_values, line_values, out_shapes):
    steps = row_steps(rows)
    row_spec = pl.BlockSpec((rows // steps, width), lambda i: (i, 0))
    line_spec = pl.BlockSpec((1, width), lambda i: (0, 0))
    sum_spec = pl.BlockSpec((8, width), lambda i: (0, 0))
    return pl.pallas_call(
        kernel,
        grid=(steps,),
        in_specs=[row_spec] * len(row_values) + [line_spec] * len(line_values),
        out_specs=[row_spec if shape.shape[0] == rows else sum_spec for shape in out_shapes],
        out_shape=out_shapes,
        compiler_params=pltpu.CompilerParams(vmem_limit_bytes=40 << 20),
        cost_estimate=pl.CostEstimate(flops=0, bytes_accessed=0, transcendentals=0),
    )(*row_values, *[value.reshape(1, width) for value in line_values])


def norm_after(low, core, x_low, mid, old, shift, gain, bias):
    rows, width = old.shape
    out = [jax.ShapeDtypeStruct((rows, width), dtype) for dtype in (f32, bf16)]
    return norm_call(
        norm_kernel, rows, width, (low, core, x_low, mid, old), (shift, gain, bias), out
    )


def norm_before(low, core, x_low, mid, grad, old, gain):
    rows, width = old.shape
    out = [jax.ShapeDtypeStruct((8, width), f32)]
    out += [jax.ShapeDtypeStruct((rows, width), dtype) for dtype in (f32, bf16)]
    return norm_call(norm_back_kernel, rows, width, (low, core, x_low, mid, grad, old), (gain,), out)


def layout(lens, total, block):
    steps_index = jnp.arange(total, dtype=jnp.int32)
    blocks_first = (lens[0] + block - 1) // block
    second_start = blocks_first * block
    in_first = steps_index < lens[0]
    in_second = (steps_index >= second_start) & (steps_index < second_start + lens[1])
    return jnp.where(in_first, steps_index, jnp.where(in_second, steps_index - second_start, 0))


def rotary_tables(position):
    half_rot = ROT // 2
    lane = jnp.arange(LANES, dtype=jnp.int32) % HEAD_DIM
    freqs = 10000.0 ** (-((lane % half_rot).astype(f32) * 2.0) / ROT)
    angles = position.astype(f32)[..., None] * freqs
    cosine, sine = jnp.cos(angles), jnp.sin(angles)
    return (
        jnp.where(lane < ROT, cosine, 1.0),
        jnp.where(lane < half_rot, -sine, 0.0),
        jnp.where((lane >= half_rot) & (lane < ROT), sine, 0.0),
    )


def turn(field, cos, above, below, back=False):
    up = pltpu.roll(field, LANES - ROT // 2, 1) * above
    down = pltpu.roll(field, ROT // 2, 1) * below
    return field * cos - (up + down) if back else field * cos + (up + down)


def allowed_bias(scalars, group, first_row, rows, cols):
    first_len, second_len = scalars[2 * group], scalars[2 * group + 1]
    second_start = ((first_len + BLOCK - 1) // BLOCK) * BLOCK
    row = first_row + lax.broadcasted_iota(jnp.int32, (rows, 1), 0)
    in_second = (row >= second_start) & (row < second_start + second_len)
    start = jnp.where(row < first_len, 0, jnp.where(in_second, second_start, row))
    col = lax.broadcasted_iota(jnp.int32, (rows, cols), 1)
    return jnp.where((col >= start) & (col <= row), 0.0, neg_large)


def chunk_places(scalars, rows):
    me = scalars[4]
    return [pl.multiple_of((me ^ ((r % 2) * 2 + r // 2)) * rows, 64) for r in range(4)]


def head_mask(head):
    lane = lax.broadcasted_iota(jnp.int32, (1, LANES), 1)
    return jnp.where(lane // HEAD_DIM == head, 1.0, 0.0).astype(bf16)


def nt(left, right):
    return lax.dot_general(left, right, (((1,), (1,)), ((), ())), preferred_element_type=f32)


def nn(left, right):
    return jnp.dot(left, right, preferred_element_type=f32)


def tn(left, right):
    return lax.dot_general(left, right, (((0,), (0,)), ((), ())), preferred_element_type=f32)


def attention_kernel(
    scalars, mixed_ref, cos_ref, above_ref, below_ref, out_ref, kept_ref, sums_ref, held
):
    group = pl.program_id(0)
    rows = mixed_ref.shape[2]
    width = mixed_ref.shape[3] // 3
    total = 4 * rows
    places = chunk_places(scalars, rows)
    for r in range(4):
        at = pl.ds(places[r], rows)
        cos, above, below = cos_ref[0, at, :], above_ref[0, at, :], below_ref[0, at, :]
        for part in range(0, 2 * width, LANES):
            turned = turn(mixed_ref[r, 0, :, part : part + LANES], cos, above, below)
            if part < width:
                turned = turned.astype(bf16) * HEAD_DIM**-0.5
            kept_ref[0, at, part : part + LANES] = turned.astype(bf16)
        kept_ref[0, at, 2 * width :] = mixed_ref[r, 0, :, 2 * width :].astype(bf16)
    for first in range(0, total, TILE):
        cols = first + TILE
        bias = allowed_bias(scalars, group, first, TILE, cols)
        for pair in range(0, width, LANES):
            query = kept_ref[0, first:cols, pair : pair + LANES]
            key = kept_ref[0, :cols, width + pair : width + pair + LANES]
            value = kept_ref[0, :cols, 2 * width + pair : 2 * width + pair + LANES]
            result = None
            for head in range(LANES // HEAD_DIM):
                mask = head_mask(head)
                scores = nt(query * mask, key) + bias
                top = jnp.max(scores, axis=1, keepdims=True)
                expo = jnp.exp(scores - top)
                mass = jnp.sum(expo, axis=1, keepdims=True)
                probs16 = (expo * (1.0 / mass)).astype(bf16)
                mine = nn(probs16, value * mask)
                result = mine if result is None else result + mine
                at_head = pair // HEAD_DIM + head
                sums_ref[0, first:cols, at_head : at_head + 1] = top + jnp.log(mass)
            held[first:cols, pair : pair + LANES] = result.astype(bf16)
    for r in range(4):
        out_ref[r, 0] = held[pl.ds(places[r], rows), :]


def attention_back_kernel(
    scalars,
    kept_ref,
    sums_ref,
    grad_ref,
    cos_ref,
    above_ref,
    below_ref,
    out_ref,
    held,
    query_grad,
    key_grad,
    value_grad,
):
    group = pl.program_id(0)
    rows = grad_ref.shape[2]
    width = grad_ref.shape[3]
    total = 4 * rows
    places = chunk_places(scalars, rows)
    for r in range(4):
        held[pl.ds(places[r], rows), :] = grad_ref[r, 0]
    for first in reversed(range(0, total, TILE)):
        cols = first + TILE
        bias = allowed_bias(scalars, group, first, TILE, cols)
        for pair in range(0, width, LANES):
            lanes = slice(pair, pair + LANES)
            query = kept_ref[0, first:cols, pair : pair + LANES]
            key = kept_ref[0, :cols, width + pair : width + pair + LANES]
            value = kept_ref[0, :cols, 2 * width + pair : 2 * width + pair + LANES]
            grad = held[first:cols, lanes]
            grads = [None, None, None]
            for head in range(LANES // HEAD_DIM):
                mask = head_mask(head)
                at_head = pair // HEAD_DIM + head
                query_head, grad_head = query * mask, grad * mask
                scores = nt(query_head, key) + bias
                probs = jnp.exp(scores - sums_ref[0, first:cols, at_head : at_head + 1])
                prob_grad = nt(grad_head, value)
                mean = jnp.sum(probs * prob_grad, axis=1, keepdims=True)
                score_grad = (probs * (prob_grad - mean)).astype(bf16)
                mine = (
                    nn(score_grad, key * mask),
                    tn(score_grad, query_head),
                    tn(probs.astype(bf16), grad_head),
                )
                grads = [m if g is None else g + m for g, m in zip(grads, mine)]
            query_grad[first:cols, lanes] = grads[0]
            if cols == total:
                key_grad[:, lanes] = grads[1]
                value_grad[:, lanes] = grads[2]
            else:
                key_grad[:cols, lanes] += grads[1]
                value_grad[:cols, lanes] += grads[2]
    for r in range(4):
        at = pl.ds(places[r], rows)
        cos, above, below = cos_ref[0, at, :], above_ref[0, at, :], below_ref[0, at, :]
        for pair in range(0, width, LANES):
            query = turn(query_grad[at, pair : pair + LANES] * HEAD_DIM**-0.5, cos, above, below, True)
            key = turn(key_grad[at, pair : pair + LANES], cos, above, below, True)
            out_ref[r, 0, :, pair : pair + LANES] = query.astype(bf16)
            out_ref[r, 0, :, width + pair : width + pair + LANES] = key.astype(bf16)
        out_ref[r, 0, :, 2 * width :] = value_grad[at, :].astype(bf16)


def chunk_spec(rows, width):
    return pl.BlockSpec((4, 1, rows, width), lambda g, scalars: (0, g, 0, 0))


def group_spec(total, width):
    return pl.BlockSpec((1, total, width), lambda g, scalars: (g, 0, 0))


def attention_forward(mixed, tables, scalars, rows):
    width = mixed.shape[1] // 3
    total = 4 * rows
    attended, kept, sums = pl.pallas_call(
        attention_kernel,
        grid_spec=pltpu.PrefetchScalarGridSpec(
            num_scalar_prefetch=1,
            grid=(2,),
            in_specs=[chunk_spec(rows, 3 * width)] + [group_spec(total, LANES)] * 3,
            out_specs=[
                chunk_spec(rows, width),
                group_spec(total, 3 * width),
                group_spec(total, LANES),
            ],
            scratch_shapes=[pltpu.VMEM((total, width), bf16)],
        ),
        out_shape=[
            jax.ShapeDtypeStruct((4, 2, rows, width), bf16),
            jax.ShapeDtypeStruct((2, total, 3 * width), bf16),
            jax.ShapeDtypeStruct((2, total, LANES), f32),
        ],
        compiler_params=pltpu.CompilerParams(vmem_limit_bytes=40 << 20),
        cost_estimate=pl.CostEstimate(flops=0, bytes_accessed=0, transcendentals=0),
    )(scalars, mixed.reshape(4, 2, rows, 3 * width), *tables)
    return attended.reshape(8 * rows, width), kept, sums


def attention_backward(kept, sums, grad16, tables, scalars, rows):
    width = grad16.shape[1]
    total = 4 * rows
    mixed_grad = pl.pallas_call(
        attention_back_kernel,
        grid_spec=pltpu.PrefetchScalarGridSpec(
            num_scalar_prefetch=1,
            grid=(2,),
            in_specs=[
                group_spec(total, 3 * width),
                group_spec(total, LANES),
                chunk_spec(rows, width),
            ]
            + [group_spec(total, LANES)] * 3,
            out_specs=chunk_spec(rows, 3 * width),
            scratch_shapes=[pltpu.VMEM((total, width), bf16)]
            + [pltpu.VMEM((total, width), f32)] * 3,
        ),
        out_shape=jax.ShapeDtypeStruct((4, 2, rows, 3 * width), bf16),
        compiler_params=pltpu.CompilerParams(vmem_limit_bytes=40 << 20),
        cost_estimate=pl.CostEstimate(flops=0, bytes_accessed=0, transcendentals=0),
    )(scalars, kept, sums, grad16.reshape(4, 2, rows, width), *tables)
    return mixed_grad.reshape(8 * rows, 3 * width)


def call(kernel, args, grid, in_specs, out_specs, out_shape, scratch_shapes=(), scalars=0):
    return pl.pallas_call(
        kernel,
        grid_spec=pltpu.PrefetchScalarGridSpec(
            num_scalar_prefetch=scalars,
            grid=grid,
            in_specs=in_specs,
            out_specs=out_specs,
            scratch_shapes=scratch_shapes,
        ),
        out_shape=out_shape,
        compiler_params=pltpu.CompilerParams(vmem_limit_bytes=48 << 20),
        cost_estimate=pl.CostEstimate(flops=0, bytes_accessed=0, transcendentals=0),
    )(*args)


def mix_kernel(left_ref, right_ref, shift_ref, out_ref):
    out_ref[...] = nn(left_ref[...], right_ref[...]) + shift_ref[...]


def mix_product(normed, mixed_full, shift):
    rows, width = normed.shape
    cols = shift.shape[1]
    block = rows // 3
    return call(
        mix_kernel,
        (normed, mixed_full, shift.reshape(1, cols)),
        (3,),
        [
            pl.BlockSpec((block, width), lambda i: (i, 0)),
            pl.BlockSpec((width, cols), lambda i: (0, 0)),
            pl.BlockSpec((1, cols), lambda i: (0, 0)),
        ],
        pl.BlockSpec((block, cols), lambda i: (i, 0)),
        jax.ShapeDtypeStruct((rows, cols), f32),
    )


def hide_kernel(left_ref, right_ref, shift_ref, out_ref, slope_ref):
    value = nn(left_ref[...], right_ref[...]) + shift_ref[...]
    inner = math.sqrt(2.0 / math.pi)
    square = value * value
    bend = jnp.tanh(inner * value * (1.0 + 0.044715 * square))
    half = 0.5 * (1.0 + bend)
    out_ref[...] = (value * half).astype(bf16)
    slope = 0.5 * value * (1.0 - bend * bend) * (inner * (1.0 + 3.0 * 0.044715 * square))
    slope_ref[...] = (half + slope).astype(slope_ref.dtype)


def hide_product(normed, up_full, shift):
    rows, width = normed.shape
    cols = up_full.shape[1]
    block = rows // 6
    out = pl.BlockSpec((block, cols), lambda i: (i, 0))
    return call(
        hide_kernel,
        (normed, up_full, shift.reshape(1, cols)),
        (6,),
        [
            pl.BlockSpec((block, width), lambda i: (i, 0)),
            pl.BlockSpec((width, cols), lambda i: (0, 0)),
            pl.BlockSpec((1, cols), lambda i: (0, 0)),
        ],
        [out, out],
        [jax.ShapeDtypeStruct((rows, cols), dtype) for dtype in (bf16, f32)],
    )


def out_kernel(first_ref, second_ref, dense_ref, down_ref, out_ref):
    value = nt(first_ref[...], dense_ref[...]) + nn(second_ref[...], down_ref[...])
    out_ref[...] = value.astype(out_ref.dtype)


def out_product(attended, hidden, mixed_full, down_full, half, dtype):
    rows, width = attended.shape[0] // 2, down_full.shape[1]
    heads = attended.shape[1]
    return call(
        out_kernel,
        (attended, hidden, mixed_full, down_full),
        (width // 512,),
        [
            pl.BlockSpec((rows, heads), lambda j: (half, 0)),
            pl.BlockSpec((rows, hidden.shape[1]), lambda j: (half, 0)),
            pl.BlockSpec((512, heads), lambda j: (j, 3)),
            pl.BlockSpec((hidden.shape[1], 512), lambda j: (0, j)),
        ],
        pl.BlockSpec((rows, 512), lambda j: (0, j)),
        jax.ShapeDtypeStruct((rows, width), dtype),
    )


def nn_kernel(left_ref, right_ref, out_ref):
    out_ref[...] = nn(left_ref[...], right_ref[...]).astype(out_ref.dtype)


def nt_scaled_kernel(left_ref, right_ref, slope_ref, out_ref):
    value = nt(left_ref[...], right_ref[...]) * slope_ref[...].astype(f32)
    out_ref[...] = value.astype(out_ref.dtype)


def attended_back(grad16, mixed_full, heads):
    rows, width = grad16.shape
    block = rows // 3
    return call(
        nn_kernel,
        (grad16, mixed_full),
        (3,),
        [
            pl.BlockSpec((block, width), lambda i: (i, 0)),
            pl.BlockSpec((width, heads), lambda i: (0, 3)),
        ],
        pl.BlockSpec((block, heads), lambda i: (i, 0)),
        jax.ShapeDtypeStruct((rows, heads), bf16),
    )


def hidden_back(grad16, down_full, slope):
    rows, width = grad16.shape
    cols = slope.shape[1]
    block = rows // 2
    spec = pl.BlockSpec((block, 256), lambda i, j: (i, j))
    return call(
        nt_scaled_kernel,
        (grad16, down_full, slope),
        (2, cols // 256),
        [
            pl.BlockSpec((block, width), lambda i, j: (i, 0)),
            pl.BlockSpec((256, width), lambda i, j: (j, 0)),
            spec,
        ],
        spec,
        jax.ShapeDtypeStruct((rows, cols), bf16),
    )


def both_kernel(first_ref, second_ref, proj_ref, up_ref, out_ref):
    value = nt(first_ref[...], proj_ref[...]) + nt(second_ref[...], up_ref[...])
    out_ref[...] = value.astype(out_ref.dtype)


def normed_back(mixed_grad, pre_grad, mixed_full, up_full, half, dtype):
    rows, width = mixed_grad.shape[0] // 2, up_full.shape[0]
    return call(
        both_kernel,
        (mixed_grad, pre_grad, mixed_full, up_full),
        (width // 512,),
        [
            pl.BlockSpec((rows, mixed_grad.shape[1]), lambda j: (half, 0)),
            pl.BlockSpec((rows, pre_grad.shape[1]), lambda j: (half, 0)),
            pl.BlockSpec((512, mixed_grad.shape[1]), lambda j: (j, 0)),
            pl.BlockSpec((512, up_full.shape[1]), lambda j: (j, 0)),
        ],
        pl.BlockSpec((rows, 512), lambda j: (0, j)),
        jax.ShapeDtypeStruct((rows, width), dtype),
    )


def in_grad_kernel(left_ref, right_ref, *refs):
    value = tn(left_ref[...], right_ref[...])
    for ref in refs[:-1]:
        value = value + ref[...].astype(f32)
    refs[-1][...] = value.astype(bf16)


def in_grad(part, k, normed, grad, *others):
    rows, cols = grad.shape
    block = min(part, 256)
    steps = part // block
    spec = pl.BlockSpec((block, cols), lambda i: (i, 0))
    return call(
        in_grad_kernel,
        (normed, grad, *others),
        (steps,),
        [
            pl.BlockSpec((rows, block), lambda i: (0, k * steps + i)),
            pl.BlockSpec((rows, cols), lambda i: (0, 0)),
        ]
        + [spec] * len(others),
        spec,
        jax.ShapeDtypeStruct((part, cols), bf16),
    )


def down_grad(part, k, hidden, grad, *others):
    rows, height = hidden.shape
    block = min(part, 256)
    steps = part // block
    spec = pl.BlockSpec((height, block), lambda j: (0, j))
    return call(
        in_grad_kernel,
        (hidden, grad, *others),
        (steps,),
        [
            pl.BlockSpec((rows, height), lambda j: (0, 0)),
            pl.BlockSpec((rows, block), lambda j: (0, k * steps + j)),
        ]
        + [spec] * len(others),
        spec,
        jax.ShapeDtypeStruct((height, part), bf16),
    )


def mixed_grad_kernel(normed_ref, mixed_ref, grad_ref, attended_ref, *refs):
    split = mixed_ref.shape[1]
    values = (tn(normed_ref[...], mixed_ref[...]), tn(grad_ref[...], attended_ref[...]))
    for value, cols in zip(values, (slice(0, split), slice(split, None))):
        for ref in refs[:-1]:
            value = value + ref[:, cols].astype(f32)
        refs[-1][:, cols] = value.astype(bf16)


def mixed_weight_grad(part, k, normed, mixed_grad, grad, attended, *others):
    rows, heads = attended.shape
    width = mixed_grad.shape[1] + heads
    block = min(part, 256)
    steps = part // block
    spec = pl.BlockSpec((block, width), lambda i: (i, 0))
    slice_spec = pl.BlockSpec((rows, block), lambda i: (0, k * steps + i))
    return call(
        mixed_grad_kernel,
        (normed, mixed_grad, grad, attended, *others),
        (steps,),
        [
            slice_spec,
            pl.BlockSpec(mixed_grad.shape, lambda i: (0, 0)),
            slice_spec,
            pl.BlockSpec(attended.shape, lambda i: (0, 0)),
        ]
        + [spec] * len(others),
        spec,
        jax.ShapeDtypeStruct((part, width), bf16),
    )


def halves_kernel(axis, mid_ref, keep_ref, other_ref, *refs):
    out_ref, size = refs[-1], keep_ref.shape[axis]
    for part_ref, half in ((keep_ref, mid_ref[0]), (other_ref, 1 - mid_ref[0])):
        at = pl.ds(pl.multiple_of(half * size, LANES), size)
        if axis:
            out_ref[0, :, at] = part_ref[...].astype(f32)
        else:
            out_ref[0, at, :] = part_ref[...].astype(f32)


def place_halves(keep, other, mid, axis, layer, layers, before=None):
    rows, cols = keep.shape
    shape = (rows, 2 * cols) if axis else (2 * rows, cols)
    if cols % LANES or (axis == 0 and rows % LANES):
        line = jnp.concatenate([pick(keep, other, mid), pick(other, keep, mid)], axis=axis)
        line = line.astype(f32)[None]
        if before is None:
            return jnp.concatenate([jnp.zeros_like(line)] * layer + [line], axis=0)
        return jnp.concatenate([line, before[1:]], axis=0)
    spec = pl.BlockSpec((rows, cols), lambda i, mid_ref: (0, 0))
    given = [] if before is None else [before]
    return pl.pallas_call(
        partial(halves_kernel, axis),
        grid_spec=pltpu.PrefetchScalarGridSpec(
            num_scalar_prefetch=1,
            grid=(1,),
            in_specs=[spec, spec] + [pl.BlockSpec(memory_space=pl.ANY)] * len(given),
            out_specs=pl.BlockSpec((1, *shape), lambda i, mid_ref: (layer, 0, 0)),
        ),
        out_shape=jax.ShapeDtypeStruct((layers, *shape), f32),
        input_output_aliases={3: 0} if given else {},
        compiler_params=pltpu.CompilerParams(vmem_limit_bytes=32 << 20),
        cost_estimate=pl.CostEstimate(flops=0, bytes_accessed=0, transcendentals=0),
    )(mid.reshape(1), keep, other, *given)


def last_kernel(
    order_ref, low_ref, core_ref, x_ref, mid_ref, old_ref, shift_ref, out_ref, held
):
    branch = low_ref[...] + core_ref[...].astype(f32) + x_ref[...].astype(f32)
    held[...] = old_ref[...] + (branch + mid_ref[...].astype(f32)) + shift_ref[...]
    order_kernel(True, order_ref, held, out_ref)


def last_stream(order, low, core, x_low, mid, old, shift):
    rows, width = old.shape
    if width // order.shape[0] % LANES:
        branch = low[:rows] + core[:rows].astype(f32) + x_low.astype(f32) + mid.astype(f32)
        return reorder(old + branch + shift, order, f32, True)
    steps = row_steps(rows)
    row_spec = pl.BlockSpec((rows // steps, width), lambda i, order_ref: (i, 0))
    return call(
        last_kernel,
        (order, low, core, x_low, mid, old, shift),
        (steps,),
        [row_spec] * 5 + [pl.BlockSpec((1, width), lambda i, order_ref: (0, 0))],
        row_spec,
        jax.ShapeDtypeStruct((rows, width), f32),
        [pltpu.VMEM((rows // steps, width), f32)],
        scalars=1,
    )


def halves(value, half, axis):
    size = value.shape[axis] // 2
    return lax.dynamic_slice_in_dim(value, half * size, size, axis)


class Small:
    def __init__(self, seq, mine, tensor, mid):
        self.seq, self.tensor = seq, tensor
        self.mine = seq.settle(
            lambda mine: pair_up(mine, swap(mine, "dp", MID), mid, 0), mine[None]
        )

    def second(self):
        def step(mine):
            for bit in side_bits():
                mine = jnp.concatenate([mine, swap(mine, "dp", bit)], axis=0)
            return mine[None]

        self.mine = self.seq.settle(step, self.mine)

    def finish(self, unpack):
        def step(mine):
            for bit in (0, 1):
                mine = pair_up(mine, swap(mine, "tensor", bit), (self.tensor >> bit) & 1, 0)
            return unpack(jnp.swapaxes(mine, 0, 1))

        return self.seq.settle(step, self.mine)


class SmallSums:
    def __init__(self, seq, norm_grads, in_bgrads, mid):
        self.seq, self.mid = seq, mid
        self.norm_grads, self.in_bgrads = norm_grads, in_bgrads
        self.layers, self.kinds = len(norm_grads), 3
        self.sides = side_bits()

    def halve(self, sums, biases, axis, half, move):
        keep, sent = halves(sums, half, axis), halves(sums, 1 - half, axis)
        split = biases.shape[0]
        received = move(jnp.concatenate([biases, sent.reshape(-1)]))
        return keep + received[split:].reshape(keep.shape), received[:split]

    def side(self, s, sums, biases):
        sums, other = self.halve(
            sums, biases, 1, 0, lambda value: swap(value, "dp", self.sides[s])
        )
        return sums, biases + other

    def first(self):
        tensor = lax.axis_index("tensor")

        def step(*values):
            sums = jnp.stack([value[: self.kinds] for value in values[: self.layers]])
            biases = jnp.concatenate(values[self.layers :])
            shape = (self.layers * self.kinds, 1 << len(self.sides), 2, lax.axis_size("tensor"), -1)
            sums, biases = self.side(len(self.sides) - 1, sums.reshape(shape), biases)
            none = biases[:0]
            for bit in (1, 0):
                sums, _ = self.halve(
                    sums, none, 3, (tensor >> bit) & 1, lambda value: swap(value, "tensor", bit)
                )
            sums, other = self.halve(
                sums, biases, 2, self.mid, lambda value: swap(value, "dp", MID)
            )
            pair = (pick(biases, other, self.mid), pick(other, biases, self.mid))
            return sums, jnp.concatenate(pair)

        values = [value for pair in self.in_bgrads for value in pair]
        self.sums, self.biases = self.seq.settle(step, *self.norm_grads, *values)

    def finish(self):
        def step(sums, biases):
            for s in reversed(range(len(self.sides) - 1)):
                sums, biases = self.side(s, sums, biases)
            return sums, biases

        sums, biases = self.seq.settle(step, self.sums, self.biases)
        return sums.reshape(self.layers, self.kinds, -1), biases.reshape(2, -1)


def shards(
    tokens_in,
    lengths,
    norm_gain,
    norm_bias,
    proj_weight,
    proj_bias,
    dense_weight,
    dense_bias,
    up_weight,
    up_bias,
    down_weight,
    down_bias,
    cotangent,
):
    rows, width = tokens_in.shape
    layer_count = proj_weight.shape[0]
    n_dp = lax.axis_size("dp")
    dp = lax.axis_index("dp")
    tensor = lax.axis_index("tensor")
    mid = (dp >> MID) & 1
    order = slice_order()
    seq = Sequence(lengths[0, 0].astype(f32), lengths[0, 0] > 0)

    def take_mixed(l, half, weight=proj_weight):
        proj = halves(weight[l], half, 2).reshape(weight.shape[1], -1)
        return jnp.concatenate([proj, halves(dense_weight[l], half, 0).T], axis=1)

    def take_up(l, half, weight=up_weight):
        return halves(weight[l], half, 1)

    def take_down(l, half, weight=down_weight):
        return halves(weight[l], half, 0)

    takes = ((take_mixed, 0), (take_up, 0), (take_down, 1))

    def set_out(l, i):
        weight = (proj_weight, up_weight, down_weight)[i]
        part = seq.run(lambda value: takes[i][0](l, 1 - mid, value), weight, apart=True)
        return seq.start(part, "dp", MID)

    def paired(l, i, moving):
        return joined(l, i, seq.wait(moving))

    def joined(l, i, received):
        take, axis = takes[i]
        block = seq.run(
            lambda other: pair_up(take(l, mid), other, mid, axis), received, apart=True
        )
        return Spread(seq, block, axis)

    moving = [set_out(0, 0), set_out(0, 1)]
    whole_lens = lengths.reshape(-1).astype(f32)
    coarse = jnp.floor(whole_lens / 8.0)
    small = Small(
        seq,
        jnp.concatenate(
            [
                value.reshape(-1)
                for value in (norm_gain, norm_bias, dense_bias, down_bias, proj_bias, up_bias)
            ]
            + [coarse.astype(bf16), (whole_lens - 8.0 * coarse).astype(bf16)]
        ),
        tensor,
        mid,
    )
    small.second()
    m0 = paired(0, 0, moving[0])
    u0 = paired(0, 1, moving[1])
    m0.near()
    m0.far()
    cot = seq.run(lambda value: reorder(value, order, bf16), cotangent)
    each, proj_each, up_each = norm_gain.shape[1], proj_bias.shape[3], up_bias.shape[2]

    def unpack(everyone):
        pair_lens = lax.dynamic_index_in_dim(everyone[:2, :, -4:], tensor, 1, keepdims=False)
        pair_lens = pair_lens.astype(f32)
        pair_lens = (pair_lens[:, :2] * 8.0 + pair_lens[:, 2:]).astype(jnp.int32)
        lens = pick(pair_lens, pair_lens[::-1], mid)
        everyone = everyone[:, :, :-4]
        at = 4 * layer_count * each
        norm_parts = everyone[:, :, :at].reshape(n_dp, -1, 4 * layer_count, each)
        norm_parts = jnp.transpose(norm_parts, (2, 0, 1, 3)).reshape(4, layer_count, width)
        norm_parts = norm_parts.astype(f32)
        same_heads = lax.dynamic_index_in_dim(everyone[:, :, at:], tensor, 1, keepdims=False)
        same_heads = halves(same_heads[slice_places()], mid, 0).astype(f32)
        proj_at = layer_count * 3 * proj_each
        proj_shift = jnp.transpose(
            same_heads[:, :proj_at].reshape(-1, layer_count * 3, proj_each), (1, 0, 2)
        ).reshape(layer_count, -1)
        up_shift = jnp.transpose(
            same_heads[:, proj_at:].reshape(-1, layer_count, up_each), (1, 0, 2)
        ).reshape(layer_count, -1)
        gains, biases = norm_parts[0], norm_parts[1]
        shifts = norm_parts[2] + norm_parts[3]
        scalars = jnp.concatenate([lens.reshape(-1), tensor[None].astype(jnp.int32)])
        lines = [value[l] for value in (gains, biases, shifts) for l in range(layer_count)]
        lines += [value[l] for value in (proj_shift, up_shift) for l in range(layer_count)]
        return [line[None] for line in lines], lens, scalars.astype(jnp.int32)

    lines, lens, scalars = small.finish(unpack)
    gains, biases, out_shifts, proj_shift, up_shift = (
        lines[i * layer_count : (i + 1) * layer_count] for i in range(5)
    )

    def mix(l, normed, proj_full):
        return seq.run(mix_product, normed, proj_full, proj_shift[l])

    def attend(mixed):
        return seq.run(lambda value: attention_forward(value, tables, scalars, rows), mixed)

    def hide(l, normed, up_full):
        return seq.run(hide_product, normed, up_full, up_shift[l])

    def make_tables():
        return rotary_tables(jax.vmap(partial(layout, total=4 * rows, block=BLOCK))(lens))

    stream, own = seq.run(
        lambda value: norm_first(value, order, gains[0], biases[0]), tokens_in
    )
    def with_cot(own, cot):
        mid, across = swap(own, "dp", MID), swap(own, "tensor", 1)
        across, moved = lax.optimization_barrier((across, cot))
        cot_across = swap(moved, "tensor", 1)
        mid, cot_across, own = lax.optimization_barrier((mid, cot_across, own))
        return (own, mid, across, swap(own, "tensor", 0), swap(across, "tensor", 0)), cot_across

    (token_parts, cot_across), tables = seq.settle(with_cot, own, cot, beside=make_tables)
    m0.near_wait()
    m0.far_wait()
    u0.far()
    m0.last()
    u0.near()
    sent = seq.run(lambda value: take_down(0, 1 - mid, value), down_weight, apart=True)

    def with_others(own, mid, across, core_own, core_across, sent, cot):
        received, both = swap(sent, "dp", MID), swap(mid, "tensor", 1)
        received, cot, mid = lax.optimization_barrier((received, cot, mid))
        cot_mid, core_mid = swap(cot, "dp", MID), swap(mid, "tensor", 0)
        both, core_mid = lax.optimization_barrier((both, core_mid))
        core_both = swap(both, "tensor", 0)
        parts = (own, mid, across, both, core_own, core_mid, core_across, core_both)
        return assemble(parts, 0), received, cot_mid

    normed, received, cot_mid = seq.settle(with_others, *token_parts, sent, cot)
    d0 = joined(0, 2, received)
    u0.far_wait()
    seq.tick(3)
    u0.near_wait()
    m0.last_wait()
    u0.last()
    d0.far()
    mixed_full = m0.whole()
    mixed = mix(0, normed, mixed_full)
    d0.near()
    moving = [set_out(1, 0), set_out(1, 1)]
    attended, kept, sums = attend(mixed)
    u0.last_wait()
    up_full = u0.whole()
    hidden, slope = hide(0, normed, up_full)
    m1 = paired(1, 0, moving[0])
    u1 = paired(1, 1, moving[1])
    d0.far_wait()
    seq.tick(3)
    d0.near_wait()
    d0.last()
    m1.far()
    moving = [set_out(1, 2)]
    d0.last_wait()
    down_full = d0.whole()
    m1.near()
    saved = [(normed, kept, sums, slope, attended, hidden)]
    weights = [(mixed_full, up_full, down_full)]
    streams = [stream]

    branch = Scatter(seq, out_product, (attended, hidden, mixed_full, down_full), rows)
    branch.begin()
    m1.far_wait()
    m1.near_wait()
    u1.far()
    m1.last()
    branch.second()
    d1 = paired(1, 2, moving[0])
    m1.last_wait()
    u1.near()
    branch.third()
    u1.far_wait()
    seq.tick(4)
    u1.near_wait()
    d1.far()
    u1.last()
    stream, own = branch.finish(
        norm_after, stream, out_shifts[0], gains[1], biases[1]
    )
    streams.append(stream)

    def with_cores(mine, mid, cot, across):
        parts, both = gather_start_beside(mine, mid)
        *parts, cot, across = lax.optimization_barrier((*parts, cot, across))
        return parts, both, swap(cot, "tensor", 0), swap(across, "tensor", 0)

    parts, cot_both, cot_core_own, cot_core_across = seq.settle(
        with_cores, own, cot_mid, cot, cot_across
    )
    u1.last_wait()
    d1.near()
    (grad16, normed), mixed_full = seq.settle(
        lambda *values: gather_finish_beside(values[:5], values[5:]),
        *parts,
        cot,
        cot_mid,
        cot_across,
        cot_both,
        cot_core_own,
        cot_core_across,
        beside=lambda: m1.plain(),
    )
    d1.far_wait()
    seq.tick(3)
    d1.near_wait()
    d1.last()
    mixed = mix(1, normed, mixed_full)
    attended, kept, sums = attend(mixed)
    up_full = u1.whole()
    hidden, slope = hide(1, normed, up_full)
    d1.last_wait()
    down_full = d1.whole()
    saved.append((normed, kept, sums, slope, attended, hidden))
    weights.append((mixed_full, up_full, down_full))

    heads_width = attended.shape[1]
    parts = 1 << len(side_bits())
    norm_grads, in_bgrads = [None] * layer_count, [None] * layer_count

    part = width // parts

    def down_grads(l, grad16):
        return Reduce(seq, partial(down_grad, part), saved[l][5], grad16)

    def up_grads(l, grad):
        return Reduce(seq, partial(in_grad, part), saved[l][0], grad)

    def mixed_grads(l, grad, grad16):
        values = saved[l][0], grad, grad16, saved[l][4]
        return Reduce(seq, partial(mixed_weight_grad, part), *values)

    def attend_back(l, grad16):
        kept, sums = saved[l][1:3]
        mixed_full = weights[l][0]

        def step(value):
            grad = attended_back(value, mixed_full, heads_width)
            return attention_backward(kept, sums, grad, tables, scalars, rows)

        return seq.run(step, grad16)

    def hide_back(l, grad16):
        slope, down_full = saved[l][3], weights[l][2]
        return seq.run(lambda value: hidden_back(value, down_full, slope), grad16)

    def rows_back(l, mixed_grad, pre_grad):
        return Scatter(seq, normed_back, (mixed_grad, pre_grad, *weights[l][:2]), rows)

    def bias_back(mixed_grad, pre_grad):
        return jnp.sum(mixed_grad, axis=0, dtype=f32), jnp.sum(pre_grad, axis=0, dtype=f32)

    def own_start(total, axis):
        return halves(total, mid, axis), seq.start(halves(total, 1 - mid, axis), "dp", MID)

    def own_wait(pair):
        keep, moving = pair
        received = seq.wait(moving)
        return pick(keep, received, mid).astype(f32), pick(received, keep, mid).astype(f32)

    first, second = 0, 1
    early = len(side_bits()) == 2

    def send(reduce, which):
        reduce.send(reduce.near(which))

    def arrive(reduce, which):
        reduce.wait(reduce.near(which))

    def rest(reduce):
        for which in (first, second):
            reduce.make(reduce.near(which))
            send(reduce, which)
            arrive(reduce, which)
        reduce.make_far()
        reduce.send_far()
        reduce.wait_far()
        reduce.finish()

    down2 = down_grads(1, grad16)
    down2.make(down2.near(first))
    if early:
        send(down2, first)
    mixed_grad = attend_back(1, grad16)
    if early:
        down2.make(down2.near(second))
        send(down2, second)
    pre_grad = hide_back(1, grad16)
    up2, mix2 = up_grads(1, pre_grad), mixed_grads(1, mixed_grad, grad16)
    back = rows_back(1, mixed_grad, pre_grad)
    back.begin()
    branch = Scatter(seq, out_product, (attended, hidden, *weights[1][::2]), rows)
    if early:
        arrive(down2, first)
        up2.make(up2.near(first))
        send(up2, first)
    made = back.second(
        lambda: (
            down2.plain(down2.far()) if early else (),
            up2.plain(up2.near(second)),
            mix2.plain(mix2.near(first)),
            mix2.plain(mix2.near(second)),
            bias_back(mixed_grad, pre_grad),
        )
    )
    in_bgrads[1] = made[4]
    if early:
        down2.take(down2.far(), made[0])
        up2.take(up2.near(second), made[1])
        mix2.take(mix2.near(first), made[2])
        mix2.take(mix2.near(second), made[3])
        arrive(down2, second)
        seq.tick(4)
        arrive(up2, first)
        send(up2, second)
    made = back.third(lambda: (up2.plain(up2.far()) if early else (), branch.plain()))
    branch.take(made[1])
    norm_grads[1], grad_stream, own = back.finish(
        norm_before, cot, streams[1], gains[1]
    )
    if early:
        up2.take(up2.far(), made[0])
        arrive(up2, second)
        send(mix2, first)
        down2.send_far()
    (branch.later, branch.x_high), coming = seq.settle(
        lambda own, low, core: gather_start_with(own, low, core, branch.sent_across),
        own,
        branch.low_part,
        branch.core,
    )
    if early:
        arrive(mix2, first)
        send(mix2, second)
        up2.send_far()
        grad16, made = seq.settle(gather_finish, *coming, beside=lambda: mix2.plain(mix2.far()))
        mix2.take(mix2.far(), made)
        mix2.send_far()
        down2.wait_far()
    else:
        grad16 = seq.settle(gather_finish, *coming)
        rest(down2)
        rest(up2)
        rest(mix2)

    results = {}

    def own_start(total, axis):
        keep, sent = seq.run(
            lambda value: (halves(value, mid, axis), halves(value, 1 - mid, axis)),
            total,
            apart=True,
        )
        return keep, seq.start(sent, "dp", MID)

    def own_finish(l, name, axis, pair):
        keep, moving = pair
        received = seq.wait(moving)
        before = results.get(name)
        given = () if before is None else (before,)
        results[name] = seq.run(
            lambda keep, other, *given: place_halves(
                keep, other, mid, axis, l, layer_count, *given
            ),
            keep,
            received,
            *given,
        )

    def mixed_finish(pair):
        keep, moving = pair
        received = seq.wait(moving)
        cols = 3 * heads_width

        def step(keep, other):
            pair = [pick(keep, other, mid).astype(f32), pick(other, keep, mid).astype(f32)]
            proj = [value[:, :cols].reshape(value.shape[0], 3, -1) for value in pair]
            dense = [value[:, cols:].T for value in pair]
            return jnp.concatenate(proj, axis=2), jnp.concatenate(dense, axis=0)

        return seq.run(step, keep, received, apart=True)

    down1 = down_grads(0, grad16)
    down1.make(down1.near(first))
    if early:
        send(down1, first)
        down2.make([0])
    down2_pair = own_start(down2.blocks[0], 1)
    mixed_grad = attend_back(0, grad16)
    down1.make(down1.near(second))
    if early:
        up2.wait_far()
        arrive(mix2, second)
        send(down1, second)
    pre_grad = hide_back(0, grad16)
    up1, mix1 = up_grads(0, pre_grad), mixed_grads(0, mixed_grad, grad16)
    up1.make(up1.near(first))
    if early:
        send(up1, first)
        up2.make([0])
    own_finish(1, "down", 0, down2_pair)
    up1.make(up1.near(second))
    mix1.make(mix1.near(first))
    if early:
        mix2.wait_far()
        seq.tick(5)
        arrive(down1, first)
        down1.make_far()
        arrive(down1, second)
        down1.send_far()
        send(up1, second)
    up2_pair = own_start(up2.blocks[0], 0)
    back = rows_back(0, mixed_grad, pre_grad)
    back.begin()
    if early:
        arrive(up1, first)
        up1.make_far()
        up1.send_far()
        send(mix1, first)
        mix2.make([0])
    own_finish(1, "up", 1, up2_pair)
    mix2_pair = own_start(mix2.blocks[0], 0)
    made = back.second(
        lambda: (
            mix1.plain(mix1.near(second)),
            bias_back(mixed_grad, pre_grad),
        )
    )
    mix1.take(mix1.near(second), made[0])
    in_bgrads[0] = made[1]
    if early:
        down1.wait_far()
        seq.tick(1)
        arrive(up1, second)
        seq.tick(1)
        arrive(mix1, first)
        mix1.make_far()
        mix1.send_far()
        send(mix1, second)
    made = back.third(lambda: down1.plain([0]) if early else ())
    norm_grads[0], grad_stream, own = back.finish(
        norm_before, grad_stream, streams[0], gains[0]
    )
    if early:
        down1.take([0], made)
    else:
        rest(down1)
        rest(up1)
        rest(mix1)
    down1_pair = own_start(down1.blocks[0], 1)
    small_sums = SmallSums(seq, norm_grads, in_bgrads, mid)
    small_sums.first()
    if early:
        up1.wait_far()
        up1.make([0])
    up1_pair = own_start(up1.blocks[0], 0)
    mix2_own = mixed_finish(mix2_pair)
    input_grad = branch.third(lambda: reorder(grad_stream, order, f32, True))
    activations = branch.finish(partial(last_stream, order), streams[1], out_shifts[1])
    if early:
        mix1.wait_far()
        seq.tick(4)
        arrive(mix1, second)
        mix1.make([0])
    mix1_pair = own_start(mix1.blocks[0], 0)
    own_finish(0, "down", 0, down1_pair)
    own_finish(0, "up", 1, up1_pair)
    norm_owned, bias_both = small_sums.finish()
    mix1_own = mixed_finish(mix1_pair)
    bias_both = bias_both + 0.0 * seq.scalar
    per_layer = bias_both.shape[1] // layer_count
    bias_both = bias_both.reshape(2, layer_count, per_layer)
    proj_b = jnp.transpose(
        bias_both[:, :, : 3 * heads_width].reshape(2, layer_count, 3, heads_width), (1, 2, 0, 3)
    ).reshape(layer_count, 3, 1, 2 * heads_width)
    up_b = jnp.transpose(bias_both[:, :, 3 * heads_width :], (1, 0, 2)).reshape(layer_count, 1, -1)
    return (
        activations,
        input_grad,
        norm_owned[:, 0],
        norm_owned[:, 1],
        jnp.stack([mix1_own[0], mix2_own[0]]),
        lax.dynamic_slice_in_dim(proj_b, dp * proj_each, proj_each, 3),
        jnp.stack([mix1_own[1], mix2_own[1]]),
        norm_owned[:, 2],
        results["up"],
        lax.dynamic_slice_in_dim(up_b, dp * up_each, up_each, 2),
        results["down"],
        norm_owned[:, 2],
    )


def solution(mesh):
    in_specs = (
        P(("dp", "tensor"), None),
        P("dp", None),
        P(None, ("dp", "tensor")),
        P(None, ("dp", "tensor")),
        P(None, "dp", None, "tensor"),
        P(None, None, "tensor", "dp"),
        P(None, "tensor", "dp"),
        P(None, ("dp", "tensor")),
        P(None, "dp", "tensor"),
        P(None, "tensor", "dp"),
        P(None, "tensor", "dp"),
        P(None, ("dp", "tensor")),
        P(("dp", "tensor"), None),
    )
    out_specs = (
        P(("dp", "tensor"), None),
        P(("dp", "tensor"), None),
        P(None, ("dp", "tensor")),
        P(None, ("dp", "tensor")),
        P(None, "dp", None, "tensor"),
        P(None, None, "tensor", "dp"),
        P(None, "tensor", "dp"),
        P(None, ("dp", "tensor")),
        P(None, "dp", "tensor"),
        P(None, "tensor", "dp"),
        P(None, "tensor", "dp"),
        P(None, ("dp", "tensor")),
    )
    return jax.shard_map(shards, mesh=mesh, in_specs=in_specs, out_specs=out_specs, check_vma=False)
```

time: 1420 us -> 1060 us (0.75)
  waiting for transfers between devices: 751 us -> 410 us
  Pallas kernels: 79.4 us -> 404 us
  matrix products: 271 us -> 0 us
  blocking collectives: 43.7 us -> 0 us
  local copies, waits for them, and re-layouts: 104 us -> 87.8 us
    ppermute x102, waiting for transfers between devices: 751 us -> 410 us  [swap(): return lax.ppermute(value, axis, [(i, i ^ 1 << bit) for i in range(size)])]
    pallas_call x4 -> x70, Pallas kernels: 24.2 us -> 345 us  [the longest x42 273 us: call(): pl.pallas_call(kernel, grid_spec=pltpu.PrefetchScalarGridSpec(num_scalar_...]
    dot_general x56 -> x0, matrix products: 271 us -> none  [the longest x16 99.8 us: nt(): lax.dot_general(left, right, (((1,), (1,)), ((), ())), preferred_element_...]
    all_gather x1 -> x0, blocking collectives: 43.7 us -> none  [shards(): everyone = lax.all_gather(small, ('dp', 'tensor'), axis=0)]
    unnamed x339 -> x165, local copies, waits for them, and re-layouts: 57.3 us -> 15.5 us
    convert_element_type x4 -> x15, other arithmetic: 2.6 us -> 26.4 us  [the longest x4 14.1 us: sent(): return tuple((self.chunk(low, core, k).astype(bf16) for k in (2, 3)))]
    optimization_barrier x0 -> x9, local copies, waits for them, and re-layouts: none -> 16.4 us  [gate(): *values, self.scalar = lax.optimization_barrier((*values, self.scalar))]
    concatenate x14 -> x1, local copies, waits for them, and re-layouts: 16.3 us -> 0.01 us  [halve(): received = move(jnp.concatenate([biases, sent.reshape(-1)]))]
  transfers between devices with their start and end apart: 102 -> 102, of which waited for: 39 -> 48; matrix products, arithmetic and copies ran while one was open for 18% -> 10% of each run, Pallas kernels for 2% -> 38%
where the time goes in v2:
time: 1060 us; the launch traced here: 1050 us
  waiting for transfers between devices  410 us (39%)
  Pallas kernels  404 us (38%)
  starting transfers between devices  90.8 us (9%)
  local copies, waits for them, and re-layouts  87.8 us (8%)
  other arithmetic  50.5 us (5%)
    ppermute x102, waiting for transfers between devices, swap(): return lax.ppermute(value, axis, [(i, i ^ 1 << bit) for i in range(size)])  410 us
    pallas_call x42, Pallas kernels, call(): pl.pallas_call(kernel, grid_spec=pltpu.PrefetchScalarGridSpec(num_scalar_...  273 us
    ppermute x102, starting transfers between devices, swap(): return lax.ppermute(value, axis, [(i, i ^ 1 << bit) for i in range(size)])  90.8 us
    pallas_call x2, Pallas kernels, attention_backward(): pl.pallas_call(attention_back_kernel, grid_spec=pltpu.PrefetchScalarGridS...  34.8 us
    pallas_call x10, Pallas kernels, assemble(): pl.pallas_call(partial(assemble_kernel, axis, window), in_specs=[pl.Block...  33.2 us
    pallas_call x2, Pallas kernels, attention_forward(): pl.pallas_call(attention_kernel, grid_spec=pltpu.PrefetchScalarGridSpec(n...  24.7 us
  transfers between devices with their start and end apart: 102, of which 48 were waited for; matrix products, arithmetic and copies ran while one was open for 10% of the time, Pallas kernels for 38%

profile of v2, /device:TPU:0, one launch (start us, length us, event | category | flops | bytes accessed | tf_op | source)
XLA Modules:
  0.0 1049.6 jit_solution(9385172700218811593)
XLA Ops:
  10.0 20.5 %conditional.43 = (bf16[2,1412]{1,0:T(2,128)(2,1)S(1)}) conditional(s32[]{:T(128)} %bitcast.63, () %tuple.564, (s32[]{:T(128)}, bf16[1,1412]{1,0:T(2,128)(2,1)S(1)}) %tuple.574), branch_computations={%region_4.0_spmd, %region_5.6_spmd} | conditional | flops 14121 | bytes 33946 | solution.py:63
  11.9 18.5 %collective-permute-done.23 = bf16[1,1412]{1,0:T(2,128)(2,1)S(1)} collective-permute-done((bf16[1,1412]{1,0:T(2,128)(2,1)S(1)}, bf16[1,1412]{1,0:T(2,128)(2,1)S(1)}, u32[]{:S(2)}, u32[]{:S(2)}) %collective-permute-start.23) | collective-permute-done | bytes 2856 | tf_op jit(solution)/shard_map/cond/branch_1_fun/ppermute | solution.py:27
  68.0 49.1 %conditional.48 = (bf16[192,2048]{1,0:T(8,128)(2,1)}, bf16[192,2048]{1,0:T(8,128)(2,1)}, bf16[192,2048]{1,0:T(8,128)(2,1)}, bf16[192,2048]{1,0:T(8,128)(2,1)}, b...) conditional(s32[]{:T(128)} %bitcast.63, () %tuple.596, ...), branch_computations={%region_14.15_spmd, %region_15.16_spmd} | conditional | flops 1000228 | bytes 19675248 | solution.py:63
  71.2 16.0 %collective-permute-done.49 = bf16[192,2048]{1,0:T(8,128)(2,1)} collective-permute-done((bf16[192,2048]{1,0:T(8,128)(2,1)}, bf16[192,2048]{1,0:T(8,128)(2,1)}, u32[]{:S(2)}, u32[]{:S(2)}) %collective-permute-start.49) | collective-permute-done | bytes 786464 | tf_op jit(solution)/shard_map/cond/branch_1_fun/ppermute | solution.py:27
  88.8 21.0 %collective-permute-done.48 = bf16[192,2048]{1,0:T(8,128)(2,1)} collective-permute-done((bf16[192,2048]{1,0:T(8,128)(2,1)}, bf16[192,2048]{1,0:T(8,128)(2,1)}, u32[]{:S(2)}, u32[]{:S(2)}) %collective-permute-start.48) | collective-permute-done | bytes 786464 | tf_op jit(solution)/shard_map/cond/branch_1_fun/ppermute | solution.py:27
  121.8 61.2 %conditional.50 = (bf16[1536,2048]{1,0:T(8,128)(2,1)}, bf16[1024,256]{1,0:T(8,128)(2,1)}, bf16[192,2048]{1,0:T(8,128)(2,1)}) conditional(s32[]{:T(128)} %bitcast.63, () %tuple.595, (bf16[1024,256]{1,0:T(8,128)(2,1)}, bf16[192,2048]{1,0:T(8,128)(2,1)}, bf16[192,2048]{1,0:T(8,128)(2,1)}, bf16[192,2048]{1,0:T(8,128)(2,1)}, ...), branch_computations={%region_18.19_spmd, %region_19.20_spmd} | conditional | bytes 14680288 | solution.py:63
  124.9 27.5 %collective-permute-done = bf16[1024,256]{1,0:T(8,128)(2,1)} collective-permute-done((bf16[1024,256]{1,0:T(8,128)(2,1)}, bf16[1024,256]{1,0:T(8,128)(2,1)}, u32[]{:S(2)}, u32[]{:S(2)}) %collective-permute-start) | collective-permute-done | bytes 524320 | tf_op jit(solution)/shard_map/cond/branch_1_fun/ppermute | solution.py:27
  161.5 21.6 %collective-permute-done.4 = bf16[192,2048]{1,0:T(8,128)(2,1)} collective-permute-done((bf16[192,2048]{1,0:T(8,128)(2,1)}, bf16[192,2048]{1,0:T(8,128)(2,1)}, u32[]{:S(2)}, u32[]{:S(2)}) %collective-permute-start.4) | collective-permute-done | bytes 786464 | tf_op jit(solution)/shard_map/cond/branch_1_fun/ppermute | solution.py:27
  267.2 18.7 %collective-permute-done.67.refs_3_ = bf16[1024,512]{1,0:T(8,128)(2,1)} collective-permute-done((bf16[1024,512]{1,0:T(8,128)(2,1)}, bf16[1024,512]{1,0:T(8,128)(2,1)}, u32[]{:S(2)}, u32[]{:S(2)}) %collective-permute-start.67) | collective-permute-done | bytes 1048608 | tf_op jit(solution)/shard_map/ppermute | solution.py:27
  317.3 21.7 %conditional.58 = (bf16[192,2048]{1,0:T(8,128)(2,1)S(1)}, bf16[192,2048]{1,0:T(8,128)(2,1)}) conditional(s32[]{:T(128)} %bitcast.63, () %tuple.668, (f32[768,2048]{1,0:T(8,128)}, bf16[768,2048]{1,0:T(8,128)(2,1)}) %tuple.674), branch_computations={%region_34.35_spmd, %region_35.36_spmd} | conditional | flops 2359296 | bytes 9437240 | solution.py:63
  320.9 18.2 %collective-permute-done.26 = bf16[192,2048]{1,0:T(8,128)(2,1)} collective-permute-done((bf16[192,2048]{1,0:T(8,128)(2,1)S(1)}, bf16[192,2048]{1,0:T(8,128)(2,1)}, u32[]{:S(2)}, u32[]{:S(2)}) %collective-permute-start.26) | collective-permute-done | bytes 786464 | tf_op jit(solution)/shard_map/cond/branch_1_fun/ppermute | solution.py:27
  342.3 32.7 %conditional.60 = (bf16[192,2048]{1,0:T(8,128)(2,1)}, bf16[192,2048]{1,0:T(8,128)(2,1)}) conditional(s32[]{:T(128)} %bitcast.63, () %tuple.667, (f32[768,2048]{1,0:T(8,128)}, bf16[768,2048]{1,0:T(8,128)(2,1)}, bf16[192,2048]{1,0:T(8,128)(2,1)}, bf16[192,2048]{1,0:T(8,128)(2,1)S(1)}) %tuple.683), branch_computations={%region_38.39_spmd, %region_39.40_spmd} | conditional | flops 1966080 | bytes 10223712 | solution.py:63
  345.3 29.7 %collective-permute-done.27 = bf16[192,2048]{1,0:T(8,128)(2,1)} collective-permute-done((bf16[192,2048]{1,0:T(8,128)(2,1)S(1)}, bf16[192,2048]{1,0:T(8,128)(2,1)}, u32[]{:S(2)}, u32[]{:S(2)}) %collective-permute-start.27) | collective-permute-done | bytes 786464 | tf_op jit(solution)/shard_map/cond/branch_1_fun/ppermute | solution.py:27
  382.2 41.5 %conditional.61 = (bf16[192,2048]{1,0:T(8,128)(2,1)S(1)}, bf16[192,2048]{1,0:T(8,128)(2,1)}, bf16[192,2048]{1,0:T(8,128)(2,1)}, bf16[192,2048]{1,0:T(8,128)(2,1)...) conditional(s32[]{:T(128)} %bitcast.63, () %tuple.593, ...), branch_computations={%region_40.41_spmd, %region_41.42_spmd} | conditional | bytes 23593304 | solution.py:63
  400.4 15.9 %collective-permute-done.6 = bf16[192,2048]{1,0:T(8,128)(2,1)} collective-permute-done((bf16[192,2048]{1,0:T(8,128)(2,1)S(1)}, bf16[192,2048]{1,0:T(8,128)(2,1)}, u32[]{:S(2)}, u32[]{:S(2)}) %collective-permute-start.6) | collective-permute-done | bytes 786464 | tf_op jit(solution)/shard_map/cond/branch_1_fun/ppermute | solution.py:27
  424.3 40.3 %conditional.62 = (bf16[1536,2048]{1,0:T(8,128)(2,1)}, bf16[1536,2048]{1,0:T(8,128)(2,1)}, bf16[2048,1024]{1,0:T(8,128)(2,1)}) conditional(s32[]{:T(128)} %bitcast.63, () %tuple.592, (bf16[192,2048]{1,0:T(8,128)(2,1)}, bf16[192,2048]{1,0:T(8,128)(2,1)}, bf16[192,2048]{1,0:T(8,128)(2,1)}, bf16[192,2048]{1,0:T(8,128)(2,1)}, ...), branch_computations={%region_42.43_spmd, %region_43.44_spmd} | conditional | bytes 50332152 | solution.py:63
  431.3 16.7 %collective-permute-done.15.refs_3_ = bf16[192,2048]{1,0:T(8,128)(2,1)} collective-permute-done((bf16[192,2048]{1,0:T(8,128)(2,1)}, bf16[192,2048]{1,0:T(8,128)(2,1)}, u32[]{:S(2)}, u32[]{:S(2)}) %collective-permute-start.15) | collective-permute-done | bytes 786464 | tf_op jit(solution)/shard_map/cond/branch_1_fun/ppermute | solution.py:27
  520.1 17.4 %shard_map.241 = bf16[4,2,192,768]{3,2,1,0:T(8,128)(2,1)S(1)} custom-call(s32[5]{0:T(128)S(1)} %copy-done.94, bf16[2,768,768]{2,1,0:T(8,128)(2,1)S(1)} %get-tuple-element.1756.kept_ref, f32[2,768,128]{2,1,0:T(8,128)S(1)} %get-tuple-element.1757.sums_ref, bf16[4,2,192,256]{3,2,1,0:T(8,128)(2,1)S(1)} %bitcast.166, f32[2,768,128]{2,1,0:T(8,128)S(1)} %copy-done.54, ...), custom_call_target="tpu_custom_call" | custom-call | tf_op jit(solution)/shard_map/pallas_call | solution.py:737
  581.2 23.5 %conditional.64 = (bf16[192,2048]{1,0:T(8,128)(2,1)}, bf16[192,2048]{1,0:T(8,128)(2,1)}, bf16[1024,512]{1,0:T(8,128)(2,1)}, bf16[512,1024]{1,0:T(8,128)(2,1)}, b...) conditional(s32[]{:T(128)} %bitcast.63, () %tuple.724, ...), branch_computations={%region_46.47_spmd, %region_47.50_spmd} | conditional | flops 7862528 | bytes 14949480 | solution.py:63
  607.4 31.9 %conditional.65 = (bf16[192,2048]{1,0:T(8,128)(2,1)}, bf16[192,2048]{1,0:T(8,128)(2,1)}, bf16[512,1024]{1,0:T(8,128)(2,1)S(1)}, f32[768,2048]{1,0:T(8,128)}, bf16[768,2048]{1,0:T(8,128)(2,1)}) conditional(s32[]{:T(128)} %bitcast.63, () %tuple.560, (f32[768,2048]{1,0:T(8,128)}, bf16[768,2048]{1,0:T(8,128)(2,1)}, bf16[192,2048]{1,0:T(8,128)(2,1)}, ...), branch_computations={%region_50.51_spmd, %region_51.52_spmd} | conditional | flops 1966080 | bytes 51118324 | solution.py:63
  646.3 44.0 %conditional.66 = (bf16[192,2048]{1,0:T(8,128)(2,1)}, bf16[192,2048]{1,0:T(8,128)(2,1)}, bf16[192,2048]{1,0:T(8,128)(2,1)S(1)}, bf16[192,2048]{1,0:T(8,128)(2,1)...) conditional(s32[]{:T(128)} %bitcast.63, () %tuple.738, ...), branch_computations={%region_52.53_spmd, %region_53.54_spmd} | conditional | flops 2359296 | bytes 23593216 | solution.py:63
  648.5 16.3 %collective-permute-done.33 = bf16[192,2048]{1,0:T(8,128)(2,1)} collective-permute-done((bf16[192,2048]{1,0:T(8,128)(2,1)S(1)}, bf16[192,2048]{1,0:T(8,128)(2,1)}, u32[]{:S(2)}, u32[]{:S(2)}) %collective-permute-start.33) | collective-permute-done | bytes 786464 | tf_op jit(solution)/shard_map/cond/branch_1_fun/ppermute | solution.py:27
  669.1 16.2 %collective-permute-done.34 = bf16[192,2048]{1,0:T(8,128)(2,1)} collective-permute-done((bf16[192,2048]{1,0:T(8,128)(2,1)S(1)}, bf16[192,2048]{1,0:T(8,128)(2,1)}, u32[]{:S(2)}, u32[]{:S(2)}) %collective-permute-start.34) | collective-permute-done | bytes 786464 | tf_op jit(solution)/shard_map/cond/branch_1_fun/ppermute | solution.py:27
  693.2 27.1 %conditional.67 = (bf16[1536,2048]{1,0:T(8,128)(2,1)S(1)}, bf16[512,1024]{1,0:T(8,128)(2,1)}) conditional(s32[]{:T(128)} %bitcast.63, () %tuple.752, (bf16[192,2048]{1,0:T(8,128)(2,1)}, bf16[192,2048]{1,0:T(8,128)(2,1)S(1)}, bf16[192,2048]{1,0:T(8,128)(2,1)}, bf16[192,2048]{1,0:T(8,128)(2,1)}, bf16[192,2048]{1,0:T(8,128)(2,1)}, ...), branch_computations={%region_54.55_spmd, %region_55.56_spmd} | conditional | bytes 15728832 | solution.py:63
  693.7 18.7 %collective-permute-done.19.refs_3_ = bf16[192,2048]{1,0:T(8,128)(2,1)S(1)} collective-permute-done((bf16[192,2048]{1,0:T(8,128)(2,1)}, bf16[192,2048]{1,0:T(8,128)(2,1)S(1)}, u32[]{:S(2)}, u32[]{:S(2)}) %collective-permute-start.19) | collective-permute-done | bytes 786464 | tf_op jit(solution)/shard_map/cond/branch_1_fun/ppermute | solution.py:27
  740.1 17.4 %shard_map.251 = bf16[4,2,192,768]{3,2,1,0:T(8,128)(2,1)S(1)} custom-call(s32[5]{0:T(128)S(1)} %copy-done.94, bf16[2,768,768]{2,1,0:T(8,128)(2,1)S(1)} %copy-done.4, f32[2,768,128]{2,1,0:T(8,128)S(1)} %copy-done.12, bf16[4,2,192,256]{3,2,1,0:T(8,128)(2,1)S(1)} %bitcast.165, f32[2,768,128]{2,1,0:T(8,128)} %copy-done.53, ...), custom_call_target="tpu_custom_call" | custom-call | tf_op jit(solution)/shard_map/pallas_call | solution.py:737
  843.5 19.3 %collective-permute-done.91.other_ref = bf16[256,1024]{1,0:T(8,128)(2,1)S(1)} collective-permute-done((bf16[256,1024]{1,0:T(8,128)(2,1)}, bf16[256,1024]{1,0:T(8,128)(2,1)S(1)}, u32[]{:S(2)}, u32[]{:S(2)}) %collective-permute-start.91) | collective-permute-done | bytes 524320 | tf_op jit(solution)/shard_map/ppermute | solution.py:27
  867.6 23.6 %conditional.72 = (bf16[192,2048]{1,0:T(8,128)(2,1)}, bf16[192,2048]{1,0:T(8,128)(2,1)}, bf16[512,1024]{1,0:T(8,128)(2,1)}, f32[768]{0:T(1024)S(1)}, f32[1024]{0:T(1024)S(1)}) conditional(s32[]{:T(128)} %bitcast.63, () %tuple.817, (f32[768,2048]{1,0:T(8,128)}, bf16[768,2048]{1,0:T(8,128)(2,1)}, bf16[1536,2048]{1,0:T(8,128)(2,1)}, ...), branch_computations={%region_64.65_spmd, %region_65.68_spmd} | conditional | flops 7862528 | bytes 62135460 | solution.py:63
  902.6 36.1 %conditional.73 = (bf16[192,2048]{1,0:T(8,128)(2,1)}, bf16[192,2048]{1,0:T(8,128)(2,1)}, bf16[1024,512]{1,0:T(8,128)(2,1)}) conditional(s32[]{:T(128)} %bitcast.63, () %tuple.824, (f32[768,2048]{1,0:T(8,128)}, bf16[768,2048]{1,0:T(8,128)(2,1)}, bf16[192,2048]{1,0:T(8,128)(2,1)}, bf16[192,2048]{1,0:T(8,128)(2,1)}, bf16[1536,1024]{1,0:T(8,128)(2,1)}, ...), branch_computations={%region_68.69_spmd, %region_69.70_spmd} | conditional | flops 1966080 | bytes 22806660 | solution.py:63
  912.0 26.7 %collective-permute-done.39 = bf16[192,2048]{1,0:T(8,128)(2,1)} collective-permute-done((bf16[192,2048]{1,0:T(8,128)(2,1)S(1)}, bf16[192,2048]{1,0:T(8,128)(2,1)}, u32[]{:S(2)}, u32[]{:S(2)}) %collective-permute-start.39) | collective-permute-done | bytes 786464 | tf_op jit(solution)/shard_map/cond/branch_1_fun/ppermute | solution.py:27
  977.0 21.8 %conditional.78 = (bf16[192,2048]{1,0:T(8,128)(2,1)}, bf16[192,2048]{1,0:T(8,128)(2,1)}, f32[192,2048]{1,0:T(8,128)}) conditional(s32[]{:T(128)} %bitcast.63, () %tuple.737, (f32[768,2048]{1,0:T(8,128)}, bf16[768,2048]{1,0:T(8,128)(2,1)}, bf16[192,2048]{1,0:T(8,128)(2,1)}, bf16[192,2048]{1,0:T(8,128)(2,1)}, s32[8]{0:T(128)S(1)}, ...), branch_computations={%region_78.79_spmd, %region_79.80_spmd} | conditional | flops 1966080 | bytes 10223720 | solution.py:63
  983.8 15.0 %collective-permute-done.41 = bf16[192,2048]{1,0:T(8,128)(2,1)} collective-permute-done((bf16[192,2048]{1,0:T(8,128)(2,1)}, bf16[192,2048]{1,0:T(8,128)(2,1)}, u32[]{:S(2)}, u32[]{:S(2)}) %collective-permute-start.41) | collective-permute-done | bytes 786464 | tf_op jit(solution)/shard_map/cond/branch_1_fun/ppermute | solution.py:27
  (695 shorter events, 811.8 us)
Async XLA Ops:
  47.3 69.8 %collective-permute-start.58 = (bf16[512,1024]{1,0:T(8,128)(2,1)}, bf16[512,1024]{1,0:T(8,128)(2,1)S(1)}, u32[]{:S(2)}, u32[]{:S(2)}) collective-permute-start(bf16[512,1024]{1,0:T(8,128)(2,1)} %copy.73), channel_id=1, source_target_pairs={{0,4},{4,0},{8,12},{12,8},{16,20},{20,16},{24,28},{28,24},{1,5},{5... | collective-permute-start | bytes 3145736 | tf_op jit(solution)/shard_map/ppermute | solution.py:27
  51.3 65.9 %collective-permute-start.57 = (bf16[512,1024]{1,0:T(8,128)(2,1)}, bf16[512,1024]{1,0:T(8,128)(2,1)}, u32[]{:S(2)}, u32[]{:S(2)}) collective-permute-start(bf16[512,1024]{1,0:T(8,128)(2,1)} %copy.72), channel_id=1, source_target_pairs={{0,16},{4,20},{8,24},{12,28},{16,0},{20,4},{24,8},{28,12},{1,17},{... | collective-permute-start | bytes 3145736 | tf_op jit(solution)/shard_map/ppermute | solution.py:27
  117.2 69.5 %collective-permute-start.61 = (bf16[512,1024]{1,0:T(8,128)(2,1)}, bf16[512,1024]{1,0:T(8,128)(2,1)}, u32[]{:S(2)}, u32[]{:S(2)}) collective-permute-start(bf16[512,1024]{1,0:T(8,128)(2,1)} %copy-done.62), channel_id=1, source_target_pairs={{0,16},{4,20},{8,24},{12,28},{16,0},{20,4},{24,8},{28,12},{1,17},{... | collective-permute-start | bytes 3145736 | tf_op jit(solution)/shard_map/ppermute | solution.py:27
  117.7 69.5 %collective-permute-start.60 = (bf16[512,1024]{1,0:T(8,128)(2,1)}, bf16[512,1024]{1,0:T(8,128)(2,1)}, u32[]{:S(2)}, u32[]{:S(2)}) collective-permute-start(bf16[512,1024]{1,0:T(8,128)(2,1)} %copy-done.62), channel_id=1, source_target_pairs={{0,4},{4,0},{8,12},{12,8},{16,20},{20,16},{24,28},{28,24},{1,5},{5... | collective-permute-start | bytes 3145736 | tf_op jit(solution)/shard_map/ppermute | solution.py:27
  118.2 69.0 %collective-permute-start.59 = (bf16[512,1024]{1,0:T(8,128)(2,1)}, bf16[512,1024]{1,0:T(8,128)(2,1)}, u32[]{:S(2)}, u32[]{:S(2)}) collective-permute-start(bf16[512,1024]{1,0:T(8,128)(2,1)} %collective-permute-done.57.refs_1_), channel_id=1, source_target_pairs={{0,4},{4,0},{8,12},{12,8},{16,20},{20,16},{24,28},{28,24},{1,5},{5... | collective-permute-start | bytes 3145736 | tf_op jit(solution)/shard_map/ppermute | solution.py:27
  187.2 43.8 %collective-permute-start.62 = (bf16[512,1024]{1,0:T(8,128)(2,1)}, bf16[512,1024]{1,0:T(8,128)(2,1)}, u32[]{:S(2)}, u32[]{:S(2)}) collective-permute-start(bf16[512,1024]{1,0:T(8,128)(2,1)} %collective-permute-done.61.refs_1_), channel_id=1, source_target_pairs={{0,4},{4,0},{8,12},{12,8},{16,20},{20,16},{24,28},{28,24},{1,5},{5... | collective-permute-start | bytes 3145736 | tf_op jit(solution)/shard_map/ppermute | solution.py:27
  187.8 72.6 %collective-permute-start.63 = (bf16[1024,512]{1,0:T(8,128)(2,1)}, bf16[1024,512]{1,0:T(8,128)(2,1)}, u32[]{:S(2)}, u32[]{:S(2)}) collective-permute-start(bf16[1024,512]{1,0:T(8,128)(2,1)} %get-tuple-element.2663.refs_0_), channel_id=1, source_target_pairs={{0,16},{4,20},{8,24},{12,28},{16,0},{20,4},{24,8},{28,12},{1,17},{... | collective-permute-start | bytes 3145736 | tf_op jit(solution)/shard_map/ppermute | solution.py:27
  203.1 58.4 %collective-permute-start.66 = (bf16[1024,512]{1,0:T(8,128)(2,1)}, bf16[1024,512]{1,0:T(8,128)(2,1)S(1)}, u32[]{:S(2)}, u32[]{:S(2)}) collective-permute-start(bf16[1024,512]{1,0:T(8,128)(2,1)} %get-tuple-element.2663.refs_0_), channel_id=1, source_target_pairs={{0,4},{4,0},{8,12},{12,8},{16,20},{20,16},{24,28},{28,24},{1,5},{5... | collective-permute-start | bytes 3145736 | tf_op jit(solution)/shard_map/ppermute | solution.py:27
  214.1 42.7 %collective-permute-start.64 = (bf16[256,1024]{1,0:T(8,128)(2,1)}, bf16[256,1024]{1,0:T(8,128)(2,1)}, u32[]{:S(2)}, u32[]{:S(2)}) collective-permute-start(bf16[256,1024]{1,0:T(8,128)(2,1)} %get-tuple-element.2665), channel_id=1, source_target_pairs={{0,8},{4,12},{8,0},{12,4},{16,24},{20,28},{24,16},{28,20},{1,9},{5... | collective-permute-start | bytes 1572872 | tf_op jit(solution)/shard_map/ppermute | solution.py:27
  266.6 46.7 %collective-permute-start.68 = (bf16[512,1024]{1,0:T(8,128)(2,1)}, bf16[512,1024]{1,0:T(8,128)(2,1)}, u32[]{:S(2)}, u32[]{:S(2)}) collective-permute-start(bf16[512,1024]{1,0:T(8,128)(2,1)} %copy.77), channel_id=1, source_target_pairs={{0,16},{4,20},{8,24},{12,28},{16,0},{20,4},{24,8},{28,12},{1,17},{... | collective-permute-start | bytes 3145736 | tf_op jit(solution)/shard_map/ppermute | solution.py:27
  315.0 60.0 %collective-permute-start.72 = (bf16[512,1024]{1,0:T(8,128)(2,1)}, bf16[512,1024]{1,0:T(8,128)(2,1)}, u32[]{:S(2)}, u32[]{:S(2)}) collective-permute-start(bf16[512,1024]{1,0:T(8,128)(2,1)} %get-tuple-element.2667.refs_0_), channel_id=1, source_target_pairs={{0,16},{4,20},{8,24},{12,28},{16,0},{20,4},{24,8},{28,12},{1,17},{... | collective-permute-start | bytes 3145736 | tf_op jit(solution)/shard_map/ppermute | solution.py:27
  377.2 46.6 %collective-permute-start.74 = (bf16[512,1024]{1,0:T(8,128)(2,1)}, bf16[512,1024]{1,0:T(8,128)(2,1)}, u32[]{:S(2)}, u32[]{:S(2)}) collective-permute-start(bf16[512,1024]{1,0:T(8,128)(2,1)} %collective-permute-done.72.refs_1_), channel_id=1, source_target_pairs={{0,4},{4,0},{8,12},{12,8},{16,20},{20,16},{24,28},{28,24},{1,5},{5... | collective-permute-start | bytes 3145736 | tf_op jit(solution)/shard_map/ppermute | solution.py:27
  378.6 86.0 %collective-permute-start.75 = (bf16[1024,512]{1,0:T(8,128)(2,1)}, bf16[1024,512]{1,0:T(8,128)(2,1)}, u32[]{:S(2)}, u32[]{:S(2)}) collective-permute-start(bf16[1024,512]{1,0:T(8,128)(2,1)} %copy-done.64), channel_id=1, source_target_pairs={{0,16},{4,20},{8,24},{12,28},{16,0},{20,4},{24,8},{28,12},{1,17},{... | collective-permute-start | bytes 3145736 | tf_op jit(solution)/shard_map/ppermute | solution.py:27
  423.8 42.0 %collective-permute-start.76 = (bf16[1024,512]{1,0:T(8,128)(2,1)}, bf16[1024,512]{1,0:T(8,128)(2,1)}, u32[]{:S(2)}, u32[]{:S(2)}) collective-permute-start(bf16[1024,512]{1,0:T(8,128)(2,1)} %copy-done.64), channel_id=1, source_target_pairs={{0,4},{4,0},{8,12},{12,8},{16,20},{20,16},{24,28},{28,24},{1,5},{5... | collective-permute-start | bytes 3145736 | tf_op jit(solution)/shard_map/ppermute | solution.py:27
  465.8 40.2 %collective-permute-start.77 = (bf16[1024,512]{1,0:T(8,128)(2,1)}, bf16[1024,512]{1,0:T(8,128)(2,1)S(1)}, u32[]{:S(2)}, u32[]{:S(2)}) collective-permute-start(bf16[1024,512]{1,0:T(8,128)(2,1)} %collective-permute-done.75.refs_1_), channel_id=1, source_target_pairs={{0,4},{4,0},{8,12},{12,8},{16,20},{20,16},{24,28},{28,24},{1,5},{5... | collective-permute-start | bytes 3145736 | tf_op jit(solution)/shard_map/ppermute | solution.py:27
  514.6 60.9 %collective-permute-start.78 = (bf16[1024,512]{1,0:T(8,128)(2,1)}, bf16[1024,512]{1,0:T(8,128)(2,1)}, u32[]{:S(2)}, u32[]{:S(2)}) collective-permute-start(bf16[1024,512]{1,0:T(8,128)(2,1)} %shard_map.239), channel_id=1, source_target_pairs={{0,4},{4,0},{8,12},{12,8},{16,20},{20,16},{24,28},{28,24},{1,5},{5... | collective-permute-start | bytes 3145736 | tf_op jit(solution)/shard_map/ppermute | solution.py:27
  542.3 62.4 %collective-permute-start.80 = (bf16[1024,512]{1,0:T(8,128)(2,1)}, bf16[1024,512]{1,0:T(8,128)(2,1)}, u32[]{:S(2)}, u32[]{:S(2)}) collective-permute-start(bf16[1024,512]{1,0:T(8,128)(2,1)} %shard_map.242), channel_id=1, source_target_pairs={{0,4},{4,0},{8,12},{12,8},{16,20},{20,16},{24,28},{28,24},{1,5},{5... | collective-permute-start | bytes 3145736 | tf_op jit(solution)/shard_map/ppermute | solution.py:27
  644.1 46.3 %collective-permute-start.82 = (bf16[512,1024]{1,0:T(8,128)(2,1)}, bf16[512,1024]{1,0:T(8,128)(2,1)}, u32[]{:S(2)}, u32[]{:S(2)}) collective-permute-start(bf16[512,1024]{1,0:T(8,128)(2,1)} %get-tuple-element.1896), channel_id=1, source_target_pairs={{0,4},{4,0},{8,12},{12,8},{16,20},{20,16},{24,28},{28,24},{1,5},{5... | collective-permute-start | bytes 3145736 | tf_op jit(solution)/shard_map/ppermute | solution.py:27
  645.3 76.2 %collective-permute-start.85 = (bf16[1024,512]{1,0:T(8,128)(2,1)}, bf16[1024,512]{1,0:T(8,128)(2,1)}, u32[]{:S(2)}, u32[]{:S(2)}) collective-permute-start(bf16[1024,512]{1,0:T(8,128)(2,1)} %get-tuple-element.1922), channel_id=1, source_target_pairs={{0,16},{4,20},{8,24},{12,28},{16,0},{20,4},{24,8},{28,12},{1,17},{... | collective-permute-start | bytes 3145736 | tf_op jit(solution)/shard_map/ppermute | solution.py:27
  690.4 73.3 %collective-permute-start.84 = (bf16[512,1024]{1,0:T(8,128)(2,1)}, bf16[512,1024]{1,0:T(8,128)(2,1)}, u32[]{:S(2)}, u32[]{:S(2)}) collective-permute-start(bf16[512,1024]{1,0:T(8,128)(2,1)} %copy-done.79), channel_id=1, source_target_pairs={{0,16},{4,20},{8,24},{12,28},{16,0},{20,4},{24,8},{28,12},{1,17},{... | collective-permute-start | bytes 3145736 | tf_op jit(solution)/shard_map/ppermute | solution.py:27
  692.3 71.3 %collective-permute-start.83 = (bf16[512,1024]{1,0:T(8,128)(2,1)}, bf16[512,1024]{1,0:T(8,128)(2,1)}, u32[]{:S(2)}, u32[]{:S(2)}) collective-permute-start(bf16[512,1024]{1,0:T(8,128)(2,1)} %get-tuple-element.1899), channel_id=1, source_target_pairs={{0,4},{4,0},{8,12},{12,8},{16,20},{20,16},{24,28},{28,24},{1,5},{5... | collective-permute-start | bytes 3145736 | tf_op jit(solution)/shard_map/ppermute | solution.py:27
  720.3 79.5 %collective-permute-start.86 = (bf16[512,1024]{1,0:T(8,128)(2,1)}, bf16[512,1024]{1,0:T(8,128)(2,1)}, u32[]{:S(2)}, u32[]{:S(2)}) collective-permute-start(bf16[512,1024]{1,0:T(8,128)(2,1)} %get-tuple-element.1953), channel_id=1, source_target_pairs={{0,16},{4,20},{8,24},{12,28},{16,0},{20,4},{24,8},{28,12},{1,17},{... | collective-permute-start | bytes 3145736 | tf_op jit(solution)/shard_map/ppermute | solution.py:27
  734.2 54.6 %collective-permute-start.87 = (bf16[1024,256]{1,0:T(8,128)(2,1)}, bf16[1024,256]{1,0:T(8,128)(2,1)S(1)}, u32[]{:S(2)}, u32[]{:S(2)}) collective-permute-start(bf16[1024,256]{1,0:T(8,128)(2,1)} %get-tuple-element.1963), channel_id=1, source_target_pairs={{0,8},{4,12},{8,0},{12,4},{16,24},{20,28},{24,16},{28,20},{1,9},{5... | collective-permute-start | bytes 1572872 | tf_op jit(solution)/shard_map/ppermute | solution.py:27
  757.5 43.5 %collective-permute-start.89 = (bf16[1024,512]{1,0:T(8,128)(2,1)}, bf16[1024,512]{1,0:T(8,128)(2,1)}, u32[]{:S(2)}, u32[]{:S(2)}) collective-permute-start(bf16[1024,512]{1,0:T(8,128)(2,1)} %shard_map.248), channel_id=1, source_target_pairs={{0,4},{4,0},{8,12},{12,8},{16,20},{20,16},{24,28},{28,24},{1,5},{5... | collective-permute-start | bytes 3145736 | tf_op jit(solution)/shard_map/ppermute | solution.py:27
  763.6 42.7 %collective-permute-start.90 = (bf16[1024,512]{1,0:T(8,128)(2,1)}, bf16[1024,512]{1,0:T(8,128)(2,1)}, u32[]{:S(2)}, u32[]{:S(2)}) collective-permute-start(bf16[1024,512]{1,0:T(8,128)(2,1)} %shard_map.252), channel_id=1, source_target_pairs={{0,4},{4,0},{8,12},{12,8},{16,20},{20,16},{24,28},{28,24},{1,5},{5... | collective-permute-start | bytes 3145736 | tf_op jit(solution)/shard_map/ppermute | solution.py:27
  782.0 48.5 %collective-permute-start.88 = (bf16[512,1024]{1,0:T(8,128)(2,1)}, bf16[512,1024]{1,0:T(8,128)(2,1)}, u32[]{:S(2)}, u32[]{:S(2)}) collective-permute-start(bf16[512,1024]{1,0:T(8,128)(2,1)} %shard_map.254), channel_id=1, source_target_pairs={{0,4},{4,0},{8,12},{12,8},{16,20},{20,16},{24,28},{28,24},{1,5},{5... | collective-permute-start | bytes 3145736 | tf_op jit(solution)/shard_map/ppermute | solution.py:27
  806.4 84.8 %collective-permute-start.94 = (bf16[1024,512]{1,0:T(8,128)(2,1)}, bf16[1024,512]{1,0:T(8,128)(2,1)}, u32[]{:S(2)}, u32[]{:S(2)}) collective-permute-start(bf16[1024,512]{1,0:T(8,128)(2,1)} %shard_map.260), channel_id=1, source_target_pairs={{0,16},{4,20},{8,24},{12,28},{16,0},{20,4},{24,8},{28,12},{1,17},{... | collective-permute-start | bytes 3145736 | tf_op jit(solution)/shard_map/ppermute | solution.py:27
  808.1 84.2 %collective-permute-start.93 = (bf16[512,1024]{1,0:T(8,128)(2,1)}, bf16[512,1024]{1,0:T(8,128)(2,1)}, u32[]{:S(2)}, u32[]{:S(2)}) collective-permute-start(bf16[512,1024]{1,0:T(8,128)(2,1)} %shard_map.257), channel_id=1, source_target_pairs={{0,4},{4,0},{8,12},{12,8},{16,20},{20,16},{24,28},{28,24},{1,5},{5... | collective-permute-start | bytes 3145736 | tf_op jit(solution)/shard_map/ppermute | solution.py:27
  835.9 57.7 %collective-permute-start.96 = (bf16[512,1024]{1,0:T(8,128)(2,1)}, bf16[512,1024]{1,0:T(8,128)(2,1)}, u32[]{:S(2)}, u32[]{:S(2)}) collective-permute-start(bf16[512,1024]{1,0:T(8,128)(2,1)} %shard_map.258), channel_id=1, source_target_pairs={{0,4},{4,0},{8,12},{12,8},{16,20},{20,16},{24,28},{28,24},{1,5},{5... | collective-permute-start | bytes 3145736 | tf_op jit(solution)/shard_map/ppermute | solution.py:27
  841.7 122.0 %collective-permute-start.95 = (bf16[512,1024]{1,0:T(8,128)(2,1)}, bf16[512,1024]{1,0:T(8,128)(2,1)}, u32[]{:S(2)}, u32[]{:S(2)}) collective-permute-start(bf16[512,1024]{1,0:T(8,128)(2,1)} %shard_map.262), channel_id=1, source_target_pairs={{0,16},{4,20},{8,24},{12,28},{16,0},{20,4},{24,8},{28,12},{1,17},{... | collective-permute-start | bytes 3145736 | tf_op jit(solution)/shard_map/ppermute | solution.py:27
  899.4 106.2 %collective-permute-start.99 = (bf16[512,1024]{1,0:T(8,128)(2,1)}, bf16[512,1024]{1,0:T(8,128)(2,1)}, u32[]{:S(2)}, u32[]{:S(2)}) collective-permute-start(bf16[512,1024]{1,0:T(8,128)(2,1)} %shard_map.267), channel_id=1, source_target_pairs={{0,16},{4,20},{8,24},{12,28},{16,0},{20,4},{24,8},{28,12},{1,17},{... | collective-permute-start | bytes 3145736 | tf_op jit(solution)/shard_map/ppermute | solution.py:27
  899.4 107.4 %collective-permute-start.100 = (bf16[512,1024]{1,0:T(8,128)(2,1)}, bf16[512,1024]{1,0:T(8,128)(2,1)}, u32[]{:S(2)}, u32[]{:S(2)}) collective-permute-start(bf16[512,1024]{1,0:T(8,128)(2,1)} %get-tuple-element.2196), channel_id=1, source_target_pairs={{0,4},{4,0},{8,12},{12,8},{16,20},{20,16},{24,28},{28,24},{1,5},{5... | collective-permute-start | bytes 3145736 | tf_op jit(solution)/shard_map/ppermute | solution.py:27
  (173 other events, 2249.2 us)

commit v3 on v2

--- a/solution.py
+++ b/solution.py
@@ -271,7 +271,7 @@
     return (own, near, across, swap(own, "tensor", 0), swap(across, "tensor", 0)), both
 
 
-def gather_finish_beside(parts, other):
+def gather_finish_beside(parts, other, beside):
     own, mid, across, core_own, core_across = parts
     other_own, other_mid, other_across, other_both, other_core_own, other_core_across = other
     both, core_mid = swap(mid, "tensor", 1), swap(mid, "tensor", 0)
@@ -279,25 +279,27 @@
     other_core_mid = swap(other_mid, "tensor", 0)
     other_core_mid, other_both = lax.optimization_barrier((other_core_mid, other_both))
     other_core_both = swap(other_both, "tensor", 0)
-    both, other_core_both = lax.optimization_barrier((both, other_core_both))
+    others = (other_own, other_mid, other_across, other_both)
+    others += (other_core_own, other_core_mid, other_core_across, other_core_both)
+    whole, made = assemble(others, 0), beside()
+    both, whole, made = lax.optimization_barrier((both, whole, made))
     core_both = swap(both, "tensor", 0)
     mine = (own, mid, across, both, core_own, core_mid, core_across, core_both)
-    others = (other_own, other_mid, other_across, other_both)
-    others += (other_core_own, other_core_mid, other_core_across, other_core_both)
-    return assemble(others, 0), assemble(mine, 0)
+    return whole, assemble(mine, 0), made
 
 
 class Scatter:
     def __init__(self, seq, product, operands, rows):
         self.seq, self.product, self.operands, self.rows = seq, product, operands, rows
 
-    def begin(self):
+    def begin(self, beside=tuple):
         high = self.seq.run(lambda *values: self.product(*values, 1, bf16), *self.operands)
-        self.core, self.low_part = self.seq.settle(
+        self.core, (self.low_part, made) = self.seq.settle(
             lambda high: swap(high, "tensor", 0),
             high,
-            beside=lambda: self.product(*self.operands, 0, f32),
+            beside=lambda: (self.product(*self.operands, 0, f32), beside()),
         )
+        return made
 
     def plain(self):
         high = self.product(*self.operands, 1, bf16)
@@ -1059,10 +1061,10 @@
 
 
 class Small:
-    def __init__(self, seq, mine, tensor, mid):
+    def __init__(self, seq, mine, tensor, mid, beside):
         self.seq, self.tensor = seq, tensor
-        self.mine = seq.settle(
-            lambda mine: pair_up(mine, swap(mine, "dp", MID), mid, 0), mine[None]
+        self.mine, self.beside = seq.settle(
+            lambda mine: pair_up(mine, swap(mine, "dp", MID), mid, 0), mine[None], beside=beside
         )
 
     def second(self):
@@ -1185,6 +1187,7 @@
         return Spread(seq, block, axis)
 
     moving = [set_out(0, 0), set_out(0, 1)]
+    cot = seq.run(lambda value: reorder(value, order, bf16), cotangent)
     whole_lens = lengths.reshape(-1).astype(f32)
     coarse = jnp.floor(whole_lens / 8.0)
     small = Small(
@@ -1198,13 +1201,14 @@
         ),
         tensor,
         mid,
-    )
+        lambda: swap(cot, "tensor", 1),
+    )
+    cot_across = small.beside
     small.second()
     m0 = paired(0, 0, moving[0])
     u0 = paired(0, 1, moving[1])
     m0.near()
     m0.far()
-    cot = seq.run(lambda value: reorder(value, order, bf16), cotangent)
     each, proj_each, up_each = norm_gain.shape[1], proj_bias.shape[3], up_bias.shape[2]
 
     def unpack(everyone):
@@ -1253,14 +1257,8 @@
     stream, own = seq.run(
         lambda value: norm_first(value, order, gains[0], biases[0]), tokens_in
     )
-    def with_cot(own, cot):
-        mid, across = swap(own, "dp", MID), swap(own, "tensor", 1)
-        across, moved = lax.optimization_barrier((across, cot))
-        cot_across = swap(moved, "tensor", 1)
-        mid, cot_across, own = lax.optimization_barrier((mid, cot_across, own))
-        return (own, mid, across, swap(own, "tensor", 0), swap(across, "tensor", 0)), cot_across
-
-    (token_parts, cot_across), tables = seq.settle(with_cot, own, cot, beside=make_tables)
+    tokens = Gather(seq, own, make_tables)
+    token_parts, tables = tokens.parts, tokens.beside
     m0.near_wait()
     m0.far_wait()
     u0.far()
@@ -1268,16 +1266,14 @@
     u0.near()
     sent = seq.run(lambda value: take_down(0, 1 - mid, value), down_weight, apart=True)
 
-    def with_others(own, mid, across, core_own, core_across, sent, cot):
+    def with_half(sent, own, mid, across, core_own, core_across):
         received, both = swap(sent, "dp", MID), swap(mid, "tensor", 1)
-        received, cot, mid = lax.optimization_barrier((received, cot, mid))
-        cot_mid, core_mid = swap(cot, "dp", MID), swap(mid, "tensor", 0)
-        both, core_mid = lax.optimization_barrier((both, core_mid))
-        core_both = swap(both, "tensor", 0)
+        received, both, mid = lax.optimization_barrier((received, both, mid))
+        core_mid, core_both = swap(mid, "tensor", 0), swap(both, "tensor", 0)
         parts = (own, mid, across, both, core_own, core_mid, core_across, core_both)
-        return assemble(parts, 0), received, cot_mid
-
-    normed, received, cot_mid = seq.settle(with_others, *token_parts, sent, cot)
+        return received, assemble(parts, 0)
+
+    received, normed = seq.settle(with_half, sent, *token_parts)
     d0 = joined(0, 2, received)
     u0.far_wait()
     seq.tick(3)
@@ -1299,31 +1295,27 @@
     seq.tick(3)
     d0.near_wait()
     d0.last()
+    cot_mid = seq.swap(cot, "dp", MID)
     m1.far()
-    moving = [set_out(1, 2)]
     d0.last_wait()
     down_full = d0.whole()
     m1.near()
+    moving = [set_out(1, 2)]
     saved = [(normed, kept, sums, slope, attended, hidden)]
     weights = [(mixed_full, up_full, down_full)]
     streams = [stream]
 
     branch = Scatter(seq, out_product, (attended, hidden, mixed_full, down_full), rows)
     branch.begin()
-    m1.far_wait()
-    m1.near_wait()
-    u1.far()
-    m1.last()
     branch.second()
     d1 = paired(1, 2, moving[0])
-    m1.last_wait()
+    m1.far_wait()
+    seq.tick(2)
+    m1.near_wait()
+    m1.last()
+    branch.third()
     u1.near()
-    branch.third()
-    u1.far_wait()
-    seq.tick(4)
-    u1.near_wait()
-    d1.far()
-    u1.last()
+    u1.far()
     stream, own = branch.finish(
         norm_after, stream, out_shifts[0], gains[1], biases[1]
     )
@@ -1337,10 +1329,14 @@
     parts, cot_both, cot_core_own, cot_core_across = seq.settle(
         with_cores, own, cot_mid, cot, cot_across
     )
-    u1.last_wait()
+    m1.last_wait()
+    u1.near_wait()
+    u1.far_wait()
     d1.near()
-    (grad16, normed), mixed_full = seq.settle(
-        lambda *values: gather_finish_beside(values[:5], values[5:]),
+    d1.far()
+    u1.last()
+    grad16, normed, mixed_full = seq.settle(
+        lambda *values: gather_finish_beside(values[:5], values[5:], m1.plain),
         *parts,
         cot,
         cot_mid,
@@ -1348,20 +1344,17 @@
         cot_both,
         cot_core_own,
         cot_core_across,
-        beside=lambda: m1.plain(),
-    )
-    d1.far_wait()
-    seq.tick(3)
+    )
+    mixed = mix(1, normed, mixed_full)
     d1.near_wait()
-    d1.last()
-    mixed = mix(1, normed, mixed_full)
+    u1.last_wait()
     attended, kept, sums = attend(mixed)
     up_full = u1.whole()
     hidden, slope = hide(1, normed, up_full)
-    d1.last_wait()
-    down_full = d1.whole()
+    d1.far_wait()
+    d1.last()
     saved.append((normed, kept, sums, slope, attended, hidden))
-    weights.append((mixed_full, up_full, down_full))
+    weights.append((mixed_full, up_full, None))
 
     heads_width = attended.shape[1]
     parts = 1 << len(side_bits())
@@ -1431,6 +1424,8 @@
     if early:
         send(down2, first)
     mixed_grad = attend_back(1, grad16)
+    d1.last_wait()
+    weights[1] = (mixed_full, up_full, d1.whole())
     if early:
         down2.make(down2.near(second))
         send(down2, second)
@@ -1558,21 +1553,25 @@
         arrive(down1, second)
         down1.send_far()
         send(up1, second)
-    up2_pair = own_start(up2.blocks[0], 0)
     back = rows_back(0, mixed_grad, pre_grad)
     back.begin()
     if early:
         arrive(up1, first)
         up1.make_far()
         up1.send_far()
+    branch.third()
+    if early:
         send(mix1, first)
         mix2.make([0])
-    own_finish(1, "up", 1, up2_pair)
-    mix2_pair = own_start(mix2.blocks[0], 0)
+    activations = branch.finish(partial(last_stream, order), streams[1], out_shifts[1])
+    up2_halves = seq.run(
+        lambda value: (halves(value, mid, 0), halves(value, 1 - mid, 0)), up2.blocks[0], apart=True
+    )
     made = back.second(
         lambda: (
             mix1.plain(mix1.near(second)),
             bias_back(mixed_grad, pre_grad),
+            swap(up2_halves[1], "dp", MID),
         )
     )
     mix1.take(mix1.near(second), made[0])
@@ -1586,6 +1585,11 @@
         mix1.make_far()
         mix1.send_far()
         send(mix1, second)
+    results["up"] = seq.run(
+        lambda keep, other: place_halves(keep, other, mid, 1, 1, layer_count),
+        up2_halves[0],
+        made[2],
+    )
     made = back.third(lambda: down1.plain([0]) if early else ())
     norm_grads[0], grad_stream, own = back.finish(
         norm_before, grad_stream, streams[0], gains[0]
@@ -1596,22 +1600,23 @@
         rest(down1)
         rest(up1)
         rest(mix1)
-    down1_pair = own_start(down1.blocks[0], 1)
     small_sums = SmallSums(seq, norm_grads, in_bgrads, mid)
     small_sums.first()
     if early:
         up1.wait_far()
+    mix2_pair = own_start(mix2.blocks[0], 0)
+    down1_pair = own_start(down1.blocks[0], 1)
+    if early:
         up1.make([0])
     up1_pair = own_start(up1.blocks[0], 0)
     mix2_own = mixed_finish(mix2_pair)
-    input_grad = branch.third(lambda: reorder(grad_stream, order, f32, True))
-    activations = branch.finish(partial(last_stream, order), streams[1], out_shifts[1])
     if early:
         mix1.wait_far()
         seq.tick(4)
         arrive(mix1, second)
         mix1.make([0])
     mix1_pair = own_start(mix1.blocks[0], 0)
+    input_grad = seq.run(lambda value: reorder(value, order, f32, True), grad_stream)
     own_finish(0, "down", 0, down1_pair)
     own_finish(0, "up", 1, up1_pair)
     norm_owned, bias_both = small_sums.finish()

time: 1060 us -> 1040 us (0.981)
  waiting for transfers between devices: 410 us -> 373 us
  starting transfers between devices: 90.8 us -> 106 us
    ppermute x102, waiting for transfers between devices: 410 us -> 373 us  [swap(): return lax.ppermute(value, axis, [(i, i ^ 1 << bit) for i in range(size)])]
    ppermute x102, starting transfers between devices: 90.8 us -> 106 us  [swap(): return lax.ppermute(value, axis, [(i, i ^ 1 << bit) for i in range(size)])]
  transfers between devices with their start and end apart: 102 -> 102, of which waited for: 48 -> 47; matrix products, arithmetic and copies ran while one was open for 10% -> 9% of each run, Pallas kernels for 38% -> 39%
where the time goes in v3:
time: 1040 us; the launch traced here: 1030 us
  Pallas kernels  405 us (39%)
  waiting for transfers between devices  373 us (36%)
  starting transfers between devices  106 us (10%)
  local copies, waits for them, and re-layouts  87.7 us (8%)
  other arithmetic  49.7 us (5%)
    ppermute x102, waiting for transfers between devices, swap(): return lax.ppermute(value, axis, [(i, i ^ 1 << bit) for i in range(size)])  373 us
    pallas_call x42, Pallas kernels, call(): pl.pallas_call(kernel, grid_spec=pltpu.PrefetchScalarGridSpec(num_scalar_...  277 us
    ppermute x102, starting transfers between devices, swap(): return lax.ppermute(value, axis, [(i, i ^ 1 << bit) for i in range(size)])  106 us
    pallas_call x2, Pallas kernels, attention_backward(): pl.pallas_call(attention_back_kernel, grid_spec=pltpu.PrefetchScalarGridS...  36.1 us
    pallas_call x10, Pallas kernels, assemble(): pl.pallas_call(partial(assemble_kernel, axis, window), in_specs=[pl.Block...  30.7 us
    pallas_call x2, Pallas kernels, attention_forward(): pl.pallas_call(attention_kernel, grid_spec=pltpu.PrefetchScalarGridSpec(n...  25.4 us
    unnamed x181, local copies, waits for them, and re-layouts  21 us
  transfers between devices with their start and end apart: 102, of which 47 were waited for; matrix products, arithmetic and copies ran while one was open for 9% of the time, Pallas kernels for 39%

profile of v3, /device:TPU:0, one launch (start us, length us, event | category | flops | bytes accessed | tf_op | source)
XLA Modules:
  0.0 1027.8 jit_solution(5212832239779017640)
XLA Ops:
  13.4 19.4 %conditional.44 = (bf16[2,1412]{1,0:T(2,128)(2,1)S(1)}, bf16[192,2048]{1,0:T(8,128)(2,1)}) conditional(s32[]{:T(128)} %bitcast.63, () %tuple.573, (s32[]{:T(128)}, bf16[1,1412]{1,0:T(2,128)(2,1)S(1)}, bf16[192,2048]{1,0:T(8,128)(2,1)}) %tuple.585), branch_computations={%region_4.0_spmd, %region_5.6_spmd} | conditional | flops 14121 | bytes 3179722 | solution.py:63
  68.3 48.4 %conditional.49 = (bf16[192,2048]{1,0:T(8,128)(2,1)}, bf16[192,2048]{1,0:T(8,128)(2,1)}, bf16[192,2048]{1,0:T(8,128)(2,1)}, bf16[192,2048]{1,0:T(8,128)(2,1)}, b...) conditional(s32[]{:T(128)} %bitcast.63, () %tuple.607, ...), branch_computations={%region_14.15_spmd, %region_15.16_spmd} | conditional | flops 1000228 | bytes 16529472 | solution.py:63
  71.5 37.3 %collective-permute-done.50 = bf16[192,2048]{1,0:T(8,128)(2,1)} collective-permute-done((bf16[192,2048]{1,0:T(8,128)(2,1)}, bf16[192,2048]{1,0:T(8,128)(2,1)}, u32[]{:S(2)}, u32[]{:S(2)}) %collective-permute-start.50) | collective-permute-done | bytes 786464 | tf_op jit(solution)/shard_map/cond/branch_1_fun/ppermute | solution.py:27
  121.5 37.5 %conditional.51 = (bf16[1024,256]{1,0:T(8,128)(2,1)}, bf16[1536,2048]{1,0:T(8,128)(2,1)}) conditional(s32[]{:T(128)} %bitcast.63, () %tuple.605, (bf16[1024,256]{1,0:T(8,128)(2,1)}, bf16[192,2048]{1,0:T(8,128)(2,1)}, bf16[192,2048]{1,0:T(8,128)(2,1)}, bf16[192,2048]{1,0:T(8,128)(2,1)}, bf16[192,2048]{1,0:T(8,128)(2,1)}, ...), branch_computations={%region_18.19_spmd, %region_19.20_spmd} | conditional | bytes 11534512 | solution.py:63
  125.4 26.0 %collective-permute-done = bf16[1024,256]{1,0:T(8,128)(2,1)} collective-permute-done((bf16[1024,256]{1,0:T(8,128)(2,1)}, bf16[1024,256]{1,0:T(8,128)(2,1)}, u32[]{:S(2)}, u32[]{:S(2)}) %collective-permute-start) | collective-permute-done | bytes 524320 | tf_op jit(solution)/shard_map/cond/branch_1_fun/ppermute | solution.py:27
  213.5 14.4 %shard_map.227 = (bf16[1536,1024]{1,0:T(8,128)(2,1)}, f32[1536,1024]{1,0:T(8,128)}) custom-call(bf16[1536,2048]{1,0:T(8,128)(2,1)} %get-tuple-element.2190.left_ref.normed_ref, bf16[2048,1024]{1,0:T(8,128)(2,1)S(1)} %shard_map.226.right_ref.up_ref, f32[1,1024]{1,0:T(1,128)S(1)} %get-tuple-element.1582.shift_ref), custom_call_target="tpu_custom_call" | custom-call | tf_op jit(solution)/shard_map/pallas_call | solution.py:762
  240.9 17.7 %conditional.57 = (bf16[192,2048]{1,0:T(8,128)(2,1)}) conditional(s32[]{:T(128)} %bitcast.63, () %tuple.664, bf16[192,2048]{1,0:T(8,128)(2,1)} %shard_map.220.grad_ref), branch_computations={%region_30.31_spmd, %region_31.32_spmd} | conditional | bytes 3145776 | solution.py:63
  241.2 17.5 %collective-permute-done.4 = bf16[192,2048]{1,0:T(8,128)(2,1)} collective-permute-done((bf16[192,2048]{1,0:T(8,128)(2,1)}, bf16[192,2048]{1,0:T(8,128)(2,1)}, u32[]{:S(2)}, u32[]{:S(2)}) %collective-permute-start.4) | collective-permute-done | bytes 786464 | tf_op jit(solution)/shard_map/cond/branch_1_fun/ppermute | solution.py:27
  288.8 22.9 %conditional.60 = (bf16[192,2048]{1,0:T(8,128)(2,1)S(1)}, bf16[192,2048]{1,0:T(8,128)(2,1)}) conditional(s32[]{:T(128)} %bitcast.63, () %tuple.681, (f32[768,2048]{1,0:T(8,128)}, bf16[768,2048]{1,0:T(8,128)(2,1)}) %tuple.683), branch_computations={%region_36.37_spmd, %region_37.38_spmd} | conditional | flops 2359296 | bytes 9437240 | solution.py:63
  293.1 18.5 %collective-permute-done.27 = bf16[192,2048]{1,0:T(8,128)(2,1)} collective-permute-done((bf16[192,2048]{1,0:T(8,128)(2,1)S(1)}, bf16[192,2048]{1,0:T(8,128)(2,1)}, u32[]{:S(2)}, u32[]{:S(2)}) %collective-permute-start.27) | collective-permute-done | bytes 786464 | tf_op jit(solution)/shard_map/cond/branch_1_fun/ppermute | solution.py:27
  314.8 22.4 %conditional.62 = (bf16[192,2048]{1,0:T(8,128)(2,1)}, bf16[192,2048]{1,0:T(8,128)(2,1)}) conditional(s32[]{:T(128)} %bitcast.63, () %tuple.680, (f32[768,2048]{1,0:T(8,128)}, bf16[768,2048]{1,0:T(8,128)(2,1)}, bf16[192,2048]{1,0:T(8,128)(2,1)}, bf16[192,2048]{1,0:T(8,128)(2,1)S(1)}) %tuple.693), branch_computations={%region_40.41_spmd, %region_41.42_spmd} | conditional | flops 1966080 | bytes 10223712 | solution.py:63
  319.7 16.6 %collective-permute-done.28 = bf16[192,2048]{1,0:T(8,128)(2,1)} collective-permute-done((bf16[192,2048]{1,0:T(8,128)(2,1)S(1)}, bf16[192,2048]{1,0:T(8,128)(2,1)}, u32[]{:S(2)}, u32[]{:S(2)}) %collective-permute-start.28) | collective-permute-done | bytes 786464 | tf_op jit(solution)/shard_map/cond/branch_1_fun/ppermute | solution.py:27
  344.1 41.6 %conditional.63 = (bf16[192,2048]{1,0:T(8,128)(2,1)S(1)}, bf16[192,2048]{1,0:T(8,128)(2,1)}, bf16[192,2048]{1,0:T(8,128)(2,1)}, bf16[192,2048]{1,0:T(8,128)(2,1)...) conditional(s32[]{:T(128)} %bitcast.63, () %tuple.603, ...), branch_computations={%region_42.43_spmd, %region_43.44_spmd} | conditional | bytes 23593304 | solution.py:63
  347.0 14.7 %collective-permute-done.7 = bf16[192,2048]{1,0:T(8,128)(2,1)} collective-permute-done((bf16[192,2048]{1,0:T(8,128)(2,1)S(1)}, bf16[192,2048]{1,0:T(8,128)(2,1)}, u32[]{:S(2)}, u32[]{:S(2)}) %collective-permute-start.7) | collective-permute-done | bytes 786464 | tf_op jit(solution)/shard_map/cond/branch_1_fun/ppermute | solution.py:27
  363.2 15.1 %collective-permute-done.6 = bf16[192,2048]{1,0:T(8,128)(2,1)} collective-permute-done((bf16[192,2048]{1,0:T(8,128)(2,1)S(1)}, bf16[192,2048]{1,0:T(8,128)(2,1)}, u32[]{:S(2)}, u32[]{:S(2)}) %collective-permute-start.6) | collective-permute-done | bytes 786464 | tf_op jit(solution)/shard_map/cond/branch_1_fun/ppermute | solution.py:27
  390.8 32.0 %conditional.64 = (bf16[1536,2048]{1,0:T(8,128)(2,1)}, bf16[1536,2048]{1,0:T(8,128)(2,1)S(1)}, bf16[2048,1024]{1,0:T(8,128)(2,1)S(1)}) conditional(s32[]{:T(128)} %bitcast.63, () %tuple.602, (bf16[192,2048]{1,0:T(8,128)(2,1)}, bf16[192,2048]{1,0:T(8,128)(2,1)}, bf16[192,2048]{1,0:T(8,128)(2,1)}, bf16[192,2048]{1,0:T(8,128)(2,1)}, ...), branch_computations={%region_44.45_spmd, %region_45.46_spmd} | conditional | bytes 40894884 | solution.py:63
  452.7 14.5 %shard_map.236 = (bf16[1536,1024]{1,0:T(8,128)(2,1)}, f32[1536,1024]{1,0:T(8,128)}) custom-call(bf16[1536,2048]{1,0:T(8,128)(2,1)S(1)} %bitcast.166, bf16[2048,1024]{1,0:T(8,128)(2,1)} %shard_map.235.right_ref.up_ref, f32[1,1024]{1,0:T(1,128)S(1)} %get-tuple-element.1769.shift_ref), custom_call_target="tpu_custom_call" | custom-call | tf_op jit(solution)/shard_map/pallas_call | solution.py:762
  479.2 17.7 %shard_map.239 = bf16[4,2,192,768]{3,2,1,0:T(8,128)(2,1)S(1)} custom-call(s32[5]{0:T(128)S(1)} %copy-done.91, bf16[2,768,768]{2,1,0:T(8,128)(2,1)S(1)} %get-tuple-element.1753.kept_ref, f32[2,768,128]{2,1,0:T(8,128)S(1)} %get-tuple-element.1754.sums_ref, bf16[4,2,192,256]{3,2,1,0:T(8,128)(2,1)S(1)} %bitcast.164, f32[2,768,128]{2,1,0:T(8,128)S(1)} %copy-done.52, ...), custom_call_target="tpu_custom_call" | custom-call | tf_op jit(solution)/shard_map/pallas_call | solution.py:739
  545.1 24.2 %conditional.66 = (bf16[192,2048]{1,0:T(8,128)(2,1)}, bf16[192,2048]{1,0:T(8,128)(2,1)}, bf16[1024,512]{1,0:T(8,128)(2,1)}, bf16[512,1024]{1,0:T(8,128)(2,1)}, b...) conditional(s32[]{:T(128)} %bitcast.63, () %tuple.737, ...), branch_computations={%region_48.49_spmd, %region_49.52_spmd} | conditional | flops 7862528 | bytes 40115332 | solution.py:63
  572.1 31.9 %conditional.67 = (bf16[192,2048]{1,0:T(8,128)(2,1)}, bf16[192,2048]{1,0:T(8,128)(2,1)}, bf16[512,1024]{1,0:T(8,128)(2,1)}, f32[768,2048]{1,0:T(8,128)}, bf16[768,2048]{1,0:T(8,128)(2,1)}) conditional(s32[]{:T(128)} %bitcast.63, () %tuple.569, (f32[768,2048]{1,0:T(8,128)}, bf16[768,2048]{1,0:T(8,128)(2,1)}, bf16[192,2048]{1,0:T(8,128)(2,1)}, ...), branch_computations={%region_52.53_spmd, %region_53.54_spmd} | conditional | flops 1966080 | bytes 54264044 | solution.py:63
  609.9 43.2 %conditional.68 = (bf16[192,2048]{1,0:T(8,128)(2,1)S(1)}, bf16[192,2048]{1,0:T(8,128)(2,1)}, bf16[192,2048]{1,0:T(8,128)(2,1)S(1)}, bf16[192,2048]{1,0:T(8,128)(...) conditional(s32[]{:T(128)} %bitcast.63, () %tuple.751, ...), branch_computations={%region_54.55_spmd, %region_55.56_spmd} | conditional | flops 2359296 | bytes 23593216 | solution.py:63
  613.1 15.8 %collective-permute-done.34 = bf16[192,2048]{1,0:T(8,128)(2,1)} collective-permute-done((bf16[192,2048]{1,0:T(8,128)(2,1)S(1)}, bf16[192,2048]{1,0:T(8,128)(2,1)}, u32[]{:S(2)}, u32[]{:S(2)}) %collective-permute-start.34) | collective-permute-done | bytes 786464 | tf_op jit(solution)/shard_map/cond/branch_1_fun/ppermute | solution.py:27
  633.2 15.5 %collective-permute-done.35 = bf16[192,2048]{1,0:T(8,128)(2,1)} collective-permute-done((bf16[192,2048]{1,0:T(8,128)(2,1)S(1)}, bf16[192,2048]{1,0:T(8,128)(2,1)}, u32[]{:S(2)}, u32[]{:S(2)}) %collective-permute-start.35) | collective-permute-done | bytes 786464 | tf_op jit(solution)/shard_map/cond/branch_1_fun/ppermute | solution.py:27
  657.1 27.1 %conditional.69 = (bf16[1536,2048]{1,0:T(8,128)(2,1)S(1)}, bf16[512,1024]{1,0:T(8,128)(2,1)}) conditional(s32[]{:T(128)} %bitcast.63, () %tuple.760, (bf16[192,2048]{1,0:T(8,128)(2,1)}, bf16[192,2048]{1,0:T(8,128)(2,1)S(1)}, bf16[192,2048]{1,0:T(8,128)(2,1)}, bf16[192,2048]{1,0:T(8,128)(2,1)}, bf16[192,2048]{1,0:T(8,128)(2,1)}, ...), branch_computations={%region_56.57_spmd, %region_57.58_spmd} | conditional | bytes 15728832 | solution.py:63
  658.6 17.7 %collective-permute-done.19.refs_3_ = bf16[192,2048]{1,0:T(8,128)(2,1)S(1)} collective-permute-done((bf16[192,2048]{1,0:T(8,128)(2,1)}, bf16[192,2048]{1,0:T(8,128)(2,1)S(1)}, u32[]{:S(2)}, u32[]{:S(2)}) %collective-permute-start.19) | collective-permute-done | bytes 786464 | tf_op jit(solution)/shard_map/cond/branch_1_fun/ppermute | solution.py:27
  703.9 18.4 %shard_map.250 = bf16[4,2,192,768]{3,2,1,0:T(8,128)(2,1)} custom-call(s32[5]{0:T(128)S(1)} %copy-done.91, bf16[2,768,768]{2,1,0:T(8,128)(2,1)S(1)} %copy-done.4, f32[2,768,128]{2,1,0:T(8,128)S(1)} %copy-done.12, bf16[4,2,192,256]{3,2,1,0:T(8,128)(2,1)S(1)} %bitcast.163, f32[2,768,128]{2,1,0:T(8,128)S(1)} %copy-done.53, ...), custom_call_target="tpu_custom_call" | custom-call | tf_op jit(solution)/shard_map/pallas_call | solution.py:739
  798.8 38.1 %conditional.72 = (bf16[192,2048]{1,0:T(8,128)(2,1)}, bf16[192,2048]{1,0:T(8,128)(2,1)}) conditional(s32[]{:T(128)} %bitcast.63, () %tuple.750, (f32[768,2048]{1,0:T(8,128)}, bf16[768,2048]{1,0:T(8,128)(2,1)}, bf16[192,2048]{1,0:T(8,128)(2,1)}, bf16[192,2048]{1,0:T(8,128)(2,1)S(1)}) %tuple.1076), branch_computations={%region_62.63_spmd, %region_63.64_spmd} | conditional | flops 1966080 | bytes 10223712 | solution.py:63
  803.9 33.0 %collective-permute-done.39 = bf16[192,2048]{1,0:T(8,128)(2,1)} collective-permute-done((bf16[192,2048]{1,0:T(8,128)(2,1)S(1)}, bf16[192,2048]{1,0:T(8,128)(2,1)}, u32[]{:S(2)}, u32[]{:S(2)}) %collective-permute-start.39) | collective-permute-done | bytes 786464 | tf_op jit(solution)/shard_map/cond/branch_1_fun/ppermute | solution.py:27
  850.7 23.2 %conditional.74 = (bf16[192,2048]{1,0:T(8,128)(2,1)}, bf16[192,2048]{1,0:T(8,128)(2,1)}, bf16[512,1024]{1,0:T(8,128)(2,1)}, f32[768]{0:T(1024)S(1)}, f32[1024]{0:T(1024)S(1)}, /*index=5*/bf16[256,1024]{1,0:T(8,128)(2,1)}) conditional(s32[]{:T(128)} %bitcast.63, () %tuple.821, (f32[768,2048]{1,0:T(8,128)}, bf16[768,2048]{1,0:T(8,128)(2,1)}, ...), branch_computations={%region_66.67_spmd, %region_67.70_spmd} | conditional | flops 7862528 | bytes 64232660 | solution.py:63
  888.2 47.0 %conditional.75 = (bf16[192,2048]{1,0:T(8,128)(2,1)}, bf16[192,2048]{1,0:T(8,128)(2,1)}, bf16[1024,512]{1,0:T(8,128)(2,1)S(1)}) conditional(s32[]{:T(128)} %bitcast.63, () %tuple.820, (f32[768,2048]{1,0:T(8,128)}, bf16[768,2048]{1,0:T(8,128)(2,1)}, bf16[192,2048]{1,0:T(8,128)(2,1)}, bf16[192,2048]{1,0:T(8,128)(2,1)}, ...), branch_computations={%region_70.71_spmd, %region_71.72_spmd} | conditional | flops 1966080 | bytes 10223720 | solution.py:63
  895.8 39.4 %collective-permute-done.43 = bf16[192,2048]{1,0:T(8,128)(2,1)} collective-permute-done((bf16[192,2048]{1,0:T(8,128)(2,1)S(1)}, bf16[192,2048]{1,0:T(8,128)(2,1)}, u32[]{:S(2)}, u32[]{:S(2)}) %collective-permute-start.43) | collective-permute-done | bytes 786464 | tf_op jit(solution)/shard_map/cond/branch_1_fun/ppermute | solution.py:27
  941.4 24.7 %conditional.76 = (f32[6,2,1,1,64]{4,3,2,1,0:T(1,128)S(1)}, f32[7168]{0:T(1024)S(1)}) conditional(s32[]{:T(128)} %bitcast.63, () %tuple.845, (f32[8,2048]{1,0:T(8,128)S(1)}, f32[8,2048]{1,0:T(8,128)S(1)}, f32[768]{0:T(1024)S(1)}, f32[1024]{0:T(1024)S(1)}, f32[768]{0:T(1024)S(1)}, /*index=5*/f32[1024]{0:T(1024)S(1)}, s32[]{:T(128)}, ...), branch_computations={%region_72.73_spmd, %region_73.74_spmd} | conditional | flops 56860 | bytes 1338890 | solution.py:63
  (709 shorter events, 792.3 us)
Async XLA Ops:
  50.5 66.3 %collective-permute-start.59 = (bf16[512,1024]{1,0:T(8,128)(2,1)}, bf16[512,1024]{1,0:T(8,128)(2,1)S(1)}, u32[]{:S(2)}, u32[]{:S(2)}) collective-permute-start(bf16[512,1024]{1,0:T(8,128)(2,1)} %copy.72), channel_id=1, source_target_pairs={{0,4},{4,0},{8,12},{12,8},{16,20},{20,16},{24,28},{28,24},{1,5},{5... | collective-permute-start | bytes 3145736 | tf_op jit(solution)/shard_map/ppermute | solution.py:27
  54.4 62.4 %collective-permute-start.58 = (bf16[512,1024]{1,0:T(8,128)(2,1)}, bf16[512,1024]{1,0:T(8,128)(2,1)}, u32[]{:S(2)}, u32[]{:S(2)}) collective-permute-start(bf16[512,1024]{1,0:T(8,128)(2,1)} %copy.71), channel_id=1, source_target_pairs={{0,16},{4,20},{8,24},{12,28},{16,0},{20,4},{24,8},{28,12},{1,17},{... | collective-permute-start | bytes 3145736 | tf_op jit(solution)/shard_map/ppermute | solution.py:27
  116.8 48.5 %collective-permute-start.62 = (bf16[512,1024]{1,0:T(8,128)(2,1)}, bf16[512,1024]{1,0:T(8,128)(2,1)}, u32[]{:S(2)}, u32[]{:S(2)}) collective-permute-start(bf16[512,1024]{1,0:T(8,128)(2,1)} %copy-done.61), channel_id=1, source_target_pairs={{0,16},{4,20},{8,24},{12,28},{16,0},{20,4},{24,8},{28,12},{1,17},{... | collective-permute-start | bytes 3145736 | tf_op jit(solution)/shard_map/ppermute | solution.py:27
  117.3 48.6 %collective-permute-start.61 = (bf16[512,1024]{1,0:T(8,128)(2,1)}, bf16[512,1024]{1,0:T(8,128)(2,1)}, u32[]{:S(2)}, u32[]{:S(2)}) collective-permute-start(bf16[512,1024]{1,0:T(8,128)(2,1)} %copy-done.61), channel_id=1, source_target_pairs={{0,4},{4,0},{8,12},{12,8},{16,20},{20,16},{24,28},{28,24},{1,5},{5... | collective-permute-start | bytes 3145736 | tf_op jit(solution)/shard_map/ppermute | solution.py:27
  117.8 48.1 %collective-permute-start.60 = (bf16[512,1024]{1,0:T(8,128)(2,1)}, bf16[512,1024]{1,0:T(8,128)(2,1)}, u32[]{:S(2)}, u32[]{:S(2)}) collective-permute-start(bf16[512,1024]{1,0:T(8,128)(2,1)} %collective-permute-done.58.refs_1_), channel_id=1, source_target_pairs={{0,4},{4,0},{8,12},{12,8},{16,20},{20,16},{24,28},{28,24},{1,5},{5... | collective-permute-start | bytes 3145736 | tf_op jit(solution)/shard_map/ppermute | solution.py:27
  165.9 45.3 %collective-permute-start.63 = (bf16[512,1024]{1,0:T(8,128)(2,1)}, bf16[512,1024]{1,0:T(8,128)(2,1)}, u32[]{:S(2)}, u32[]{:S(2)}) collective-permute-start(bf16[512,1024]{1,0:T(8,128)(2,1)} %collective-permute-done.62.refs_1_), channel_id=1, source_target_pairs={{0,4},{4,0},{8,12},{12,8},{16,20},{20,16},{24,28},{28,24},{1,5},{5... | collective-permute-start | bytes 3145736 | tf_op jit(solution)/shard_map/ppermute | solution.py:27
  166.5 72.7 %collective-permute-start.64 = (bf16[1024,512]{1,0:T(8,128)(2,1)}, bf16[1024,512]{1,0:T(8,128)(2,1)}, u32[]{:S(2)}, u32[]{:S(2)}) collective-permute-start(bf16[1024,512]{1,0:T(8,128)(2,1)} %get-tuple-element.2659.refs_0_), channel_id=1, source_target_pairs={{0,16},{4,20},{8,24},{12,28},{16,0},{20,4},{24,8},{28,12},{1,17},{... | collective-permute-start | bytes 3145736 | tf_op jit(solution)/shard_map/ppermute | solution.py:27
  183.1 57.2 %collective-permute-start.67 = (bf16[1024,512]{1,0:T(8,128)(2,1)}, bf16[1024,512]{1,0:T(8,128)(2,1)S(1)}, u32[]{:S(2)}, u32[]{:S(2)}) collective-permute-start(bf16[1024,512]{1,0:T(8,128)(2,1)} %get-tuple-element.2659.refs_0_), channel_id=1, source_target_pairs={{0,4},{4,0},{8,12},{12,8},{16,20},{20,16},{24,28},{28,24},{1,5},{5... | collective-permute-start | bytes 3145736 | tf_op jit(solution)/shard_map/ppermute | solution.py:27
  260.9 52.6 %collective-permute-start.69 = (bf16[512,1024]{1,0:T(8,128)(2,1)}, bf16[512,1024]{1,0:T(8,128)(2,1)}, u32[]{:S(2)}, u32[]{:S(2)}) collective-permute-start(bf16[512,1024]{1,0:T(8,128)(2,1)} %copy.77), channel_id=1, source_target_pairs={{0,16},{4,20},{8,24},{12,28},{16,0},{20,4},{24,8},{28,12},{1,17},{... | collective-permute-start | bytes 3145736 | tf_op jit(solution)/shard_map/ppermute | solution.py:27
  269.8 45.0 %collective-permute-start.71 = (bf16[512,1024]{1,0:T(8,128)(2,1)}, bf16[512,1024]{1,0:T(8,128)(2,1)}, u32[]{:S(2)}, u32[]{:S(2)}) collective-permute-start(bf16[512,1024]{1,0:T(8,128)(2,1)} %copy.78), channel_id=1, source_target_pairs={{0,4},{4,0},{8,12},{12,8},{16,20},{20,16},{24,28},{28,24},{1,5},{5... | collective-permute-start | bytes 3145736 | tf_op jit(solution)/shard_map/ppermute | solution.py:27
  337.2 48.6 %collective-permute-start.74 = (bf16[512,1024]{1,0:T(8,128)(2,1)}, bf16[512,1024]{1,0:T(8,128)(2,1)}, u32[]{:S(2)}, u32[]{:S(2)}) collective-permute-start(bf16[512,1024]{1,0:T(8,128)(2,1)} %collective-permute-done.69), channel_id=1, source_target_pairs={{0,4},{4,0},{8,12},{12,8},{16,20},{20,16},{24,28},{28,24},{1,5},{5... | collective-permute-start | bytes 3145736 | tf_op jit(solution)/shard_map/ppermute | solution.py:27
  338.9 46.9 %collective-permute-start.73 = (bf16[512,1024]{1,0:T(8,128)(2,1)}, bf16[512,1024]{1,0:T(8,128)(2,1)}, u32[]{:S(2)}, u32[]{:S(2)}) collective-permute-start(bf16[512,1024]{1,0:T(8,128)(2,1)} %get-tuple-element.2663.refs_0_), channel_id=1, source_target_pairs={{0,4},{4,0},{8,12},{12,8},{16,20},{20,16},{24,28},{28,24},{1,5},{5... | collective-permute-start | bytes 3145736 | tf_op jit(solution)/shard_map/ppermute | solution.py:27
  339.2 46.7 %collective-permute-start.72 = (bf16[512,1024]{1,0:T(8,128)(2,1)}, bf16[512,1024]{1,0:T(8,128)(2,1)}, u32[]{:S(2)}, u32[]{:S(2)}) collective-permute-start(bf16[512,1024]{1,0:T(8,128)(2,1)} %get-tuple-element.2663.refs_0_), channel_id=1, source_target_pairs={{0,16},{4,20},{8,24},{12,28},{16,0},{20,4},{24,8},{28,12},{1,17},{... | collective-permute-start | bytes 3145736 | tf_op jit(solution)/shard_map/ppermute | solution.py:27
  385.9 48.8 %collective-permute-start.76 = (bf16[1024,512]{1,0:T(8,128)(2,1)}, bf16[1024,512]{1,0:T(8,128)(2,1)}, u32[]{:S(2)}, u32[]{:S(2)}) collective-permute-start(bf16[1024,512]{1,0:T(8,128)(2,1)} %copy-done.63), channel_id=1, source_target_pairs={{0,4},{4,0},{8,12},{12,8},{16,20},{20,16},{24,28},{28,24},{1,5},{5... | collective-permute-start | bytes 3145736 | tf_op jit(solution)/shard_map/ppermute | solution.py:27
  387.6 47.1 %collective-permute-start.75 = (bf16[512,1024]{1,0:T(8,128)(2,1)}, bf16[512,1024]{1,0:T(8,128)(2,1)}, u32[]{:S(2)}, u32[]{:S(2)}) collective-permute-start(bf16[512,1024]{1,0:T(8,128)(2,1)} %collective-permute-done.72.refs_1_), channel_id=1, source_target_pairs={{0,4},{4,0},{8,12},{12,8},{16,20},{20,16},{24,28},{28,24},{1,5},{5... | collective-permute-start | bytes 3145736 | tf_op jit(solution)/shard_map/ppermute | solution.py:27
  387.9 79.3 %collective-permute-start.77 = (bf16[1024,512]{1,0:T(8,128)(2,1)}, bf16[1024,512]{1,0:T(8,128)(2,1)}, u32[]{:S(2)}, u32[]{:S(2)}) collective-permute-start(bf16[1024,512]{1,0:T(8,128)(2,1)} %copy-done.63), channel_id=1, source_target_pairs={{0,16},{4,20},{8,24},{12,28},{16,0},{20,4},{24,8},{28,12},{1,17},{... | collective-permute-start | bytes 3145736 | tf_op jit(solution)/shard_map/ppermute | solution.py:27
  474.0 65.5 %collective-permute-start.79 = (bf16[1024,512]{1,0:T(8,128)(2,1)}, bf16[1024,512]{1,0:T(8,128)(2,1)}, u32[]{:S(2)}, u32[]{:S(2)}) collective-permute-start(bf16[1024,512]{1,0:T(8,128)(2,1)} %shard_map.237), channel_id=1, source_target_pairs={{0,4},{4,0},{8,12},{12,8},{16,20},{20,16},{24,28},{28,24},{1,5},{5... | collective-permute-start | bytes 3145736 | tf_op jit(solution)/shard_map/ppermute | solution.py:27
  506.2 63.1 %collective-permute-start.81 = (bf16[1024,512]{1,0:T(8,128)(2,1)}, bf16[1024,512]{1,0:T(8,128)(2,1)}, u32[]{:S(2)}, u32[]{:S(2)}) collective-permute-start(bf16[1024,512]{1,0:T(8,128)(2,1)} %shard_map.241), channel_id=1, source_target_pairs={{0,4},{4,0},{8,12},{12,8},{16,20},{20,16},{24,28},{28,24},{1,5},{5... | collective-permute-start | bytes 3145736 | tf_op jit(solution)/shard_map/ppermute | solution.py:27
  608.3 44.8 %collective-permute-start.83 = (bf16[512,1024]{1,0:T(8,128)(2,1)}, bf16[512,1024]{1,0:T(8,128)(2,1)}, u32[]{:S(2)}, u32[]{:S(2)}) collective-permute-start(bf16[512,1024]{1,0:T(8,128)(2,1)} %get-tuple-element.1902), channel_id=1, source_target_pairs={{0,4},{4,0},{8,12},{12,8},{16,20},{20,16},{24,28},{28,24},{1,5},{5... | collective-permute-start | bytes 3145736 | tf_op jit(solution)/shard_map/ppermute | solution.py:27
  608.8 75.8 %collective-permute-start.84 = (bf16[1024,512]{1,0:T(8,128)(2,1)}, bf16[1024,512]{1,0:T(8,128)(2,1)}, u32[]{:S(2)}, u32[]{:S(2)}) collective-permute-start(bf16[1024,512]{1,0:T(8,128)(2,1)} %get-tuple-element.1920), channel_id=1, source_target_pairs={{0,16},{4,20},{8,24},{12,28},{16,0},{20,4},{24,8},{28,12},{1,17},{... | collective-permute-start | bytes 3145736 | tf_op jit(solution)/shard_map/ppermute | solution.py:27
  653.1 74.9 %collective-permute-start.86 = (bf16[512,1024]{1,0:T(8,128)(2,1)}, bf16[512,1024]{1,0:T(8,128)(2,1)}, u32[]{:S(2)}, u32[]{:S(2)}) collective-permute-start(bf16[512,1024]{1,0:T(8,128)(2,1)} %get-tuple-element.1950), channel_id=1, source_target_pairs={{0,16},{4,20},{8,24},{12,28},{16,0},{20,4},{24,8},{28,12},{1,17},{... | collective-permute-start | bytes 3145736 | tf_op jit(solution)/shard_map/ppermute | solution.py:27
  655.5 72.5 %collective-permute-start.85 = (bf16[512,1024]{1,0:T(8,128)(2,1)}, bf16[512,1024]{1,0:T(8,128)(2,1)}, u32[]{:S(2)}, u32[]{:S(2)}) collective-permute-start(bf16[512,1024]{1,0:T(8,128)(2,1)} %get-tuple-element.1949), channel_id=1, source_target_pairs={{0,4},{4,0},{8,12},{12,8},{16,20},{20,16},{24,28},{28,24},{1,5},{5... | collective-permute-start | bytes 3145736 | tf_op jit(solution)/shard_map/ppermute | solution.py:27
  684.2 81.0 %collective-permute-start.90 = (bf16[512,1024]{1,0:T(8,128)(2,1)}, bf16[512,1024]{1,0:T(8,128)(2,1)}, u32[]{:S(2)}, u32[]{:S(2)}) collective-permute-start(bf16[512,1024]{1,0:T(8,128)(2,1)} %get-tuple-element.1987), channel_id=1, source_target_pairs={{0,16},{4,20},{8,24},{12,28},{16,0},{20,4},{24,8},{28,12},{1,17},{... | collective-permute-start | bytes 3145736 | tf_op jit(solution)/shard_map/ppermute | solution.py:27
  698.3 54.9 %collective-permute-start.88 = (bf16[1024,256]{1,0:T(8,128)(2,1)}, bf16[1024,256]{1,0:T(8,128)(2,1)S(1)}, u32[]{:S(2)}, u32[]{:S(2)}) collective-permute-start(bf16[1024,256]{1,0:T(8,128)(2,1)} %get-tuple-element.1966), channel_id=1, source_target_pairs={{0,8},{4,12},{8,0},{12,4},{16,24},{20,28},{24,16},{28,20},{1,9},{5... | collective-permute-start | bytes 1572872 | tf_op jit(solution)/shard_map/ppermute | solution.py:27
  747.4 46.2 %collective-permute-start.87 = (bf16[512,1024]{1,0:T(8,128)(2,1)}, bf16[512,1024]{1,0:T(8,128)(2,1)}, u32[]{:S(2)}, u32[]{:S(2)}) collective-permute-start(bf16[512,1024]{1,0:T(8,128)(2,1)} %shard_map.253), channel_id=1, source_target_pairs={{0,4},{4,0},{8,12},{12,8},{16,20},{20,16},{24,28},{28,24},{1,5},{5... | collective-permute-start | bytes 3145736 | tf_op jit(solution)/shard_map/ppermute | solution.py:27
  772.0 101.9 %collective-permute-start.94 = (bf16[1024,512]{1,0:T(8,128)(2,1)}, bf16[1024,512]{1,0:T(8,128)(2,1)}, u32[]{:S(2)}, u32[]{:S(2)}) collective-permute-start(bf16[1024,512]{1,0:T(8,128)(2,1)} %shard_map.259), channel_id=1, source_target_pairs={{0,16},{4,20},{8,24},{12,28},{16,0},{20,4},{24,8},{28,12},{1,17},{... | collective-permute-start | bytes 3145736 | tf_op jit(solution)/shard_map/ppermute | solution.py:27
  773.8 101.2 %collective-permute-start.93 = (bf16[512,1024]{1,0:T(8,128)(2,1)}, bf16[512,1024]{1,0:T(8,128)(2,1)}, u32[]{:S(2)}, u32[]{:S(2)}) collective-permute-start(bf16[512,1024]{1,0:T(8,128)(2,1)} %shard_map.256), channel_id=1, source_target_pairs={{0,4},{4,0},{8,12},{12,8},{16,20},{20,16},{24,28},{28,24},{1,5},{5... | collective-permute-start | bytes 3145736 | tf_op jit(solution)/shard_map/ppermute | solution.py:27
  873.9 92.3 %collective-permute-start.96 = (bf16[512,1024]{1,0:T(8,128)(2,1)}, bf16[512,1024]{1,0:T(8,128)(2,1)}, u32[]{:S(2)}, u32[]{:S(2)}) collective-permute-start(bf16[512,1024]{1,0:T(8,128)(2,1)} %shard_map.261), channel_id=1, source_target_pairs={{0,16},{4,20},{8,24},{12,28},{16,0},{20,4},{24,8},{28,12},{1,17},{... | collective-permute-start | bytes 3145736 | tf_op jit(solution)/shard_map/ppermute | solution.py:27
  882.0 104.3 %collective-permute-start.95 = (bf16[512,1024]{1,0:T(8,128)(2,1)}, bf16[512,1024]{1,0:T(8,128)(2,1)}, u32[]{:S(2)}, u32[]{:S(2)}) collective-permute-start(bf16[512,1024]{1,0:T(8,128)(2,1)} %shard_map.266), channel_id=1, source_target_pairs={{0,16},{4,20},{8,24},{12,28},{16,0},{20,4},{24,8},{28,12},{1,17},{... | collective-permute-start | bytes 3145736 | tf_op jit(solution)/shard_map/ppermute | solution.py:27
  884.9 103.7 %collective-permute-start.98 = (bf16[512,1024]{1,0:T(8,128)(2,1)}, bf16[512,1024]{1,0:T(8,128)(2,1)}, u32[]{:S(2)}, u32[]{:S(2)}) collective-permute-start(bf16[512,1024]{1,0:T(8,128)(2,1)} %get-tuple-element.2186), channel_id=1, source_target_pairs={{0,4},{4,0},{8,12},{12,8},{16,20},{20,16},{24,28},{28,24},{1,5},{5... | collective-permute-start | bytes 3145736 | tf_op jit(solution)/shard_map/ppermute | solution.py:27
  890.5 44.7 %collective-permute-start.43 = (bf16[192,2048]{1,0:T(8,128)(2,1)S(1)}, bf16[192,2048]{1,0:T(8,128)(2,1)}, u32[]{:S(2)}, u32[]{:S(2)}) collective-permute-start(bf16[192,2048]{1,0:T(8,128)(2,1)S(1)} %add_convert_fusion.11), channel_id=1, source_target_pairs={{0,8},{4,12},{8,0},{12,4},{16,24},{20,28},{24,16},{28,20},{1,9},{5... | collective-permute-start | bytes 2359304 | tf_op jit(solution)/shard_map/cond/branch_1_fun/ppermute | solution.py:27
  890.6 44.6 %collective-permute-start.44 = (bf16[192,2048]{1,0:T(8,128)(2,1)}, bf16[192,2048]{1,0:T(8,128)(2,1)}, u32[]{:S(2)}, u32[]{:S(2)}) collective-permute-start(bf16[192,2048]{1,0:T(8,128)(2,1)} %get-tuple-element.555), channel_id=1, source_target_pairs={{0,2},{1,3},{2,0},{3,1},{4,6},{5,7},{6,4},{7,5},{8,10},{9,11},{10,... | collective-permute-start | bytes 2359304 | tf_op jit(solution)/shard_map/cond/branch_1_fun/ppermute | solution.py:27
  (178 other events, 2378.4 us)

commit v4 on v3

--- a/solution.py
+++ b/solution.py
@@ -1116,14 +1116,20 @@
                 sums, _ = self.halve(
                     sums, none, 3, (tensor >> bit) & 1, lambda value: swap(value, "tensor", bit)
                 )
+            return sums, biases
+
+        values = [value for pair in self.in_bgrads for value in pair]
+        self.sums, self.biases = self.seq.settle(step, *self.norm_grads, *values)
+
+    def second(self):
+        def step(sums, biases):
             sums, other = self.halve(
                 sums, biases, 2, self.mid, lambda value: swap(value, "dp", MID)
             )
             pair = (pick(biases, other, self.mid), pick(other, biases, self.mid))
             return sums, jnp.concatenate(pair)
 
-        values = [value for pair in self.in_bgrads for value in pair]
-        self.sums, self.biases = self.seq.settle(step, *self.norm_grads, *values)
+        self.sums, self.biases = self.seq.settle(step, self.sums, self.biases)
 
     def finish(self):
         def step(sums, biases):
@@ -1529,96 +1535,97 @@
     if early:
         send(down1, first)
         down2.make([0])
-    down2_pair = own_start(down2.blocks[0], 1)
+    sent = seq.run(branch.next, branch.low_part, branch.core, branch.x_high, apart=True)
+    branch_mid = seq.start(sent, "dp", MID)
     mixed_grad = attend_back(0, grad16)
-    down1.make(down1.near(second))
     if early:
         up2.wait_far()
         arrive(mix2, second)
-        send(down1, second)
     pre_grad = hide_back(0, grad16)
     up1, mix1 = up_grads(0, pre_grad), mixed_grads(0, mixed_grad, grad16)
     up1.make(up1.near(first))
     if early:
         send(up1, first)
         up2.make([0])
-    own_finish(1, "down", 0, down2_pair)
+    branch.mid = seq.wait(branch_mid)
+    if early:
+        mix2.wait_far()
+        seq.tick(2)
+        arrive(down1, first)
+        down1.make_far()
+        down1.send_far()
+    branch_low = seq.start(branch.later, "tensor", 1)
+    up2_pair = own_start(up2.blocks[0], 0)
     up1.make(up1.near(second))
     mix1.make(mix1.near(first))
+    down1.make(down1.near(second))
     if early:
-        mix2.wait_far()
-        seq.tick(5)
-        arrive(down1, first)
-        down1.make_far()
-        arrive(down1, second)
-        down1.send_far()
-        send(up1, second)
+        arrive(up1, first)
+        up1.make_far()
+        send(down1, second)
+    branch.x_low = seq.wait(branch_low)
+    down2_pair = own_start(down2.blocks[0], 1)
     back = rows_back(0, mixed_grad, pre_grad)
     back.begin()
     if early:
-        arrive(up1, first)
-        up1.make_far()
+        down1.wait_far()
         up1.send_far()
-    branch.third()
+    own_finish(1, "up", 1, up2_pair)
     if early:
         send(mix1, first)
-        mix2.make([0])
-    activations = branch.finish(partial(last_stream, order), streams[1], out_shifts[1])
-    up2_halves = seq.run(
-        lambda value: (halves(value, mid, 0), halves(value, 1 - mid, 0)), up2.blocks[0], apart=True
-    )
     made = back.second(
         lambda: (
             mix1.plain(mix1.near(second)),
             bias_back(mixed_grad, pre_grad),
-            swap(up2_halves[1], "dp", MID),
         )
     )
     mix1.take(mix1.near(second), made[0])
     in_bgrads[0] = made[1]
+    own_finish(1, "down", 0, down2_pair)
     if early:
-        down1.wait_far()
-        seq.tick(1)
-        arrive(up1, second)
-        seq.tick(1)
+        seq.tick(2)
+        arrive(down1, second)
+        seq.tick(4)
         arrive(mix1, first)
-        mix1.make_far()
-        mix1.send_far()
+        send(up1, second)
         send(mix1, second)
-    results["up"] = seq.run(
-        lambda keep, other: place_halves(keep, other, mid, 1, 1, layer_count),
-        up2_halves[0],
-        made[2],
-    )
-    made = back.third(lambda: down1.plain([0]) if early else ())
+    made = back.third(
+        lambda: (mix1.plain(mix1.far()), down1.plain([0]), mix2.plain([0])) if early else ()
+    )
     norm_grads[0], grad_stream, own = back.finish(
         norm_before, grad_stream, streams[0], gains[0]
     )
     if early:
-        down1.take([0], made)
+        mix1.take(mix1.far(), made[0])
+        down1.take([0], made[1])
+        mix2.take([0], made[2])
+        up1.wait_far()
+        seq.tick(7)
+        arrive(up1, second)
+        arrive(mix1, second)
+        mix1.send_far()
     else:
         rest(down1)
         rest(up1)
         rest(mix1)
-    small_sums = SmallSums(seq, norm_grads, in_bgrads, mid)
-    small_sums.first()
-    if early:
-        up1.wait_far()
     mix2_pair = own_start(mix2.blocks[0], 0)
     down1_pair = own_start(down1.blocks[0], 1)
     if early:
         up1.make([0])
     up1_pair = own_start(up1.blocks[0], 0)
+    small_sums = SmallSums(seq, norm_grads, in_bgrads, mid)
+    small_sums.first()
+    activations = branch.finish(partial(last_stream, order), streams[1], out_shifts[1])
+    input_grad = seq.run(lambda value: reorder(value, order, f32, True), grad_stream)
     mix2_own = mixed_finish(mix2_pair)
+    own_finish(0, "down", 0, down1_pair)
+    small_sums.second()
     if early:
         mix1.wait_far()
-        seq.tick(4)
-        arrive(mix1, second)
         mix1.make([0])
     mix1_pair = own_start(mix1.blocks[0], 0)
-    input_grad = seq.run(lambda value: reorder(value, order, f32, True), grad_stream)
-    own_finish(0, "down", 0, down1_pair)
     own_finish(0, "up", 1, up1_pair)
+    seq.tick(6)
     norm_owned, bias_both = small_sums.finish()
     mix1_own = mixed_finish(mix1_pair)
     bias_both = bias_both + 0.0 * seq.scalar

time: 1040 us -> 1000 us (0.962)
  waiting for transfers between devices: 373 us -> 331 us
    ppermute x102, waiting for transfers between devices: 373 us -> 331 us  [swap(): return lax.ppermute(value, axis, [(i, i ^ 1 << bit) for i in range(size)])]
    unnamed x181 -> x205, local copies, waits for them, and re-layouts: 21 us -> 24.5 us
  transfers between devices with their start and end apart: 102 -> 102, of which waited for: 47 -> 47; matrix products, arithmetic and copies ran while one was open for 9% -> 10% of each run, Pallas kernels for 39% -> 41%
where the time goes in v4:
time: 1000 us; the launch traced here: 992 us
  Pallas kernels  405 us (40%)
  waiting for transfers between devices  331 us (33%)
  starting transfers between devices  102 us (10%)
  local copies, waits for them, and re-layouts  93.7 us (9%)
  other arithmetic  53.6 us (5%)
    ppermute x102, waiting for transfers between devices, swap(): return lax.ppermute(value, axis, [(i, i ^ 1 << bit) for i in range(size)])  331 us
    pallas_call x42, Pallas kernels, call(): pl.pallas_call(kernel, grid_spec=pltpu.PrefetchScalarGridSpec(num_scalar_...  274 us
    ppermute x102, starting transfers between devices, swap(): return lax.ppermute(value, axis, [(i, i ^ 1 << bit) for i in range(size)])  102 us
    pallas_call x2, Pallas kernels, attention_backward(): pl.pallas_call(attention_back_kernel, grid_spec=pltpu.PrefetchScalarGridS...  35.1 us
    pallas_call x10, Pallas kernels, assemble(): pl.pallas_call(partial(assemble_kernel, axis, window), in_specs=[pl.Block...  30.8 us
    pallas_call x2, Pallas kernels, attention_forward(): pl.pallas_call(attention_kernel, grid_spec=pltpu.PrefetchScalarGridSpec(n...  25.1 us
    unnamed x205, local copies, waits for them, and re-layouts  24.5 us
  transfers between devices with their start and end apart: 102, of which 47 were waited for; matrix products, arithmetic and copies ran while one was open for 10% of the time, Pallas kernels for 41%

profile of v4, /device:TPU:0, one launch (start us, length us, event | category | flops | bytes accessed | tf_op | source)
XLA Modules:
  0.0 991.9 jit_solution(6617127896504474587)
XLA Ops:
  14.2 19.4 %conditional.45 = (bf16[2,1412]{1,0:T(2,128)(2,1)S(1)}, bf16[192,2048]{1,0:T(8,128)(2,1)}) conditional(s32[]{:T(128)} %bitcast.63, () %tuple.584, (s32[]{:T(128)}, bf16[1,1412]{1,0:T(2,128)(2,1)S(1)}, bf16[192,2048]{1,0:T(8,128)(2,1)}) %tuple.596), branch_computations={%region_4.0_spmd, %region_5.6_spmd} | conditional | flops 14121 | bytes 3179722 | solution.py:63
  17.8 13.5 %collective-permute-done.23 = bf16[1,1412]{1,0:T(2,128)(2,1)S(1)} collective-permute-done((bf16[1,1412]{1,0:T(2,128)(2,1)S(1)}, bf16[1,1412]{1,0:T(2,128)(2,1)S(1)}, u32[]{:S(2)}, u32[]{:S(2)}) %collective-permute-start.23) | collective-permute-done | bytes 2856 | tf_op jit(solution)/shard_map/cond/branch_1_fun/ppermute | solution.py:27
  68.2 48.0 %conditional.50 = (bf16[192,2048]{1,0:T(8,128)(2,1)}, bf16[192,2048]{1,0:T(8,128)(2,1)}, bf16[192,2048]{1,0:T(8,128)(2,1)}, bf16[192,2048]{1,0:T(8,128)(2,1)}, b...) conditional(s32[]{:T(128)} %bitcast.63, () %tuple.618, ...), branch_computations={%region_14.15_spmd, %region_15.16_spmd} | conditional | flops 1000228 | bytes 16529472 | solution.py:63
  71.4 37.4 %collective-permute-done.47 = bf16[192,2048]{1,0:T(8,128)(2,1)} collective-permute-done((bf16[192,2048]{1,0:T(8,128)(2,1)}, bf16[192,2048]{1,0:T(8,128)(2,1)}, u32[]{:S(2)}, u32[]{:S(2)}) %collective-permute-start.47) | collective-permute-done | bytes 786464 | tf_op jit(solution)/shard_map/cond/branch_1_fun/ppermute | solution.py:27
  120.9 37.5 %conditional.52 = (bf16[1024,256]{1,0:T(8,128)(2,1)}, bf16[1536,2048]{1,0:T(8,128)(2,1)}) conditional(s32[]{:T(128)} %bitcast.63, () %tuple.616, (bf16[1024,256]{1,0:T(8,128)(2,1)}, bf16[192,2048]{1,0:T(8,128)(2,1)}, bf16[192,2048]{1,0:T(8,128)(2,1)}, bf16[192,2048]{1,0:T(8,128)(2,1)}, bf16[192,2048]{1,0:T(8,128)(2,1)}, ...), branch_computations={%region_18.19_spmd, %region_19.20_spmd} | conditional | bytes 11534512 | solution.py:63
  124.9 26.0 %collective-permute-done = bf16[1024,256]{1,0:T(8,128)(2,1)} collective-permute-done((bf16[1024,256]{1,0:T(8,128)(2,1)}, bf16[1024,256]{1,0:T(8,128)(2,1)}, u32[]{:S(2)}, u32[]{:S(2)}) %collective-permute-start) | collective-permute-done | bytes 524320 | tf_op jit(solution)/shard_map/cond/branch_1_fun/ppermute | solution.py:27
  210.9 14.4 %shard_map.227 = (bf16[1536,1024]{1,0:T(8,128)(2,1)}, f32[1536,1024]{1,0:T(8,128)}) custom-call(bf16[1536,2048]{1,0:T(8,128)(2,1)} %get-tuple-element.2247.left_ref.normed_ref, bf16[2048,1024]{1,0:T(8,128)(2,1)S(1)} %shard_map.226.right_ref.up_ref, f32[1,1024]{1,0:T(1,128)S(1)} %get-tuple-element.1618.shift_ref), custom_call_target="tpu_custom_call" | custom-call | tf_op jit(solution)/shard_map/pallas_call | solution.py:762
  238.4 17.2 %conditional.58 = (bf16[192,2048]{1,0:T(8,128)(2,1)}) conditional(s32[]{:T(128)} %bitcast.63, () %tuple.675, bf16[192,2048]{1,0:T(8,128)(2,1)} %shard_map.220.grad_ref), branch_computations={%region_30.31_spmd, %region_31.32_spmd} | conditional | bytes 3145776 | solution.py:63
  238.4 17.2 %collective-permute-done.4 = bf16[192,2048]{1,0:T(8,128)(2,1)} collective-permute-done((bf16[192,2048]{1,0:T(8,128)(2,1)}, bf16[192,2048]{1,0:T(8,128)(2,1)}, u32[]{:S(2)}, u32[]{:S(2)}) %collective-permute-start.4) | collective-permute-done | bytes 786464 | tf_op jit(solution)/shard_map/cond/branch_1_fun/ppermute | solution.py:27
  288.4 23.1 %conditional.61 = (bf16[192,2048]{1,0:T(8,128)(2,1)S(1)}, bf16[192,2048]{1,0:T(8,128)(2,1)}) conditional(s32[]{:T(128)} %bitcast.63, () %tuple.692, (f32[768,2048]{1,0:T(8,128)}, bf16[768,2048]{1,0:T(8,128)(2,1)}) %tuple.694), branch_computations={%region_36.37_spmd, %region_37.38_spmd} | conditional | flops 2359296 | bytes 9437240 | solution.py:63
  293.0 18.5 %collective-permute-done.27 = bf16[192,2048]{1,0:T(8,128)(2,1)} collective-permute-done((bf16[192,2048]{1,0:T(8,128)(2,1)S(1)}, bf16[192,2048]{1,0:T(8,128)(2,1)}, u32[]{:S(2)}, u32[]{:S(2)}) %collective-permute-start.27) | collective-permute-done | bytes 786464 | tf_op jit(solution)/shard_map/cond/branch_1_fun/ppermute | solution.py:27
  316.3 22.7 %conditional.63 = (bf16[192,2048]{1,0:T(8,128)(2,1)}, bf16[192,2048]{1,0:T(8,128)(2,1)}) conditional(s32[]{:T(128)} %bitcast.63, () %tuple.691, (f32[768,2048]{1,0:T(8,128)}, bf16[768,2048]{1,0:T(8,128)(2,1)}, bf16[192,2048]{1,0:T(8,128)(2,1)}, bf16[192,2048]{1,0:T(8,128)(2,1)}) %tuple.1103), branch_computations={%region_40.41_spmd, %region_41.42_spmd} | conditional | flops 1966080 | bytes 13369468 | solution.py:63
  321.5 16.4 %collective-permute-done.28 = bf16[192,2048]{1,0:T(8,128)(2,1)} collective-permute-done((bf16[192,2048]{1,0:T(8,128)(2,1)S(1)}, bf16[192,2048]{1,0:T(8,128)(2,1)}, u32[]{:S(2)}, u32[]{:S(2)}) %collective-permute-start.28) | collective-permute-done | bytes 786464 | tf_op jit(solution)/shard_map/cond/branch_1_fun/ppermute | solution.py:27
  345.4 41.9 %conditional.64 = (bf16[192,2048]{1,0:T(8,128)(2,1)S(1)}, bf16[192,2048]{1,0:T(8,128)(2,1)}, bf16[192,2048]{1,0:T(8,128)(2,1)}, bf16[192,2048]{1,0:T(8,128)(2,1)...) conditional(s32[]{:T(128)} %bitcast.63, () %tuple.614, ...), branch_computations={%region_42.43_spmd, %region_43.44_spmd} | conditional | bytes 23593304 | solution.py:63
  348.5 14.5 %collective-permute-done.7 = bf16[192,2048]{1,0:T(8,128)(2,1)} collective-permute-done((bf16[192,2048]{1,0:T(8,128)(2,1)S(1)}, bf16[192,2048]{1,0:T(8,128)(2,1)}, u32[]{:S(2)}, u32[]{:S(2)}) %collective-permute-start.7) | collective-permute-done | bytes 786464 | tf_op jit(solution)/shard_map/cond/branch_1_fun/ppermute | solution.py:27
  364.5 15.3 %collective-permute-done.6 = bf16[192,2048]{1,0:T(8,128)(2,1)} collective-permute-done((bf16[192,2048]{1,0:T(8,128)(2,1)S(1)}, bf16[192,2048]{1,0:T(8,128)(2,1)}, u32[]{:S(2)}, u32[]{:S(2)}) %collective-permute-start.6) | collective-permute-done | bytes 786464 | tf_op jit(solution)/shard_map/cond/branch_1_fun/ppermute | solution.py:27
  392.4 32.0 %conditional.65 = (bf16[1536,2048]{1,0:T(8,128)(2,1)}, bf16[1536,2048]{1,0:T(8,128)(2,1)S(1)}, bf16[2048,1024]{1,0:T(8,128)(2,1)S(1)}) conditional(s32[]{:T(128)} %bitcast.63, () %tuple.613, (bf16[192,2048]{1,0:T(8,128)(2,1)}, bf16[192,2048]{1,0:T(8,128)(2,1)}, bf16[192,2048]{1,0:T(8,128)(2,1)}, bf16[192,2048]{1,0:T(8,128)(2,1)}, ...), branch_computations={%region_44.45_spmd, %region_45.46_spmd} | conditional | bytes 40894884 | solution.py:63
  453.9 14.2 %shard_map.236 = (bf16[1536,1024]{1,0:T(8,128)(2,1)S(1)}, f32[1536,1024]{1,0:T(8,128)}) custom-call(bf16[1536,2048]{1,0:T(8,128)(2,1)S(1)} %bitcast.168, bf16[2048,1024]{1,0:T(8,128)(2,1)} %shard_map.235.right_ref.up_ref, f32[1,1024]{1,0:T(1,128)S(1)} %copy-done.104), custom_call_target="tpu_custom_call" | custom-call | tf_op jit(solution)/shard_map/pallas_call | solution.py:762
  479.7 17.3 %shard_map.239 = bf16[4,2,192,768]{3,2,1,0:T(8,128)(2,1)S(1)} custom-call(s32[5]{0:T(128)S(1)} %copy-done.108, bf16[2,768,768]{2,1,0:T(8,128)(2,1)S(1)} %get-tuple-element.1789.kept_ref, f32[2,768,128]{2,1,0:T(8,128)S(1)} %get-tuple-element.1790.sums_ref, bf16[4,2,192,256]{3,2,1,0:T(8,128)(2,1)S(1)} %bitcast.166, f32[2,768,128]{2,1,0:T(8,128)S(1)} %copy-done.62, ...), custom_call_target="tpu_custom_call" | custom-call | tf_op jit(solution)/shard_map/pallas_call | solution.py:739
  507.4 13.1 %shard_map.242.second_ref.right_ref = bf16[1536,1024]{1,0:T(8,128)(2,1)S(1)} custom-call(bf16[1536,2048]{1,0:T(8,128)(2,1)} %get-tuple-element.1967.right_ref.left_ref, bf16[1024,2048]{1,0:T(8,128)(2,1)} %shard_map.240.right_ref, f32[1536,1024]{1,0:T(8,128)} %get-tuple-element.1838.slope_ref), custom_call_target="tpu_custom_call" | custom-call | tf_op jit(solution)/shard_map/pallas_call | solution.py:762
  545.8 23.6 %conditional.67 = (bf16[192,2048]{1,0:T(8,128)(2,1)}, bf16[192,2048]{1,0:T(8,128)(2,1)}, bf16[1024,512]{1,0:T(8,128)(2,1)}, bf16[512,1024]{1,0:T(8,128)(2,1)}, b...) conditional(s32[]{:T(128)} %bitcast.63, () %tuple.748, ...), branch_computations={%region_48.49_spmd, %region_49.52_spmd} | conditional | flops 7862528 | bytes 40115332 | solution.py:63
  571.7 31.8 %conditional.68 = (bf16[192,2048]{1,0:T(8,128)(2,1)}, bf16[192,2048]{1,0:T(8,128)(2,1)}, bf16[512,1024]{1,0:T(8,128)(2,1)}, f32[768,2048]{1,0:T(8,128)}, bf16[768,2048]{1,0:T(8,128)(2,1)}) conditional(s32[]{:T(128)} %bitcast.63, () %tuple.580, (f32[768,2048]{1,0:T(8,128)}, bf16[768,2048]{1,0:T(8,128)(2,1)}, bf16[192,2048]{1,0:T(8,128)(2,1)}, ...), branch_computations={%region_52.53_spmd, %region_53.54_spmd} | conditional | flops 1966080 | bytes 57409800 | solution.py:63
  609.9 43.6 %conditional.69 = (bf16[192,2048]{1,0:T(8,128)(2,1)}, bf16[192,2048]{1,0:T(8,128)(2,1)}, bf16[192,2048]{1,0:T(8,128)(2,1)S(1)}, bf16[192,2048]{1,0:T(8,128)(2,1)...) conditional(s32[]{:T(128)} %bitcast.63, () %tuple.761, ...), branch_computations={%region_54.55_spmd, %region_55.56_spmd} | conditional | flops 2359296 | bytes 23593216 | solution.py:63
  613.3 15.5 %collective-permute-done.34 = bf16[192,2048]{1,0:T(8,128)(2,1)} collective-permute-done((bf16[192,2048]{1,0:T(8,128)(2,1)S(1)}, bf16[192,2048]{1,0:T(8,128)(2,1)}, u32[]{:S(2)}, u32[]{:S(2)}) %collective-permute-start.34) | collective-permute-done | bytes 786464 | tf_op jit(solution)/shard_map/cond/branch_1_fun/ppermute | solution.py:27
  633.9 14.8 %collective-permute-done.35 = bf16[192,2048]{1,0:T(8,128)(2,1)} collective-permute-done((bf16[192,2048]{1,0:T(8,128)(2,1)S(1)}, bf16[192,2048]{1,0:T(8,128)(2,1)}, u32[]{:S(2)}, u32[]{:S(2)}) %collective-permute-start.35) | collective-permute-done | bytes 786464 | tf_op jit(solution)/shard_map/cond/branch_1_fun/ppermute | solution.py:27
  656.6 26.4 %conditional.70 = (bf16[1536,2048]{1,0:T(8,128)(2,1)S(1)}, bf16[512,1024]{1,0:T(8,128)(2,1)S(1)}) conditional(s32[]{:T(128)} %bitcast.63, () %tuple.770, (bf16[192,2048]{1,0:T(8,128)(2,1)}, bf16[192,2048]{1,0:T(8,128)(2,1)S(1)}, bf16[192,2048]{1,0:T(8,128)(2,1)}, bf16[192,2048]{1,0:T(8,128)(2,1)}, bf16[192,2048]{1,0:T(8,128)(2,1)}, ...), branch_computations={%region_56.57_spmd, %region_57.58_spmd} | conditional | bytes 15728832 | solution.py:63
  658.1 17.7 %collective-permute-done.19.refs_3_ = bf16[192,2048]{1,0:T(8,128)(2,1)S(1)} collective-permute-done((bf16[192,2048]{1,0:T(8,128)(2,1)}, bf16[192,2048]{1,0:T(8,128)(2,1)S(1)}, u32[]{:S(2)}, u32[]{:S(2)}) %collective-permute-start.19) | collective-permute-done | bytes 786464 | tf_op jit(solution)/shard_map/cond/branch_1_fun/ppermute | solution.py:27
  705.9 17.8 %shard_map.250 = bf16[4,2,192,768]{3,2,1,0:T(8,128)(2,1)} custom-call(s32[5]{0:T(128)S(1)} %copy-done.108, bf16[2,768,768]{2,1,0:T(8,128)(2,1)S(1)} %copy-done.4, f32[2,768,128]{2,1,0:T(8,128)S(1)} %copy-done.12, bf16[4,2,192,256]{3,2,1,0:T(8,128)(2,1)S(1)} %bitcast.165, f32[2,768,128]{2,1,0:T(8,128)S(1)} %copy-done.63, f32[2,768,128]{2,1,0:T(8,128)S(1)} %copy-done.67, ...), custom_call_target="tpu_custom_call" | custom-call | tf_op jit(solution)/shard_map/pallas_call | solution.py:739
  725.8 13.1 %shard_map.251.right_ref.second_ref = bf16[1536,1024]{1,0:T(8,128)(2,1)S(1)} custom-call(bf16[1536,2048]{1,0:T(8,128)(2,1)} %copy-done.24, bf16[1024,2048]{1,0:T(8,128)(2,1)} %shard_map.229.down_ref.right_ref, f32[1536,1024]{1,0:T(8,128)} %get-tuple-element.1990.slope_ref), custom_call_target="tpu_custom_call" | custom-call | tf_op jit(solution)/shard_map/pallas_call | solution.py:762
  817.4 23.3 %conditional.75 = (bf16[192,2048]{1,0:T(8,128)(2,1)}, bf16[192,2048]{1,0:T(8,128)(2,1)}, bf16[512,1024]{1,0:T(8,128)(2,1)}, f32[768]{0:T(1024)S(1)}, f32[1024]{0:T(1024)S(1)}) conditional(s32[]{:T(128)} %bitcast.63, () %tuple.831, (f32[768,2048]{1,0:T(8,128)}, bf16[768,2048]{1,0:T(8,128)(2,1)}, bf16[1536,2048]{1,0:T(8,128)(2,1)}, ...), branch_computations={%region_66.67_spmd, %region_67.70_spmd} | conditional | flops 7862528 | bytes 49552520 | solution.py:63
  847.8 33.5 %conditional.76 = (bf16[192,2048]{1,0:T(8,128)(2,1)}, bf16[192,2048]{1,0:T(8,128)(2,1)}, bf16[512,1024]{1,0:T(8,128)(2,1)}, bf16[1024,512]{1,0:T(8,128)(2,1)}, bf16[512,1024]{1,0:T(8,128)(2,1)}) conditional(s32[]{:T(128)} %bitcast.63, () %tuple.830, (f32[768,2048]{1,0:T(8,128)}, bf16[768,2048]{1,0:T(8,128)(2,1)}, bf16[192,2048]{1,0:T(8,128)(2,1)}, ...), branch_computations={%region_70.71_spmd, %region_71.72_spmd} | conditional | flops 1966080 | bytes 63701264 | solution.py:63
  867.7 13.6 %collective-permute-done.40 = bf16[192,2048]{1,0:T(8,128)(2,1)} collective-permute-done((bf16[192,2048]{1,0:T(8,128)(2,1)}, bf16[192,2048]{1,0:T(8,128)(2,1)}, u32[]{:S(2)}, u32[]{:S(2)}) %collective-permute-start.40) | collective-permute-done | bytes 786464 | tf_op jit(solution)/shard_map/cond/branch_1_fun/ppermute | solution.py:27
  (755 shorter events, 800.2 us)
Async XLA Ops:
  50.3 65.9 %collective-permute-start.56 = (bf16[512,1024]{1,0:T(8,128)(2,1)}, bf16[512,1024]{1,0:T(8,128)(2,1)}, u32[]{:S(2)}, u32[]{:S(2)}) collective-permute-start(bf16[512,1024]{1,0:T(8,128)(2,1)} %copy.72), channel_id=1, source_target_pairs={{0,4},{4,0},{8,12},{12,8},{16,20},{20,16},{24,28},{28,24},{1,5},{5... | collective-permute-start | bytes 3145736 | tf_op jit(solution)/shard_map/ppermute | solution.py:27
  54.3 61.9 %collective-permute-start.55 = (bf16[512,1024]{1,0:T(8,128)(2,1)}, bf16[512,1024]{1,0:T(8,128)(2,1)}, u32[]{:S(2)}, u32[]{:S(2)}) collective-permute-start(bf16[512,1024]{1,0:T(8,128)(2,1)} %copy.71), channel_id=1, source_target_pairs={{0,16},{4,20},{8,24},{12,28},{16,0},{20,4},{24,8},{28,12},{1,17},{... | collective-permute-start | bytes 3145736 | tf_op jit(solution)/shard_map/ppermute | solution.py:27
  116.2 48.5 %collective-permute-start.59 = (bf16[512,1024]{1,0:T(8,128)(2,1)}, bf16[512,1024]{1,0:T(8,128)(2,1)}, u32[]{:S(2)}, u32[]{:S(2)}) collective-permute-start(bf16[512,1024]{1,0:T(8,128)(2,1)} %copy-done.72), channel_id=1, source_target_pairs={{0,16},{4,20},{8,24},{12,28},{16,0},{20,4},{24,8},{28,12},{1,17},{... | collective-permute-start | bytes 3145736 | tf_op jit(solution)/shard_map/ppermute | solution.py:27
  116.7 48.6 %collective-permute-start.58 = (bf16[512,1024]{1,0:T(8,128)(2,1)}, bf16[512,1024]{1,0:T(8,128)(2,1)}, u32[]{:S(2)}, u32[]{:S(2)}) collective-permute-start(bf16[512,1024]{1,0:T(8,128)(2,1)} %copy-done.72), channel_id=1, source_target_pairs={{0,4},{4,0},{8,12},{12,8},{16,20},{20,16},{24,28},{28,24},{1,5},{5... | collective-permute-start | bytes 3145736 | tf_op jit(solution)/shard_map/ppermute | solution.py:27
  117.2 48.1 %collective-permute-start.57 = (bf16[512,1024]{1,0:T(8,128)(2,1)}, bf16[512,1024]{1,0:T(8,128)(2,1)}, u32[]{:S(2)}, u32[]{:S(2)}) collective-permute-start(bf16[512,1024]{1,0:T(8,128)(2,1)} %collective-permute-done.55.refs_1_), channel_id=1, source_target_pairs={{0,4},{4,0},{8,12},{12,8},{16,20},{20,16},{24,28},{28,24},{1,5},{5... | collective-permute-start | bytes 3145736 | tf_op jit(solution)/shard_map/ppermute | solution.py:27
  165.9 70.8 %collective-permute-start.61 = (bf16[1024,512]{1,0:T(8,128)(2,1)}, bf16[1024,512]{1,0:T(8,128)(2,1)}, u32[]{:S(2)}, u32[]{:S(2)}) collective-permute-start(bf16[1024,512]{1,0:T(8,128)(2,1)} %get-tuple-element.2700.refs_0_), channel_id=1, source_target_pairs={{0,16},{4,20},{8,24},{12,28},{16,0},{20,4},{24,8},{28,12},{1,17},{... | collective-permute-start | bytes 3145736 | tf_op jit(solution)/shard_map/ppermute | solution.py:27
  181.6 56.2 %collective-permute-start.64 = (bf16[1024,512]{1,0:T(8,128)(2,1)}, bf16[1024,512]{1,0:T(8,128)(2,1)}, u32[]{:S(2)}, u32[]{:S(2)}) collective-permute-start(bf16[1024,512]{1,0:T(8,128)(2,1)} %get-tuple-element.2700.refs_0_), channel_id=1, source_target_pairs={{0,4},{4,0},{8,12},{12,8},{16,20},{20,16},{24,28},{28,24},{1,5},{5... | collective-permute-start | bytes 3145736 | tf_op jit(solution)/shard_map/ppermute | solution.py:27
  257.9 57.1 %collective-permute-start.66 = (bf16[512,1024]{1,0:T(8,128)(2,1)}, bf16[512,1024]{1,0:T(8,128)(2,1)}, u32[]{:S(2)}, u32[]{:S(2)}) collective-permute-start(bf16[512,1024]{1,0:T(8,128)(2,1)} %copy.77), channel_id=1, source_target_pairs={{0,16},{4,20},{8,24},{12,28},{16,0},{20,4},{24,8},{28,12},{1,17},{... | collective-permute-start | bytes 3145736 | tf_op jit(solution)/shard_map/ppermute | solution.py:27
  268.7 47.6 %collective-permute-start.68 = (bf16[512,1024]{1,0:T(8,128)(2,1)}, bf16[512,1024]{1,0:T(8,128)(2,1)}, u32[]{:S(2)}, u32[]{:S(2)}) collective-permute-start(bf16[512,1024]{1,0:T(8,128)(2,1)} %copy.78), channel_id=1, source_target_pairs={{0,4},{4,0},{8,12},{12,8},{16,20},{20,16},{24,28},{28,24},{1,5},{5... | collective-permute-start | bytes 3145736 | tf_op jit(solution)/shard_map/ppermute | solution.py:27
  339.0 48.3 %collective-permute-start.71 = (bf16[512,1024]{1,0:T(8,128)(2,1)}, bf16[512,1024]{1,0:T(8,128)(2,1)}, u32[]{:S(2)}, u32[]{:S(2)}) collective-permute-start(bf16[512,1024]{1,0:T(8,128)(2,1)} %collective-permute-done.66), channel_id=1, source_target_pairs={{0,4},{4,0},{8,12},{12,8},{16,20},{20,16},{24,28},{28,24},{1,5},{5... | collective-permute-start | bytes 3145736 | tf_op jit(solution)/shard_map/ppermute | solution.py:27
  340.5 46.7 %collective-permute-start.70 = (bf16[512,1024]{1,0:T(8,128)(2,1)}, bf16[512,1024]{1,0:T(8,128)(2,1)}, u32[]{:S(2)}, u32[]{:S(2)}) collective-permute-start(bf16[512,1024]{1,0:T(8,128)(2,1)} %get-tuple-element.2704.refs_0_), channel_id=1, source_target_pairs={{0,4},{4,0},{8,12},{12,8},{16,20},{20,16},{24,28},{28,24},{1,5},{5... | collective-permute-start | bytes 3145736 | tf_op jit(solution)/shard_map/ppermute | solution.py:27
  341.0 46.7 %collective-permute-start.69 = (bf16[512,1024]{1,0:T(8,128)(2,1)}, bf16[512,1024]{1,0:T(8,128)(2,1)}, u32[]{:S(2)}, u32[]{:S(2)}) collective-permute-start(bf16[512,1024]{1,0:T(8,128)(2,1)} %get-tuple-element.2704.refs_0_), channel_id=1, source_target_pairs={{0,16},{4,20},{8,24},{12,28},{16,0},{20,4},{24,8},{28,12},{1,17},{... | collective-permute-start | bytes 3145736 | tf_op jit(solution)/shard_map/ppermute | solution.py:27
  387.7 48.7 %collective-permute-start.73 = (bf16[1024,512]{1,0:T(8,128)(2,1)}, bf16[1024,512]{1,0:T(8,128)(2,1)}, u32[]{:S(2)}, u32[]{:S(2)}) collective-permute-start(bf16[1024,512]{1,0:T(8,128)(2,1)} %copy-done.74), channel_id=1, source_target_pairs={{0,4},{4,0},{8,12},{12,8},{16,20},{20,16},{24,28},{28,24},{1,5},{5... | collective-permute-start | bytes 3145736 | tf_op jit(solution)/shard_map/ppermute | solution.py:27
  389.3 47.1 %collective-permute-start.72 = (bf16[512,1024]{1,0:T(8,128)(2,1)}, bf16[512,1024]{1,0:T(8,128)(2,1)}, u32[]{:S(2)}, u32[]{:S(2)}) collective-permute-start(bf16[512,1024]{1,0:T(8,128)(2,1)} %collective-permute-done.69.refs_1_), channel_id=1, source_target_pairs={{0,4},{4,0},{8,12},{12,8},{16,20},{20,16},{24,28},{28,24},{1,5},{5... | collective-permute-start | bytes 3145736 | tf_op jit(solution)/shard_map/ppermute | solution.py:27
  389.7 78.4 %collective-permute-start.74 = (bf16[1024,512]{1,0:T(8,128)(2,1)}, bf16[1024,512]{1,0:T(8,128)(2,1)}, u32[]{:S(2)}, u32[]{:S(2)}) collective-permute-start(bf16[1024,512]{1,0:T(8,128)(2,1)} %copy-done.74), channel_id=1, source_target_pairs={{0,16},{4,20},{8,24},{12,28},{16,0},{20,4},{24,8},{28,12},{1,17},{... | collective-permute-start | bytes 3145736 | tf_op jit(solution)/shard_map/ppermute | solution.py:27
  473.9 65.7 %collective-permute-start.76 = (bf16[1024,512]{1,0:T(8,128)(2,1)}, bf16[1024,512]{1,0:T(8,128)(2,1)}, u32[]{:S(2)}, u32[]{:S(2)}) collective-permute-start(bf16[1024,512]{1,0:T(8,128)(2,1)} %shard_map.237), channel_id=1, source_target_pairs={{0,4},{4,0},{8,12},{12,8},{16,20},{20,16},{24,28},{28,24},{1,5},{5... | collective-permute-start | bytes 3145736 | tf_op jit(solution)/shard_map/ppermute | solution.py:27
  506.3 63.1 %collective-permute-start.78 = (bf16[1024,512]{1,0:T(8,128)(2,1)}, bf16[1024,512]{1,0:T(8,128)(2,1)}, u32[]{:S(2)}, u32[]{:S(2)}) collective-permute-start(bf16[1024,512]{1,0:T(8,128)(2,1)} %shard_map.241), channel_id=1, source_target_pairs={{0,4},{4,0},{8,12},{12,8},{16,20},{20,16},{24,28},{28,24},{1,5},{5... | collective-permute-start | bytes 3145736 | tf_op jit(solution)/shard_map/ppermute | solution.py:27
  607.9 45.6 %collective-permute-start.80 = (bf16[512,1024]{1,0:T(8,128)(2,1)}, bf16[512,1024]{1,0:T(8,128)(2,1)}, u32[]{:S(2)}, u32[]{:S(2)}) collective-permute-start(bf16[512,1024]{1,0:T(8,128)(2,1)} %get-tuple-element.1937), channel_id=1, source_target_pairs={{0,4},{4,0},{8,12},{12,8},{16,20},{20,16},{24,28},{28,24},{1,5},{5... | collective-permute-start | bytes 3145736 | tf_op jit(solution)/shard_map/ppermute | solution.py:27
  609.0 75.9 %collective-permute-start.81 = (bf16[1024,512]{1,0:T(8,128)(2,1)}, bf16[1024,512]{1,0:T(8,128)(2,1)}, u32[]{:S(2)}, u32[]{:S(2)}) collective-permute-start(bf16[1024,512]{1,0:T(8,128)(2,1)} %get-tuple-element.1952), channel_id=1, source_target_pairs={{0,16},{4,20},{8,24},{12,28},{16,0},{20,4},{24,8},{28,12},{1,17},{... | collective-permute-start | bytes 3145736 | tf_op jit(solution)/shard_map/ppermute | solution.py:27
  653.5 72.3 %collective-permute-start.85 = (bf16[512,1024]{1,0:T(8,128)(2,1)}, bf16[512,1024]{1,0:T(8,128)(2,1)}, u32[]{:S(2)}, u32[]{:S(2)}) collective-permute-start(bf16[512,1024]{1,0:T(8,128)(2,1)} %get-tuple-element.1978), channel_id=1, source_target_pairs={{0,16},{4,20},{8,24},{12,28},{16,0},{20,4},{24,8},{28,12},{1,17},{... | collective-permute-start | bytes 3145736 | tf_op jit(solution)/shard_map/ppermute | solution.py:27
  655.5 70.3 %collective-permute-start.86 = (bf16[512,1024]{1,0:T(8,128)(2,1)}, bf16[512,1024]{1,0:T(8,128)(2,1)}, u32[]{:S(2)}, u32[]{:S(2)}) collective-permute-start(bf16[512,1024]{1,0:T(8,128)(2,1)} %get-tuple-element.1986), channel_id=1, source_target_pairs={{0,4},{4,0},{8,12},{12,8},{16,20},{20,16},{24,28},{28,24},{1,5},{5... | collective-permute-start | bytes 3145736 | tf_op jit(solution)/shard_map/ppermute | solution.py:27
  684.0 72.9 %collective-permute-start.83 = (bf16[512,1024]{1,0:T(8,128)(2,1)}, bf16[512,1024]{1,0:T(8,128)(2,1)}, u32[]{:S(2)}, u32[]{:S(2)}) collective-permute-start(bf16[512,1024]{1,0:T(8,128)(2,1)} %copy-done.89), channel_id=1, source_target_pairs={{0,16},{4,20},{8,24},{12,28},{16,0},{20,4},{24,8},{28,12},{1,17},{... | collective-permute-start | bytes 3145736 | tf_op jit(solution)/shard_map/ppermute | solution.py:27
  691.4 66.7 %collective-permute-start.82 = (bf16[1024,512]{1,0:T(8,128)(2,1)}, bf16[1024,512]{1,0:T(8,128)(2,1)}, u32[]{:S(2)}, u32[]{:S(2)}) collective-permute-start(bf16[1024,512]{1,0:T(8,128)(2,1)} %shard_map.247), channel_id=1, source_target_pairs={{0,4},{4,0},{8,12},{12,8},{16,20},{20,16},{24,28},{28,24},{1,5},{5... | collective-permute-start | bytes 3145736 | tf_op jit(solution)/shard_map/ppermute | solution.py:27
  699.7 56.3 %collective-permute-start.84 = (bf16[192,2048]{1,0:T(8,128)(2,1)}, bf16[192,2048]{1,0:T(8,128)(2,1)S(1)}, u32[]{:S(2)}, u32[]{:S(2)}) collective-permute-start(bf16[192,2048]{1,0:T(8,128)(2,1)} %get-tuple-element.2708), channel_id=1, source_target_pairs={{0,8},{4,12},{8,0},{12,4},{16,24},{20,28},{24,16},{28,20},{1,9},{5... | collective-permute-start | bytes 2359304 | tf_op jit(solution)/shard_map/ppermute | solution.py:27
  763.4 48.4 %collective-permute-start.90 = (bf16[1024,512]{1,0:T(8,128)(2,1)}, bf16[1024,512]{1,0:T(8,128)(2,1)}, u32[]{:S(2)}, u32[]{:S(2)}) collective-permute-start(bf16[1024,512]{1,0:T(8,128)(2,1)} %shard_map.255), channel_id=1, source_target_pairs={{0,16},{4,20},{8,24},{12,28},{16,0},{20,4},{24,8},{28,12},{1,17},{... | collective-permute-start | bytes 3145736 | tf_op jit(solution)/shard_map/ppermute | solution.py:27
  789.3 55.2 %collective-permute-start.92 = (bf16[1024,512]{1,0:T(8,128)(2,1)}, bf16[1024,512]{1,0:T(8,128)(2,1)}, u32[]{:S(2)}, u32[]{:S(2)}) collective-permute-start(bf16[1024,512]{1,0:T(8,128)(2,1)} %shard_map.258), channel_id=1, source_target_pairs={{0,4},{4,0},{8,12},{12,8},{16,20},{20,16},{24,28},{28,24},{1,5},{5... | collective-permute-start | bytes 3145736 | tf_op jit(solution)/shard_map/ppermute | solution.py:27
  792.8 47.9 %collective-permute-start.93 = (bf16[1024,256]{1,0:T(8,128)(2,1)}, bf16[1024,256]{1,0:T(8,128)(2,1)}, u32[]{:S(2)}, u32[]{:S(2)}) collective-permute-start(bf16[1024,256]{1,0:T(8,128)(2,1)} %get-tuple-element.2101), channel_id=1, source_target_pairs={{0,8},{4,12},{8,0},{12,4},{16,24},{20,28},{24,16},{28,20},{1,9},{5... | collective-permute-start | bytes 1572872 | tf_op jit(solution)/shard_map/ppermute | solution.py:27
  815.5 73.1 %collective-permute-start.94 = (bf16[512,1024]{1,0:T(8,128)(2,1)}, bf16[512,1024]{1,0:T(8,128)(2,1)}, u32[]{:S(2)}, u32[]{:S(2)}) collective-permute-start(bf16[512,1024]{1,0:T(8,128)(2,1)} %shard_map.259), channel_id=1, source_target_pairs={{0,16},{4,20},{8,24},{12,28},{16,0},{20,4},{24,8},{28,12},{1,17},{... | collective-permute-start | bytes 3145736 | tf_op jit(solution)/shard_map/ppermute | solution.py:27
  847.0 45.7 %collective-permute-start.96 = (bf16[512,1024]{1,0:T(8,128)(2,1)}, bf16[512,1024]{1,0:T(8,128)(2,1)}, u32[]{:S(2)}, u32[]{:S(2)}) collective-permute-start(bf16[512,1024]{1,0:T(8,128)(2,1)} %get-tuple-element.2157), channel_id=1, source_target_pairs={{0,4},{4,0},{8,12},{12,8},{16,20},{20,16},{24,28},{28,24},{1,5},{5... | collective-permute-start | bytes 3145736 | tf_op jit(solution)/shard_map/ppermute | solution.py:27
  892.7 65.9 %collective-permute-start.100 = (bf16[512,1024]{1,0:T(8,128)(2,1)}, bf16[512,1024]{1,0:T(8,128)(2,1)S(1)}, u32[]{:S(2)}, u32[]{:S(2)}) collective-permute-start(bf16[512,1024]{1,0:T(8,128)(2,1)} %get-tuple-element.2243), channel_id=1, source_target_pairs={{0,16},{4,20},{8,24},{12,28},{16,0},{20,4},{24,8},{28,12},{1,17},{... | collective-permute-start | bytes 3145736 | tf_op jit(solution)/shard_map/ppermute | solution.py:27
  902.1 44.7 %collective-permute-start.97 = (bf16[1024,256]{1,0:T(8,128)(2,1)}, bf16[1024,256]{1,0:T(8,128)(2,1)}, u32[]{:S(2)}, u32[]{:S(2)}) collective-permute-start(bf16[1024,256]{1,0:T(8,128)(2,1)} %get-tuple-element.2213), channel_id=1, source_target_pairs={{0,8},{4,12},{8,0},{12,4},{16,24},{20,28},{24,16},{28,20},{1,9},{5... | collective-permute-start | bytes 1572872 | tf_op jit(solution)/shard_map/ppermute | solution.py:27
  910.8 54.9 %collective-permute-start.99 = (bf16[256,1024]{1,0:T(8,128)(2,1)}, bf16[256,1024]{1,0:T(8,128)(2,1)}, u32[]{:S(2)}, u32[]{:S(2)}) collective-permute-start(bf16[256,1024]{1,0:T(8,128)(2,1)} %get-tuple-element.2241), channel_id=1, source_target_pairs={{0,8},{4,12},{8,0},{12,4},{16,24},{20,28},{24,16},{28,20},{1,9},{5... | collective-permute-start | bytes 1572872 | tf_op jit(solution)/shard_map/ppermute | solution.py:27
  (199 other events, 2386.2 us)

commit v5 on v4

--- a/solution.py
+++ b/solution.py
@@ -1215,6 +1215,7 @@
     u0 = paired(0, 1, moving[1])
     m0.near()
     m0.far()
+    sent = seq.run(lambda value: take_down(0, 1 - mid, value), down_weight, apart=True)
     each, proj_each, up_each = norm_gain.shape[1], proj_bias.shape[3], up_bias.shape[2]
 
     def unpack(everyone):
@@ -1263,58 +1264,69 @@
     stream, own = seq.run(
         lambda value: norm_first(value, order, gains[0], biases[0]), tokens_in
     )
-    tokens = Gather(seq, own, make_tables)
-    token_parts, tables = tokens.parts, tokens.beside
+    mid_rows, across = seq.start(own, "dp", MID), seq.start(own, "tensor", 1)
+    moving = seq.start(sent, "dp", MID)
+    tables = seq.run(make_tables, apart=True)
+    across = seq.wait(across)
     m0.near_wait()
     m0.far_wait()
+    m0.last()
     u0.far()
-    m0.last()
+    core_parts = seq.settle(
+        lambda *values: tuple(swap(value, "tensor", 0) for value in values), own, across
+    )
     u0.near()
-    sent = seq.run(lambda value: take_down(0, 1 - mid, value), down_weight, apart=True)
-
-    def with_half(sent, own, mid, across, core_own, core_across):
-        received, both = swap(sent, "dp", MID), swap(mid, "tensor", 1)
-        received, both, mid = lax.optimization_barrier((received, both, mid))
-        core_mid, core_both = swap(mid, "tensor", 0), swap(both, "tensor", 0)
+    token_parts = (own, seq.wait(mid_rows), across, *core_parts)
+
+    def finish_first(own, mid, across, core_own, core_across):
+        both = swap(mid, "tensor", 1)
+        both, mid = lax.optimization_barrier((both, mid))
+        core_both = swap(both, "tensor", 0)
+        core_both, mid = lax.optimization_barrier((core_both, mid))
+        core_mid = swap(mid, "tensor", 0)
         parts = (own, mid, across, both, core_own, core_mid, core_across, core_both)
-        return received, assemble(parts, 0)
-
-    received, normed = seq.settle(with_half, sent, *token_parts)
+        return assemble(parts, 0)
+
+    normed = seq.settle(finish_first, *token_parts)
+    received = seq.wait(moving)
+    seq.tick(7)
     d0 = joined(0, 2, received)
+    m0.last_wait()
     u0.far_wait()
-    seq.tick(3)
+    seq.tick(1)
     u0.near_wait()
-    m0.last_wait()
     u0.last()
     d0.far()
+    d0.near()
     mixed_full = m0.whole()
     mixed = mix(0, normed, mixed_full)
-    d0.near()
-    moving = [set_out(1, 0), set_out(1, 1)]
     attended, kept, sums = attend(mixed)
     u0.last_wait()
+    seq.tick(1)
     up_full = u0.whole()
     hidden, slope = hide(0, normed, up_full)
-    m1 = paired(1, 0, moving[0])
-    u1 = paired(1, 1, moving[1])
     d0.far_wait()
     seq.tick(3)
     d0.near_wait()
     d0.last()
-    cot_mid = seq.swap(cot, "dp", MID)
+    m1 = paired(1, 0, set_out(1, 0))
     m1.far()
+    moving = set_out(1, 1)
+    cot_mid = seq.start(cot, "dp", MID)
     d0.last_wait()
     down_full = d0.whole()
     m1.near()
-    moving = [set_out(1, 2)]
     saved = [(normed, kept, sums, slope, attended, hidden)]
     weights = [(mixed_full, up_full, down_full)]
     streams = [stream]
 
     branch = Scatter(seq, out_product, (attended, hidden, mixed_full, down_full), rows)
     branch.begin()
+    u1 = paired(1, 1, moving)
+    moving = set_out(1, 2)
     branch.second()
-    d1 = paired(1, 2, moving[0])
+    cot_mid = seq.wait(cot_mid)
+    d1 = paired(1, 2, moving)
     m1.far_wait()
     seq.tick(2)
     m1.near_wait()

time: 1000 us -> 986 us (0.986)
    unnamed x205 -> x207, local copies, waits for them, and re-layouts: 24.5 us -> 19.6 us
  transfers between devices with their start and end apart: 102 -> 102, of which waited for: 47 -> 52; matrix products, arithmetic and copies ran while one was open for 10% -> 10% of each run, Pallas kernels for 41% -> 41%
where the time goes in v5:
time: 986 us; the launch traced here: 975 us
  Pallas kernels  406 us (41%)
  waiting for transfers between devices  325 us (33%)
  starting transfers between devices  97 us (10%)
  local copies, waits for them, and re-layouts  88.7 us (9%)
  other arithmetic  51.2 us (5%)
    ppermute x102, waiting for transfers between devices, swap(): return lax.ppermute(value, axis, [(i, i ^ 1 << bit) for i in range(size)])  325 us
    pallas_call x42, Pallas kernels, call(): pl.pallas_call(kernel, grid_spec=pltpu.PrefetchScalarGridSpec(num_scalar_...  278 us
    ppermute x102, starting transfers between devices, swap(): return lax.ppermute(value, axis, [(i, i ^ 1 << bit) for i in range(size)])  97 us
    pallas_call x2, Pallas kernels, attention_backward(): pl.pallas_call(attention_back_kernel, grid_spec=pltpu.PrefetchScalarGridS...  35.7 us
    pallas_call x10, Pallas kernels, assemble(): pl.pallas_call(partial(assemble_kernel, axis, window), in_specs=[pl.Block...  27.6 us
    pallas_call x2, Pallas kernels, attention_forward(): pl.pallas_call(attention_kernel, grid_spec=pltpu.PrefetchScalarGridSpec(n...  23.3 us
  transfers between devices with their start and end apart: 102, of which 52 were waited for; matrix products, arithmetic and copies ran while one was open for 10% of the time, Pallas kernels for 41%

profile of v5, /device:TPU:0, one launch (start us, length us, event | category | flops | bytes accessed | tf_op | source)
XLA Modules:
  0.0 975.1 jit_solution(5213845331872451692)
XLA Ops:
  13.5 19.4 %conditional.45 = (bf16[2,1412]{1,0:T(2,128)(2,1)S(1)}, bf16[192,2048]{1,0:T(8,128)(2,1)}) conditional(s32[]{:T(128)} %bitcast.63, () %tuple.588, (s32[]{:T(128)}, bf16[1,1412]{1,0:T(2,128)(2,1)S(1)}, bf16[192,2048]{1,0:T(8,128)(2,1)}) %tuple.600), branch_computations={%region_4.0_spmd, %region_5.6_spmd} | conditional | flops 14121 | bytes 3179722 | solution.py:63
  17.0 13.4 %collective-permute-done.23 = bf16[1,1412]{1,0:T(2,128)(2,1)S(1)} collective-permute-done((bf16[1,1412]{1,0:T(2,128)(2,1)S(1)}, bf16[1,1412]{1,0:T(2,128)(2,1)S(1)}, u32[]{:S(2)}, u32[]{:S(2)}) %collective-permute-start.23) | collective-permute-done | bytes 2856 | tf_op jit(solution)/shard_map/cond/branch_1_fun/ppermute | solution.py:27
  112.6 26.4 %conditional.53 = (bf16[1536,2048]{1,0:T(8,128)(2,1)}) conditional(s32[]{:T(128)} %bitcast.63, () %tuple.624, (bf16[192,2048]{1,0:T(8,128)(2,1)}, bf16[192,2048]{1,0:T(8,128)(2,1)}, bf16[192,2048]{1,0:T(8,128)(2,1)}, bf16[192,2048]{1,0:T(8,128)(2,1)}, bf16[192,2048]{1,0:T(8,128)(2,1)}) %tuple.643), branch_computations={%region_20.21_spmd, %region_21.22_spmd} | conditional | bytes 9437312 | solution.py:63
  113.4 16.9 %collective-permute-done.2.refs_3_ = bf16[192,2048]{1,0:T(8,128)(2,1)S(1)} collective-permute-done((bf16[192,2048]{1,0:T(8,128)(2,1)}, bf16[192,2048]{1,0:T(8,128)(2,1)S(1)}, u32[]{:S(2)}, u32[]{:S(2)}) %collective-permute-start.2) | collective-permute-done | bytes 786464 | tf_op jit(solution)/shard_map/cond/branch_1_fun/ppermute | solution.py:27
  185.1 14.4 %shard_map.229 = (bf16[1536,1024]{1,0:T(8,128)(2,1)}, f32[1536,1024]{1,0:T(8,128)}) custom-call(bf16[1536,2048]{1,0:T(8,128)(2,1)} %get-tuple-element.2680.left_ref.normed_ref, bf16[2048,1024]{1,0:T(8,128)(2,1)S(1)} %shard_map.228.right_ref.up_ref, f32[1,1024]{1,0:T(1,128)S(1)} %get-tuple-element.1608.shift_ref), custom_call_target="tpu_custom_call" | custom-call | tf_op jit(solution)/shard_map/pallas_call | solution.py:762
  208.9 12.8 %collective-permute-done.63 = bf16[256,1024]{0,1:T(8,128)(2,1)} collective-permute-done((bf16[256,1024]{0,1:T(8,128)(2,1)}, bf16[256,1024]{0,1:T(8,128)(2,1)}, u32[]{:S(2)}, u32[]{:S(2)}) %collective-permute-start.63) | collective-permute-done | bytes 524320 | tf_op jit(solution)/shard_map/ppermute | solution.py:27
  267.2 22.6 %conditional.61 = (bf16[192,2048]{1,0:T(8,128)(2,1)S(1)}, bf16[192,2048]{1,0:T(8,128)(2,1)}) conditional(s32[]{:T(128)} %bitcast.63, () %tuple.691, (f32[768,2048]{1,0:T(8,128)}, bf16[768,2048]{1,0:T(8,128)(2,1)}) %tuple.701), branch_computations={%region_36.37_spmd, %region_37.38_spmd} | conditional | flops 2359296 | bytes 9437240 | solution.py:63
  271.5 18.3 %collective-permute-done.27 = bf16[192,2048]{1,0:T(8,128)(2,1)} collective-permute-done((bf16[192,2048]{1,0:T(8,128)(2,1)S(1)}, bf16[192,2048]{1,0:T(8,128)(2,1)}, u32[]{:S(2)}, u32[]{:S(2)}) %collective-permute-start.27) | collective-permute-done | bytes 786464 | tf_op jit(solution)/shard_map/cond/branch_1_fun/ppermute | solution.py:27
  298.4 19.8 %conditional.63 = (bf16[192,2048]{1,0:T(8,128)(2,1)}, bf16[192,2048]{1,0:T(8,128)(2,1)}) conditional(s32[]{:T(128)} %bitcast.63, () %tuple.690, (f32[768,2048]{1,0:T(8,128)}, bf16[768,2048]{1,0:T(8,128)(2,1)}, bf16[192,2048]{1,0:T(8,128)(2,1)}, bf16[192,2048]{1,0:T(8,128)(2,1)S(1)}) %tuple.712), branch_computations={%region_40.41_spmd, %region_41.42_spmd} | conditional | flops 1966080 | bytes 10223712 | solution.py:63
  302.5 15.6 %collective-permute-done.28 = bf16[192,2048]{1,0:T(8,128)(2,1)} collective-permute-done((bf16[192,2048]{1,0:T(8,128)(2,1)S(1)}, bf16[192,2048]{1,0:T(8,128)(2,1)}, u32[]{:S(2)}, u32[]{:S(2)}) %collective-permute-start.28) | collective-permute-done | bytes 786464 | tf_op jit(solution)/shard_map/cond/branch_1_fun/ppermute | solution.py:27
  325.9 39.8 %conditional.64 = (bf16[192,2048]{1,0:T(8,128)(2,1)S(1)}, bf16[192,2048]{1,0:T(8,128)(2,1)}, bf16[192,2048]{1,0:T(8,128)(2,1)}, bf16[192,2048]{1,0:T(8,128)(2,1)...) conditional(s32[]{:T(128)} %bitcast.63, () %tuple.622, ...), branch_computations={%region_42.43_spmd, %region_43.44_spmd} | conditional | bytes 23593304 | solution.py:63
  327.9 15.8 %collective-permute-done.7 = bf16[192,2048]{1,0:T(8,128)(2,1)} collective-permute-done((bf16[192,2048]{1,0:T(8,128)(2,1)S(1)}, bf16[192,2048]{1,0:T(8,128)(2,1)}, u32[]{:S(2)}, u32[]{:S(2)}) %collective-permute-start.7) | collective-permute-done | bytes 786464 | tf_op jit(solution)/shard_map/cond/branch_1_fun/ppermute | solution.py:27
  345.2 13.0 %collective-permute-done.6 = bf16[192,2048]{1,0:T(8,128)(2,1)} collective-permute-done((bf16[192,2048]{1,0:T(8,128)(2,1)S(1)}, bf16[192,2048]{1,0:T(8,128)(2,1)}, u32[]{:S(2)}, u32[]{:S(2)}) %collective-permute-start.6) | collective-permute-done | bytes 786464 | tf_op jit(solution)/shard_map/cond/branch_1_fun/ppermute | solution.py:27
  370.8 32.4 %conditional.65 = (bf16[1536,2048]{1,0:T(8,128)(2,1)S(1)}, bf16[1536,2048]{1,0:T(8,128)(2,1)S(1)}, bf16[2048,1024]{1,0:T(8,128)(2,1)S(1)}) conditional(s32[]{:T(128)} %bitcast.63, () %tuple.621, (bf16[192,2048]{1,0:T(8,128)(2,1)}, bf16[192,2048]{1,0:T(8,128)(2,1)}, bf16[192,2048]{1,0:T(8,128)(2,1)}, bf16[192,2048]{1,0:T(8,128)(2,1)}, ...), branch_computations={%region_44.45_spmd, %region_45.46_spmd} | conditional | bytes 44040640 | solution.py:63
  417.1 12.0 %shard_map.236 = (bf16[4,2,192,256]{3,2,1,0:T(8,128)(2,1)}, bf16[2,768,768]{2,1,0:T(8,128)(2,1)S(1)}, f32[2,768,128]{2,1,0:T(8,128)S(1)}) custom-call(s32[5]{0:T(128)S(1)} %copy-done.106, f32[4,2,192,768]{3,2,1,0:T(8,128)S(1)} %bitcast.166, f32[2,768,128]{2,1,0:T(8,128)S(1)} %copy-done.53, f32[2,768,128]{2,1,0:T(8,128)S(1)} %copy-done.58, ...), custom_call_target="tpu_custom_call" | custom-call | tf_op jit(solution)/shard_map/pallas_call | solution.py:712
  434.1 14.5 %shard_map.238 = (bf16[1536,1024]{1,0:T(8,128)(2,1)}, f32[1536,1024]{1,0:T(8,128)}) custom-call(bf16[1536,2048]{1,0:T(8,128)(2,1)S(1)} %bitcast.171, bf16[2048,1024]{1,0:T(8,128)(2,1)} %shard_map.237.right_ref.up_ref, f32[1,1024]{1,0:T(1,128)S(1)} %get-tuple-element.1800.shift_ref), custom_call_target="tpu_custom_call" | custom-call | tf_op jit(solution)/shard_map/pallas_call | solution.py:762
  461.0 18.5 %shard_map.241 = bf16[4,2,192,768]{3,2,1,0:T(8,128)(2,1)} custom-call(s32[5]{0:T(128)S(1)} %copy-done.106, bf16[2,768,768]{2,1,0:T(8,128)(2,1)S(1)} %get-tuple-element.1784.kept_ref, f32[2,768,128]{2,1,0:T(8,128)S(1)} %get-tuple-element.1785.sums_ref, bf16[4,2,192,256]{3,2,1,0:T(8,128)(2,1)S(1)} %bitcast.169, f32[2,768,128]{2,1,0:T(8,128)S(1)} %copy-done.54, ...), custom_call_target="tpu_custom_call" | custom-call | tf_op jit(solution)/shard_map/pallas_call | solution.py:739
  489.7 12.7 %shard_map.244.second_ref.right_ref = bf16[1536,1024]{1,0:T(8,128)(2,1)} custom-call(bf16[1536,2048]{1,0:T(8,128)(2,1)S(1)} %bitcast.183, bf16[1024,2048]{1,0:T(8,128)(2,1)} %shard_map.242.right_ref, f32[1536,1024]{1,0:T(8,128)} %get-tuple-element.1833.slope_ref), custom_call_target="tpu_custom_call" | custom-call | tf_op jit(solution)/shard_map/pallas_call | solution.py:762
  526.8 26.9 %conditional.67 = (bf16[192,2048]{1,0:T(8,128)(2,1)}, bf16[192,2048]{1,0:T(8,128)(2,1)}, bf16[1024,512]{1,0:T(8,128)(2,1)}, bf16[512,1024]{1,0:T(8,128)(2,1)}, b...) conditional(s32[]{:T(128)} %bitcast.63, () %tuple.756, ...), branch_computations={%region_48.49_spmd, %region_49.52_spmd} | conditional | flops 7862528 | bytes 81009896 | solution.py:63
  556.5 30.5 %conditional.68 = (bf16[192,2048]{1,0:T(8,128)(2,1)}, bf16[192,2048]{1,0:T(8,128)(2,1)}, bf16[512,1024]{1,0:T(8,128)(2,1)}, f32[768,2048]{1,0:T(8,128)}, bf16[768,2048]{1,0:T(8,128)(2,1)}) conditional(s32[]{:T(128)} %bitcast.63, () %tuple.584, (f32[768,2048]{1,0:T(8,128)}, bf16[768,2048]{1,0:T(8,128)(2,1)}, bf16[192,2048]{1,0:T(8,128)(2,1)}, ...), branch_computations={%region_52.53_spmd, %region_53.54_spmd} | conditional | flops 1966080 | bytes 54264044 | solution.py:63
  594.1 43.6 %conditional.69 = (bf16[192,2048]{1,0:T(8,128)(2,1)}, bf16[192,2048]{1,0:T(8,128)(2,1)}, bf16[192,2048]{1,0:T(8,128)(2,1)S(1)}, bf16[192,2048]{1,0:T(8,128)(2,1)...) conditional(s32[]{:T(128)} %bitcast.63, () %tuple.769, ...), branch_computations={%region_54.55_spmd, %region_55.56_spmd} | conditional | flops 2359296 | bytes 23593216 | solution.py:63
  595.7 17.1 %collective-permute-done.34 = bf16[192,2048]{1,0:T(8,128)(2,1)} collective-permute-done((bf16[192,2048]{1,0:T(8,128)(2,1)S(1)}, bf16[192,2048]{1,0:T(8,128)(2,1)}, u32[]{:S(2)}, u32[]{:S(2)}) %collective-permute-start.34) | collective-permute-done | bytes 786464 | tf_op jit(solution)/shard_map/cond/branch_1_fun/ppermute | solution.py:27
  617.4 15.5 %collective-permute-done.35 = bf16[192,2048]{1,0:T(8,128)(2,1)} collective-permute-done((bf16[192,2048]{1,0:T(8,128)(2,1)S(1)}, bf16[192,2048]{1,0:T(8,128)(2,1)}, u32[]{:S(2)}, u32[]{:S(2)}) %collective-permute-start.35) | collective-permute-done | bytes 786464 | tf_op jit(solution)/shard_map/cond/branch_1_fun/ppermute | solution.py:27
  641.2 26.4 %conditional.70 = (bf16[1536,2048]{1,0:T(8,128)(2,1)S(1)}, bf16[512,1024]{1,0:T(8,128)(2,1)S(1)}) conditional(s32[]{:T(128)} %bitcast.63, () %tuple.778, (bf16[192,2048]{1,0:T(8,128)(2,1)}, bf16[192,2048]{1,0:T(8,128)(2,1)S(1)}, bf16[192,2048]{1,0:T(8,128)(2,1)}, bf16[192,2048]{1,0:T(8,128)(2,1)}, bf16[192,2048]{1,0:T(8,128)(2,1)}, ...), branch_computations={%region_56.57_spmd, %region_57.58_spmd} | conditional | bytes 15728832 | solution.py:63
  642.2 18.3 %collective-permute-done.19.refs_3_ = bf16[192,2048]{1,0:T(8,128)(2,1)S(1)} collective-permute-done((bf16[192,2048]{1,0:T(8,128)(2,1)}, bf16[192,2048]{1,0:T(8,128)(2,1)S(1)}, u32[]{:S(2)}, u32[]{:S(2)}) %collective-permute-start.19) | collective-permute-done | bytes 786464 | tf_op jit(solution)/shard_map/cond/branch_1_fun/ppermute | solution.py:27
  689.7 17.2 %shard_map.252 = bf16[4,2,192,768]{3,2,1,0:T(8,128)(2,1)} custom-call(s32[5]{0:T(128)S(1)} %copy-done.106, bf16[2,768,768]{2,1,0:T(8,128)(2,1)S(1)} %copy-done.2, f32[2,768,128]{2,1,0:T(8,128)S(1)} %copy-done.10, bf16[4,2,192,256]{3,2,1,0:T(8,128)(2,1)S(1)} %bitcast.168, f32[2,768,128]{2,1,0:T(8,128)S(1)} %copy-done.55, f32[2,768,128]{2,1,0:T(8,128)S(1)} %copy-done.59, ...), custom_call_target="tpu_custom_call" | custom-call | tf_op jit(solution)/shard_map/pallas_call | solution.py:739
  710.0 13.1 %shard_map.253.right_ref.second_ref = bf16[1536,1024]{1,0:T(8,128)(2,1)S(1)} custom-call(bf16[1536,2048]{1,0:T(8,128)(2,1)} %copy-done.21, bf16[1024,2048]{1,0:T(8,128)(2,1)} %shard_map.231.down_ref.right_ref, f32[1536,1024]{1,0:T(8,128)} %get-tuple-element.1985.slope_ref), custom_call_target="tpu_custom_call" | custom-call | tf_op jit(solution)/shard_map/pallas_call | solution.py:762
  801.9 24.1 %conditional.75 = (bf16[192,2048]{1,0:T(8,128)(2,1)}, bf16[192,2048]{1,0:T(8,128)(2,1)}, bf16[512,1024]{1,0:T(8,128)(2,1)}, f32[768]{0:T(1024)S(1)}, f32[1024]{0:T(1024)S(1)}) conditional(s32[]{:T(128)} %bitcast.63, () %tuple.839, (f32[768,2048]{1,0:T(8,128)}, bf16[768,2048]{1,0:T(8,128)(2,1)}, bf16[1536,2048]{1,0:T(8,128)(2,1)}, ...), branch_computations={%region_66.67_spmd, %region_67.70_spmd} | conditional | flops 7862528 | bytes 49552520 | solution.py:63
  813.0 12.9 %collective-permute-done.39 = bf16[192,2048]{1,0:T(8,128)(2,1)} collective-permute-done((bf16[192,2048]{1,0:T(8,128)(2,1)}, bf16[192,2048]{1,0:T(8,128)(2,1)}, u32[]{:S(2)}, u32[]{:S(2)}) %collective-permute-start.39) | collective-permute-done | bytes 786464 | tf_op jit(solution)/shard_map/cond/branch_1_fun/ppermute | solution.py:27
  833.0 32.7 %conditional.76 = (bf16[192,2048]{1,0:T(8,128)(2,1)}, bf16[192,2048]{1,0:T(8,128)(2,1)}, bf16[512,1024]{1,0:T(8,128)(2,1)}, bf16[1024,512]{1,0:T(8,128)(2,1)}, bf16[512,1024]{1,0:T(8,128)(2,1)}) conditional(s32[]{:T(128)} %bitcast.63, () %tuple.838, (f32[768,2048]{1,0:T(8,128)}, bf16[768,2048]{1,0:T(8,128)(2,1)}, bf16[192,2048]{1,0:T(8,128)(2,1)}, ...), branch_computations={%region_70.71_spmd, %region_71.72_spmd} | conditional | flops 1966080 | bytes 60555508 | solution.py:63
  853.0 12.7 %collective-permute-done.40 = bf16[192,2048]{1,0:T(8,128)(2,1)} collective-permute-done((bf16[192,2048]{1,0:T(8,128)(2,1)}, bf16[192,2048]{1,0:T(8,128)(2,1)}, u32[]{:S(2)}, u32[]{:S(2)}) %collective-permute-start.40) | collective-permute-done | bytes 786464 | tf_op jit(solution)/shard_map/cond/branch_1_fun/ppermute | solution.py:27
  919.3 12.4 %collective-permute-done.97.other_ref = bf16[1024,256]{1,0:T(8,128)(2,1)} collective-permute-done((bf16[1024,256]{1,0:T(8,128)(2,1)}, bf16[1024,256]{1,0:T(8,128)(2,1)}, u32[]{:S(2)}, u32[]{:S(2)}) %collective-permute-start.97) | collective-permute-done | bytes 524320 | tf_op jit(solution)/shard_map/ppermute | solution.py:27
  (764 shorter events, 805.6 us)
Async XLA Ops:
  72.0 67.0 %collective-permute-start.56 = (bf16[1024,256]{1,0:T(8,128)(2,1)}, bf16[1024,256]{1,0:T(8,128)(2,1)}, u32[]{:S(2)}, u32[]{:S(2)}) collective-permute-start(bf16[1024,256]{1,0:T(8,128)(2,1)} %copy-done.90), channel_id=1, source_target_pairs={{0,8},{4,12},{8,0},{12,4},{16,24},{20,28},{24,16},{28,20},{1,9},{5... | collective-permute-start | bytes 1572872 | tf_op jit(solution)/shard_map/ppermute | solution.py:27
  98.4 45.0 %collective-permute-start.55 = (bf16[512,1024]{1,0:T(8,128)(2,1)}, bf16[512,1024]{1,0:T(8,128)(2,1)}, u32[]{:S(2)}, u32[]{:S(2)}) collective-permute-start(bf16[512,1024]{1,0:T(8,128)(2,1)} %collective-permute-done.53.refs_1_), channel_id=1, source_target_pairs={{0,4},{4,0},{8,12},{12,8},{16,20},{20,16},{24,28},{28,24},{1,5},{5... | collective-permute-start | bytes 3145736 | tf_op jit(solution)/shard_map/ppermute | solution.py:27
  102.6 48.9 %collective-permute-start.57 = (bf16[512,1024]{1,0:T(8,128)(2,1)}, bf16[512,1024]{1,0:T(8,128)(2,1)}, u32[]{:S(2)}, u32[]{:S(2)}) collective-permute-start(bf16[512,1024]{1,0:T(8,128)(2,1)} %copy-done.68), channel_id=1, source_target_pairs={{0,16},{4,20},{8,24},{12,28},{16,0},{20,4},{24,8},{28,12},{1,17},{... | collective-permute-start | bytes 3145736 | tf_op jit(solution)/shard_map/ppermute | solution.py:27
  102.6 50.1 %collective-permute-start.58 = (bf16[512,1024]{1,0:T(8,128)(2,1)}, bf16[512,1024]{1,0:T(8,128)(2,1)}, u32[]{:S(2)}, u32[]{:S(2)}) collective-permute-start(bf16[512,1024]{1,0:T(8,128)(2,1)} %copy-done.68), channel_id=1, source_target_pairs={{0,4},{4,0},{8,12},{12,8},{16,20},{20,16},{24,28},{28,24},{1,5},{5... | collective-permute-start | bytes 3145736 | tf_op jit(solution)/shard_map/ppermute | solution.py:27
  154.3 47.0 %collective-permute-start.60 = (bf16[1024,512]{1,0:T(8,128)(2,1)}, bf16[1024,512]{1,0:T(8,128)(2,1)}, u32[]{:S(2)}, u32[]{:S(2)}) collective-permute-start(bf16[1024,512]{1,0:T(8,128)(2,1)} %get-tuple-element.2681.refs_0_), channel_id=1, source_target_pairs={{0,16},{4,20},{8,24},{12,28},{16,0},{20,4},{24,8},{28,12},{1,17},{... | collective-permute-start | bytes 3145736 | tf_op jit(solution)/shard_map/ppermute | solution.py:27
  154.3 48.2 %collective-permute-start.61 = (bf16[1024,512]{1,0:T(8,128)(2,1)}, bf16[1024,512]{1,0:T(8,128)(2,1)}, u32[]{:S(2)}, u32[]{:S(2)}) collective-permute-start(bf16[1024,512]{1,0:T(8,128)(2,1)} %get-tuple-element.2681.refs_0_), channel_id=1, source_target_pairs={{0,4},{4,0},{8,12},{12,8},{16,20},{20,16},{24,28},{28,24},{1,5},{5... | collective-permute-start | bytes 3145736 | tf_op jit(solution)/shard_map/ppermute | solution.py:27
  233.4 63.7 %collective-permute-start.65 = (bf16[512,1024]{1,0:T(8,128)(2,1)}, bf16[512,1024]{1,0:T(8,128)(2,1)}, u32[]{:S(2)}, u32[]{:S(2)}) collective-permute-start(bf16[512,1024]{1,0:T(8,128)(2,1)} %copy.77), channel_id=1, source_target_pairs={{0,16},{4,20},{8,24},{12,28},{16,0},{20,4},{24,8},{28,12},{1,17},{... | collective-permute-start | bytes 3145736 | tf_op jit(solution)/shard_map/ppermute | solution.py:27
  241.2 57.1 %collective-permute-start.68 = (bf16[512,1024]{1,0:T(8,128)(2,1)}, bf16[512,1024]{1,0:T(8,128)(2,1)}, u32[]{:S(2)}, u32[]{:S(2)}) collective-permute-start(bf16[512,1024]{1,0:T(8,128)(2,1)} %copy.78), channel_id=1, source_target_pairs={{0,4},{4,0},{8,12},{12,8},{16,20},{20,16},{24,28},{28,24},{1,5},{5... | collective-permute-start | bytes 3145736 | tf_op jit(solution)/shard_map/ppermute | solution.py:27
  242.8 47.0 %collective-permute-start.67 = (bf16[192,2048]{1,0:T(8,128)(2,1)}, bf16[192,2048]{1,0:T(8,128)(2,1)S(1)}, u32[]{:S(2)}, u32[]{:S(2)}) collective-permute-start(bf16[192,2048]{1,0:T(8,128)(2,1)} %shard_map.220.grad_ref), channel_id=1, source_target_pairs={{0,8},{4,12},{8,0},{12,4},{16,24},{20,28},{24,16},{28,20},{1,9},{5... | collective-permute-start | bytes 2359304 | tf_op jit(solution)/shard_map/ppermute | solution.py:27
  318.2 47.6 %collective-permute-start.71 = (bf16[512,1024]{1,0:T(8,128)(2,1)}, bf16[512,1024]{1,0:T(8,128)(2,1)}, u32[]{:S(2)}, u32[]{:S(2)}) collective-permute-start(bf16[512,1024]{1,0:T(8,128)(2,1)} %collective-permute-done.65), channel_id=1, source_target_pairs={{0,4},{4,0},{8,12},{12,8},{16,20},{20,16},{24,28},{28,24},{1,5},{5... | collective-permute-start | bytes 3145736 | tf_op jit(solution)/shard_map/ppermute | solution.py:27
  320.4 45.4 %collective-permute-start.70 = (bf16[512,1024]{1,0:T(8,128)(2,1)}, bf16[512,1024]{1,0:T(8,128)(2,1)}, u32[]{:S(2)}, u32[]{:S(2)}) collective-permute-start(bf16[512,1024]{1,0:T(8,128)(2,1)} %get-tuple-element.2685.refs_0_), channel_id=1, source_target_pairs={{0,4},{4,0},{8,12},{12,8},{16,20},{20,16},{24,28},{28,24},{1,5},{5... | collective-permute-start | bytes 3145736 | tf_op jit(solution)/shard_map/ppermute | solution.py:27
  320.4 45.5 %collective-permute-start.69 = (bf16[512,1024]{1,0:T(8,128)(2,1)}, bf16[512,1024]{1,0:T(8,128)(2,1)}, u32[]{:S(2)}, u32[]{:S(2)}) collective-permute-start(bf16[512,1024]{1,0:T(8,128)(2,1)} %get-tuple-element.2685.refs_0_), channel_id=1, source_target_pairs={{0,16},{4,20},{8,24},{12,28},{16,0},{20,4},{24,8},{28,12},{1,17},{... | collective-permute-start | bytes 3145736 | tf_op jit(solution)/shard_map/ppermute | solution.py:27
  365.9 51.1 %collective-permute-start.73 = (bf16[1024,512]{1,0:T(8,128)(2,1)}, bf16[1024,512]{1,0:T(8,128)(2,1)}, u32[]{:S(2)}, u32[]{:S(2)}) collective-permute-start(bf16[1024,512]{1,0:T(8,128)(2,1)} %copy-done.70), channel_id=1, source_target_pairs={{0,4},{4,0},{8,12},{12,8},{16,20},{20,16},{24,28},{28,24},{1,5},{5... | collective-permute-start | bytes 3145736 | tf_op jit(solution)/shard_map/ppermute | solution.py:27
  367.6 49.4 %collective-permute-start.72 = (bf16[512,1024]{1,0:T(8,128)(2,1)}, bf16[512,1024]{1,0:T(8,128)(2,1)}, u32[]{:S(2)}, u32[]{:S(2)}) collective-permute-start(bf16[512,1024]{1,0:T(8,128)(2,1)} %collective-permute-done.69.refs_1_), channel_id=1, source_target_pairs={{0,4},{4,0},{8,12},{12,8},{16,20},{20,16},{24,28},{28,24},{1,5},{5... | collective-permute-start | bytes 3145736 | tf_op jit(solution)/shard_map/ppermute | solution.py:27
  368.0 80.7 %collective-permute-start.74 = (bf16[1024,512]{1,0:T(8,128)(2,1)}, bf16[1024,512]{1,0:T(8,128)(2,1)}, u32[]{:S(2)}, u32[]{:S(2)}) collective-permute-start(bf16[1024,512]{1,0:T(8,128)(2,1)} %copy-done.70), channel_id=1, source_target_pairs={{0,16},{4,20},{8,24},{12,28},{16,0},{20,4},{24,8},{28,12},{1,17},{... | collective-permute-start | bytes 3145736 | tf_op jit(solution)/shard_map/ppermute | solution.py:27
  455.3 66.0 %collective-permute-start.76 = (bf16[1024,512]{1,0:T(8,128)(2,1)}, bf16[1024,512]{1,0:T(8,128)(2,1)}, u32[]{:S(2)}, u32[]{:S(2)}) collective-permute-start(bf16[1024,512]{1,0:T(8,128)(2,1)} %shard_map.239), channel_id=1, source_target_pairs={{0,4},{4,0},{8,12},{12,8},{16,20},{20,16},{24,28},{28,24},{1,5},{5... | collective-permute-start | bytes 3145736 | tf_op jit(solution)/shard_map/ppermute | solution.py:27
  488.1 65.6 %collective-permute-start.78 = (bf16[1024,512]{1,0:T(8,128)(2,1)}, bf16[1024,512]{1,0:T(8,128)(2,1)}, u32[]{:S(2)}, u32[]{:S(2)}) collective-permute-start(bf16[1024,512]{1,0:T(8,128)(2,1)} %shard_map.243), channel_id=1, source_target_pairs={{0,4},{4,0},{8,12},{12,8},{16,20},{20,16},{24,28},{28,24},{1,5},{5... | collective-permute-start | bytes 3145736 | tf_op jit(solution)/shard_map/ppermute | solution.py:27
  591.4 46.3 %collective-permute-start.80 = (bf16[512,1024]{1,0:T(8,128)(2,1)}, bf16[512,1024]{1,0:T(8,128)(2,1)}, u32[]{:S(2)}, u32[]{:S(2)}) collective-permute-start(bf16[512,1024]{1,0:T(8,128)(2,1)} %get-tuple-element.1932), channel_id=1, source_target_pairs={{0,4},{4,0},{8,12},{12,8},{16,20},{20,16},{24,28},{28,24},{1,5},{5... | collective-permute-start | bytes 3145736 | tf_op jit(solution)/shard_map/ppermute | solution.py:27
  592.0 77.5 %collective-permute-start.81 = (bf16[1024,512]{1,0:T(8,128)(2,1)}, bf16[1024,512]{1,0:T(8,128)(2,1)}, u32[]{:S(2)}, u32[]{:S(2)}) collective-permute-start(bf16[1024,512]{1,0:T(8,128)(2,1)} %get-tuple-element.1947), channel_id=1, source_target_pairs={{0,16},{4,20},{8,24},{12,28},{16,0},{20,4},{24,8},{28,12},{1,17},{... | collective-permute-start | bytes 3145736 | tf_op jit(solution)/shard_map/ppermute | solution.py:27
  637.7 72.3 %collective-permute-start.85 = (bf16[512,1024]{1,0:T(8,128)(2,1)}, bf16[512,1024]{1,0:T(8,128)(2,1)}, u32[]{:S(2)}, u32[]{:S(2)}) collective-permute-start(bf16[512,1024]{1,0:T(8,128)(2,1)} %get-tuple-element.1973), channel_id=1, source_target_pairs={{0,16},{4,20},{8,24},{12,28},{16,0},{20,4},{24,8},{28,12},{1,17},{... | collective-permute-start | bytes 3145736 | tf_op jit(solution)/shard_map/ppermute | solution.py:27
  639.7 70.2 %collective-permute-start.86 = (bf16[512,1024]{1,0:T(8,128)(2,1)}, bf16[512,1024]{1,0:T(8,128)(2,1)}, u32[]{:S(2)}, u32[]{:S(2)}) collective-permute-start(bf16[512,1024]{1,0:T(8,128)(2,1)} %get-tuple-element.1981), channel_id=1, source_target_pairs={{0,4},{4,0},{8,12},{12,8},{16,20},{20,16},{24,28},{28,24},{1,5},{5... | collective-permute-start | bytes 3145736 | tf_op jit(solution)/shard_map/ppermute | solution.py:27
  668.6 72.4 %collective-permute-start.83 = (bf16[512,1024]{1,0:T(8,128)(2,1)}, bf16[512,1024]{1,0:T(8,128)(2,1)}, u32[]{:S(2)}, u32[]{:S(2)}) collective-permute-start(bf16[512,1024]{1,0:T(8,128)(2,1)} %copy-done.85), channel_id=1, source_target_pairs={{0,16},{4,20},{8,24},{12,28},{16,0},{20,4},{24,8},{28,12},{1,17},{... | collective-permute-start | bytes 3145736 | tf_op jit(solution)/shard_map/ppermute | solution.py:27
  676.0 66.2 %collective-permute-start.82 = (bf16[1024,512]{1,0:T(8,128)(2,1)}, bf16[1024,512]{1,0:T(8,128)(2,1)}, u32[]{:S(2)}, u32[]{:S(2)}) collective-permute-start(bf16[1024,512]{1,0:T(8,128)(2,1)} %shard_map.249), channel_id=1, source_target_pairs={{0,4},{4,0},{8,12},{12,8},{16,20},{20,16},{24,28},{28,24},{1,5},{5... | collective-permute-start | bytes 3145736 | tf_op jit(solution)/shard_map/ppermute | solution.py:27
  684.0 56.1 %collective-permute-start.84 = (bf16[192,2048]{1,0:T(8,128)(2,1)}, bf16[192,2048]{1,0:T(8,128)(2,1)S(1)}, u32[]{:S(2)}, u32[]{:S(2)}) collective-permute-start(bf16[192,2048]{1,0:T(8,128)(2,1)} %get-tuple-element.2688), channel_id=1, source_target_pairs={{0,8},{4,12},{8,0},{12,4},{16,24},{20,28},{24,16},{28,20},{1,9},{5... | collective-permute-start | bytes 2359304 | tf_op jit(solution)/shard_map/ppermute | solution.py:27
  747.5 49.0 %collective-permute-start.90 = (bf16[1024,512]{1,0:T(8,128)(2,1)}, bf16[1024,512]{1,0:T(8,128)(2,1)}, u32[]{:S(2)}, u32[]{:S(2)}) collective-permute-start(bf16[1024,512]{1,0:T(8,128)(2,1)} %shard_map.257), channel_id=1, source_target_pairs={{0,16},{4,20},{8,24},{12,28},{16,0},{20,4},{24,8},{28,12},{1,17},{... | collective-permute-start | bytes 3145736 | tf_op jit(solution)/shard_map/ppermute | solution.py:27
  751.2 45.3 %collective-permute-start.89 = (bf16[256,1024]{1,0:T(8,128)(2,1)}, bf16[256,1024]{1,0:T(8,128)(2,1)}, u32[]{:S(2)}, u32[]{:S(2)}) collective-permute-start(bf16[256,1024]{1,0:T(8,128)(2,1)} %get-tuple-element.2068), channel_id=1, source_target_pairs={{0,8},{4,12},{8,0},{12,4},{16,24},{20,28},{24,16},{28,20},{1,9},{5... | collective-permute-start | bytes 1572872 | tf_op jit(solution)/shard_map/ppermute | solution.py:27
  772.7 57.1 %collective-permute-start.92 = (bf16[1024,512]{1,0:T(8,128)(2,1)}, bf16[1024,512]{1,0:T(8,128)(2,1)}, u32[]{:S(2)}, u32[]{:S(2)}) collective-permute-start(bf16[1024,512]{1,0:T(8,128)(2,1)} %shard_map.260), channel_id=1, source_target_pairs={{0,4},{4,0},{8,12},{12,8},{16,20},{20,16},{24,28},{28,24},{1,5},{5... | collective-permute-start | bytes 3145736 | tf_op jit(solution)/shard_map/ppermute | solution.py:27
  777.5 48.5 %collective-permute-start.93 = (bf16[1024,256]{1,0:T(8,128)(2,1)}, bf16[1024,256]{1,0:T(8,128)(2,1)}, u32[]{:S(2)}, u32[]{:S(2)}) collective-permute-start(bf16[1024,256]{1,0:T(8,128)(2,1)} %get-tuple-element.2096), channel_id=1, source_target_pairs={{0,8},{4,12},{8,0},{12,4},{16,24},{20,28},{24,16},{28,20},{1,9},{5... | collective-permute-start | bytes 1572872 | tf_op jit(solution)/shard_map/ppermute | solution.py:27
  800.4 72.6 %collective-permute-start.94 = (bf16[512,1024]{1,0:T(8,128)(2,1)}, bf16[512,1024]{1,0:T(8,128)(2,1)}, u32[]{:S(2)}, u32[]{:S(2)}) collective-permute-start(bf16[512,1024]{1,0:T(8,128)(2,1)} %shard_map.261), channel_id=1, source_target_pairs={{0,16},{4,20},{8,24},{12,28},{16,0},{20,4},{24,8},{28,12},{1,17},{... | collective-permute-start | bytes 3145736 | tf_op jit(solution)/shard_map/ppermute | solution.py:27
  832.8 45.4 %collective-permute-start.96 = (bf16[512,1024]{1,0:T(8,128)(2,1)}, bf16[512,1024]{1,0:T(8,128)(2,1)}, u32[]{:S(2)}, u32[]{:S(2)}) collective-permute-start(bf16[512,1024]{1,0:T(8,128)(2,1)} %get-tuple-element.2152), channel_id=1, source_target_pairs={{0,4},{4,0},{8,12},{12,8},{16,20},{20,16},{24,28},{28,24},{1,5},{5... | collective-permute-start | bytes 3145736 | tf_op jit(solution)/shard_map/ppermute | solution.py:27
  878.2 65.6 %collective-permute-start.100 = (bf16[512,1024]{1,0:T(8,128)(2,1)}, bf16[512,1024]{1,0:T(8,128)(2,1)S(1)}, u32[]{:S(2)}, u32[]{:S(2)}) collective-permute-start(bf16[512,1024]{1,0:T(8,128)(2,1)} %get-tuple-element.2238), channel_id=1, source_target_pairs={{0,16},{4,20},{8,24},{12,28},{16,0},{20,4},{24,8},{28,12},{1,17},{... | collective-permute-start | bytes 3145736 | tf_op jit(solution)/shard_map/ppermute | solution.py:27
  894.9 54.6 %collective-permute-start.99 = (bf16[256,1024]{1,0:T(8,128)(2,1)}, bf16[256,1024]{1,0:T(8,128)(2,1)}, u32[]{:S(2)}, u32[]{:S(2)}) collective-permute-start(bf16[256,1024]{1,0:T(8,128)(2,1)} %get-tuple-element.2236), channel_id=1, source_target_pairs={{0,8},{4,12},{8,0},{12,4},{16,24},{20,28},{24,16},{28,20},{1,9},{5... | collective-permute-start | bytes 1572872 | tf_op jit(solution)/shard_map/ppermute | solution.py:27
  (201 other events, 2529.9 us)

commit v6 on v5

--- a/solution.py
+++ b/solution.py
@@ -1123,19 +1123,19 @@
 
     def second(self):
         def step(sums, biases):
+            for s in reversed(range(len(self.sides) - 1)):
+                sums, biases = self.side(s, sums, biases)
+            return sums, biases
+
+        self.sums, self.biases = self.seq.settle(step, self.sums, self.biases)
+
+    def finish(self):
+        def step(sums, biases):
             sums, other = self.halve(
                 sums, biases, 2, self.mid, lambda value: swap(value, "dp", MID)
             )
             pair = (pick(biases, other, self.mid), pick(other, biases, self.mid))
             return sums, jnp.concatenate(pair)
-
-        self.sums, self.biases = self.seq.settle(step, self.sums, self.biases)
-
-    def finish(self):
-        def step(sums, biases):
-            for s in reversed(range(len(self.sides) - 1)):
-                sums, biases = self.side(s, sums, biases)
-            return sums, biases
 
         sums, biases = self.seq.settle(step, self.sums, self.biases)
         return sums.reshape(self.layers, self.kinds, -1), biases.reshape(2, -1)
@@ -1630,14 +1630,14 @@
     activations = branch.finish(partial(last_stream, order), streams[1], out_shifts[1])
     input_grad = seq.run(lambda value: reorder(value, order, f32, True), grad_stream)
     mix2_own = mixed_finish(mix2_pair)
-    own_finish(0, "down", 0, down1_pair)
-    small_sums.second()
     if early:
         mix1.wait_far()
         mix1.make([0])
     mix1_pair = own_start(mix1.blocks[0], 0)
+    small_sums.second()
+    own_finish(0, "down", 0, down1_pair)
     own_finish(0, "up", 1, up1_pair)
-    seq.tick(6)
+    seq.tick(1)
     norm_owned, bias_both = small_sums.finish()
     mix1_own = mixed_finish(mix1_pair)
     bias_both = bias_both + 0.0 * seq.scalar

time: 986 us -> 980 us (level)
    unnamed x207 -> x199, local copies, waits for them, and re-layouts: 19.6 us -> 19.9 us
  transfers between devices with their start and end apart: 102 -> 102, of which waited for: 52 -> 51; matrix products, arithmetic and copies ran while one was open for 10% -> 10% of each run, Pallas kernels for 41% -> 42%
where the time goes in v6:
time: 980 us; the launch traced here: 969 us
  Pallas kernels  406 us (41%)
  waiting for transfers between devices  316 us (32%)
  starting transfers between devices  99.7 us (10%)
  local copies, waits for them, and re-layouts  86.2 us (9%)
  other arithmetic  54.2 us (6%)
    ppermute x102, waiting for transfers between devices, swap(): return lax.ppermute(value, axis, [(i, i ^ 1 << bit) for i in range(size)])  316 us
    pallas_call x42, Pallas kernels, call(): pl.pallas_call(kernel, grid_spec=pltpu.PrefetchScalarGridSpec(num_scalar_...  278 us
    ppermute x102, starting transfers between devices, swap(): return lax.ppermute(value, axis, [(i, i ^ 1 << bit) for i in range(size)])  99.7 us
    pallas_call x2, Pallas kernels, attention_backward(): pl.pallas_call(attention_back_kernel, grid_spec=pltpu.PrefetchScalarGridS...  35.7 us
    pallas_call x10, Pallas kernels, assemble(): pl.pallas_call(partial(assemble_kernel, axis, window), in_specs=[pl.Block...  27.6 us
    pallas_call x2, Pallas kernels, attention_forward(): pl.pallas_call(attention_kernel, grid_spec=pltpu.PrefetchScalarGridSpec(n...  23.3 us
    unnamed x199, local copies, waits for them, and re-layouts  19.9 us
  transfers between devices with their start and end apart: 102, of which 51 were waited for; matrix products, arithmetic and copies ran while one was open for 10% of the time, Pallas kernels for 42%

profile of v6, /device:TPU:0, one launch (start us, length us, event | category | flops | bytes accessed | tf_op | source)
XLA Modules:
  0.0 969.4 jit_solution(15414245279411182260)
XLA Ops:
  13.4 19.4 %conditional.45 = (bf16[2,1412]{1,0:T(2,128)(2,1)S(1)}, bf16[192,2048]{1,0:T(8,128)(2,1)}) conditional(s32[]{:T(128)} %bitcast.63, () %tuple.588, (s32[]{:T(128)}, bf16[1,1412]{1,0:T(2,128)(2,1)S(1)}, bf16[192,2048]{1,0:T(8,128)(2,1)}) %tuple.600), branch_computations={%region_4.0_spmd, %region_5.6_spmd} | conditional | flops 14121 | bytes 3179722 | solution.py:63
  16.9 13.5 %collective-permute-done.23 = bf16[1,1412]{1,0:T(2,128)(2,1)S(1)} collective-permute-done((bf16[1,1412]{1,0:T(2,128)(2,1)S(1)}, bf16[1,1412]{1,0:T(2,128)(2,1)S(1)}, u32[]{:S(2)}, u32[]{:S(2)}) %collective-permute-start.23) | collective-permute-done | bytes 2856 | tf_op jit(solution)/shard_map/cond/branch_1_fun/ppermute | solution.py:27
  112.6 26.4 %conditional.53 = (bf16[1536,2048]{1,0:T(8,128)(2,1)}) conditional(s32[]{:T(128)} %bitcast.63, () %tuple.624, (bf16[192,2048]{1,0:T(8,128)(2,1)}, bf16[192,2048]{1,0:T(8,128)(2,1)}, bf16[192,2048]{1,0:T(8,128)(2,1)}, bf16[192,2048]{1,0:T(8,128)(2,1)}, bf16[192,2048]{1,0:T(8,128)(2,1)}) %tuple.643), branch_computations={%region_20.21_spmd, %region_21.22_spmd} | conditional | bytes 9437312 | solution.py:63
  113.3 16.9 %collective-permute-done.2.refs_3_ = bf16[192,2048]{1,0:T(8,128)(2,1)S(1)} collective-permute-done((bf16[192,2048]{1,0:T(8,128)(2,1)}, bf16[192,2048]{1,0:T(8,128)(2,1)S(1)}, u32[]{:S(2)}, u32[]{:S(2)}) %collective-permute-start.2) | collective-permute-done | bytes 786464 | tf_op jit(solution)/shard_map/cond/branch_1_fun/ppermute | solution.py:27
  185.1 14.4 %shard_map.229 = (bf16[1536,1024]{1,0:T(8,128)(2,1)}, f32[1536,1024]{1,0:T(8,128)}) custom-call(bf16[1536,2048]{1,0:T(8,128)(2,1)} %get-tuple-element.2680.left_ref.normed_ref, bf16[2048,1024]{1,0:T(8,128)(2,1)S(1)} %shard_map.228.right_ref.up_ref, f32[1,1024]{1,0:T(1,128)S(1)} %get-tuple-element.1608.shift_ref), custom_call_target="tpu_custom_call" | custom-call | tf_op jit(solution)/shard_map/pallas_call | solution.py:762
  208.8 12.8 %collective-permute-done.63 = bf16[256,1024]{0,1:T(8,128)(2,1)} collective-permute-done((bf16[256,1024]{0,1:T(8,128)(2,1)}, bf16[256,1024]{0,1:T(8,128)(2,1)}, u32[]{:S(2)}, u32[]{:S(2)}) %collective-permute-start.63) | collective-permute-done | bytes 524320 | tf_op jit(solution)/shard_map/ppermute | solution.py:27
  267.1 22.6 %conditional.61 = (bf16[192,2048]{1,0:T(8,128)(2,1)S(1)}, bf16[192,2048]{1,0:T(8,128)(2,1)}) conditional(s32[]{:T(128)} %bitcast.63, () %tuple.691, (f32[768,2048]{1,0:T(8,128)}, bf16[768,2048]{1,0:T(8,128)(2,1)}) %tuple.701), branch_computations={%region_36.37_spmd, %region_37.38_spmd} | conditional | flops 2359296 | bytes 9437240 | solution.py:63
  271.5 18.3 %collective-permute-done.27 = bf16[192,2048]{1,0:T(8,128)(2,1)} collective-permute-done((bf16[192,2048]{1,0:T(8,128)(2,1)S(1)}, bf16[192,2048]{1,0:T(8,128)(2,1)}, u32[]{:S(2)}, u32[]{:S(2)}) %collective-permute-start.27) | collective-permute-done | bytes 786464 | tf_op jit(solution)/shard_map/cond/branch_1_fun/ppermute | solution.py:27
  298.3 19.8 %conditional.63 = (bf16[192,2048]{1,0:T(8,128)(2,1)}, bf16[192,2048]{1,0:T(8,128)(2,1)}) conditional(s32[]{:T(128)} %bitcast.63, () %tuple.690, (f32[768,2048]{1,0:T(8,128)}, bf16[768,2048]{1,0:T(8,128)(2,1)}, bf16[192,2048]{1,0:T(8,128)(2,1)}, bf16[192,2048]{1,0:T(8,128)(2,1)S(1)}) %tuple.712), branch_computations={%region_40.41_spmd, %region_41.42_spmd} | conditional | flops 1966080 | bytes 10223712 | solution.py:63
  302.5 15.6 %collective-permute-done.28 = bf16[192,2048]{1,0:T(8,128)(2,1)} collective-permute-done((bf16[192,2048]{1,0:T(8,128)(2,1)S(1)}, bf16[192,2048]{1,0:T(8,128)(2,1)}, u32[]{:S(2)}, u32[]{:S(2)}) %collective-permute-start.28) | collective-permute-done | bytes 786464 | tf_op jit(solution)/shard_map/cond/branch_1_fun/ppermute | solution.py:27
  325.8 39.8 %conditional.64 = (bf16[192,2048]{1,0:T(8,128)(2,1)S(1)}, bf16[192,2048]{1,0:T(8,128)(2,1)}, bf16[192,2048]{1,0:T(8,128)(2,1)}, bf16[192,2048]{1,0:T(8,128)(2,1)...) conditional(s32[]{:T(128)} %bitcast.63, () %tuple.622, ...), branch_computations={%region_42.43_spmd, %region_43.44_spmd} | conditional | bytes 23593304 | solution.py:63
  327.8 15.8 %collective-permute-done.7 = bf16[192,2048]{1,0:T(8,128)(2,1)} collective-permute-done((bf16[192,2048]{1,0:T(8,128)(2,1)S(1)}, bf16[192,2048]{1,0:T(8,128)(2,1)}, u32[]{:S(2)}, u32[]{:S(2)}) %collective-permute-start.7) | collective-permute-done | bytes 786464 | tf_op jit(solution)/shard_map/cond/branch_1_fun/ppermute | solution.py:27
  345.2 13.0 %collective-permute-done.6 = bf16[192,2048]{1,0:T(8,128)(2,1)} collective-permute-done((bf16[192,2048]{1,0:T(8,128)(2,1)S(1)}, bf16[192,2048]{1,0:T(8,128)(2,1)}, u32[]{:S(2)}, u32[]{:S(2)}) %collective-permute-start.6) | collective-permute-done | bytes 786464 | tf_op jit(solution)/shard_map/cond/branch_1_fun/ppermute | solution.py:27
  370.7 32.4 %conditional.65 = (bf16[1536,2048]{1,0:T(8,128)(2,1)S(1)}, bf16[1536,2048]{1,0:T(8,128)(2,1)S(1)}, bf16[2048,1024]{1,0:T(8,128)(2,1)S(1)}) conditional(s32[]{:T(128)} %bitcast.63, () %tuple.621, (bf16[192,2048]{1,0:T(8,128)(2,1)}, bf16[192,2048]{1,0:T(8,128)(2,1)}, bf16[192,2048]{1,0:T(8,128)(2,1)}, bf16[192,2048]{1,0:T(8,128)(2,1)}, ...), branch_computations={%region_44.45_spmd, %region_45.46_spmd} | conditional | bytes 44040640 | solution.py:63
  417.1 12.0 %shard_map.236 = (bf16[4,2,192,256]{3,2,1,0:T(8,128)(2,1)}, bf16[2,768,768]{2,1,0:T(8,128)(2,1)S(1)}, f32[2,768,128]{2,1,0:T(8,128)S(1)}) custom-call(s32[5]{0:T(128)S(1)} %copy-done.102, f32[4,2,192,768]{3,2,1,0:T(8,128)S(1)} %bitcast.166, f32[2,768,128]{2,1,0:T(8,128)S(1)} %copy-done.53, f32[2,768,128]{2,1,0:T(8,128)S(1)} %copy-done.58, ...), custom_call_target="tpu_custom_call" | custom-call | tf_op jit(solution)/shard_map/pallas_call | solution.py:712
  434.0 14.5 %shard_map.238 = (bf16[1536,1024]{1,0:T(8,128)(2,1)}, f32[1536,1024]{1,0:T(8,128)}) custom-call(bf16[1536,2048]{1,0:T(8,128)(2,1)S(1)} %bitcast.171, bf16[2048,1024]{1,0:T(8,128)(2,1)} %shard_map.237.right_ref.up_ref, f32[1,1024]{1,0:T(1,128)S(1)} %get-tuple-element.1800.shift_ref), custom_call_target="tpu_custom_call" | custom-call | tf_op jit(solution)/shard_map/pallas_call | solution.py:762
  460.9 18.5 %shard_map.241 = bf16[4,2,192,768]{3,2,1,0:T(8,128)(2,1)} custom-call(s32[5]{0:T(128)S(1)} %copy-done.102, bf16[2,768,768]{2,1,0:T(8,128)(2,1)S(1)} %get-tuple-element.1784.kept_ref, f32[2,768,128]{2,1,0:T(8,128)S(1)} %get-tuple-element.1785.sums_ref, bf16[4,2,192,256]{3,2,1,0:T(8,128)(2,1)S(1)} %bitcast.169, f32[2,768,128]{2,1,0:T(8,128)S(1)} %copy-done.54, ...), custom_call_target="tpu_custom_call" | custom-call | tf_op jit(solution)/shard_map/pallas_call | solution.py:739
  489.6 12.7 %shard_map.244.second_ref.right_ref = bf16[1536,1024]{1,0:T(8,128)(2,1)} custom-call(bf16[1536,2048]{1,0:T(8,128)(2,1)S(1)} %bitcast.183, bf16[1024,2048]{1,0:T(8,128)(2,1)} %shard_map.242.right_ref, f32[1536,1024]{1,0:T(8,128)} %get-tuple-element.1833.slope_ref), custom_call_target="tpu_custom_call" | custom-call | tf_op jit(solution)/shard_map/pallas_call | solution.py:762
  526.7 27.0 %conditional.67 = (bf16[192,2048]{1,0:T(8,128)(2,1)}, bf16[192,2048]{1,0:T(8,128)(2,1)}, bf16[1024,512]{1,0:T(8,128)(2,1)}, bf16[512,1024]{1,0:T(8,128)(2,1)}, b...) conditional(s32[]{:T(128)} %bitcast.63, () %tuple.756, ...), branch_computations={%region_48.49_spmd, %region_49.52_spmd} | conditional | flops 7862528 | bytes 81009896 | solution.py:63
  556.5 30.5 %conditional.68 = (bf16[192,2048]{1,0:T(8,128)(2,1)}, bf16[192,2048]{1,0:T(8,128)(2,1)}, bf16[512,1024]{1,0:T(8,128)(2,1)}, f32[768,2048]{1,0:T(8,128)}, bf16[768,2048]{1,0:T(8,128)(2,1)}) conditional(s32[]{:T(128)} %bitcast.63, () %tuple.584, (f32[768,2048]{1,0:T(8,128)}, bf16[768,2048]{1,0:T(8,128)(2,1)}, bf16[192,2048]{1,0:T(8,128)(2,1)}, ...), branch_computations={%region_52.53_spmd, %region_53.54_spmd} | conditional | flops 1966080 | bytes 54264044 | solution.py:63
  594.0 43.5 %conditional.69 = (bf16[192,2048]{1,0:T(8,128)(2,1)}, bf16[192,2048]{1,0:T(8,128)(2,1)}, bf16[192,2048]{1,0:T(8,128)(2,1)S(1)}, bf16[192,2048]{1,0:T(8,128)(2,1)...) conditional(s32[]{:T(128)} %bitcast.63, () %tuple.769, ...), branch_computations={%region_54.55_spmd, %region_55.56_spmd} | conditional | flops 2359296 | bytes 23593216 | solution.py:63
  595.6 17.1 %collective-permute-done.34 = bf16[192,2048]{1,0:T(8,128)(2,1)} collective-permute-done((bf16[192,2048]{1,0:T(8,128)(2,1)S(1)}, bf16[192,2048]{1,0:T(8,128)(2,1)}, u32[]{:S(2)}, u32[]{:S(2)}) %collective-permute-start.34) | collective-permute-done | bytes 786464 | tf_op jit(solution)/shard_map/cond/branch_1_fun/ppermute | solution.py:27
  617.3 15.5 %collective-permute-done.35 = bf16[192,2048]{1,0:T(8,128)(2,1)} collective-permute-done((bf16[192,2048]{1,0:T(8,128)(2,1)S(1)}, bf16[192,2048]{1,0:T(8,128)(2,1)}, u32[]{:S(2)}, u32[]{:S(2)}) %collective-permute-start.35) | collective-permute-done | bytes 786464 | tf_op jit(solution)/shard_map/cond/branch_1_fun/ppermute | solution.py:27
  641.2 26.4 %conditional.70 = (bf16[1536,2048]{1,0:T(8,128)(2,1)S(1)}, bf16[512,1024]{1,0:T(8,128)(2,1)S(1)}) conditional(s32[]{:T(128)} %bitcast.63, () %tuple.778, (bf16[192,2048]{1,0:T(8,128)(2,1)}, bf16[192,2048]{1,0:T(8,128)(2,1)S(1)}, bf16[192,2048]{1,0:T(8,128)(2,1)}, bf16[192,2048]{1,0:T(8,128)(2,1)}, bf16[192,2048]{1,0:T(8,128)(2,1)}, ...), branch_computations={%region_56.57_spmd, %region_57.58_spmd} | conditional | bytes 15728832 | solution.py:63
  642.1 18.3 %collective-permute-done.19.refs_3_ = bf16[192,2048]{1,0:T(8,128)(2,1)S(1)} collective-permute-done((bf16[192,2048]{1,0:T(8,128)(2,1)}, bf16[192,2048]{1,0:T(8,128)(2,1)S(1)}, u32[]{:S(2)}, u32[]{:S(2)}) %collective-permute-start.19) | collective-permute-done | bytes 786464 | tf_op jit(solution)/shard_map/cond/branch_1_fun/ppermute | solution.py:27
  689.6 17.2 %shard_map.252 = bf16[4,2,192,768]{3,2,1,0:T(8,128)(2,1)} custom-call(s32[5]{0:T(128)S(1)} %copy-done.102, bf16[2,768,768]{2,1,0:T(8,128)(2,1)S(1)} %copy-done.2, f32[2,768,128]{2,1,0:T(8,128)S(1)} %copy-done.10, bf16[4,2,192,256]{3,2,1,0:T(8,128)(2,1)S(1)} %bitcast.168, f32[2,768,128]{2,1,0:T(8,128)S(1)} %copy-done.55, f32[2,768,128]{2,1,0:T(8,128)S(1)} %copy-done.59, ...), custom_call_target="tpu_custom_call" | custom-call | tf_op jit(solution)/shard_map/pallas_call | solution.py:739
  709.8 13.1 %shard_map.253.right_ref.second_ref = bf16[1536,1024]{1,0:T(8,128)(2,1)S(1)} custom-call(bf16[1536,2048]{1,0:T(8,128)(2,1)} %copy-done.21, bf16[1024,2048]{1,0:T(8,128)(2,1)} %shard_map.231.down_ref.right_ref, f32[1536,1024]{1,0:T(8,128)} %get-tuple-element.1985.slope_ref), custom_call_target="tpu_custom_call" | custom-call | tf_op jit(solution)/shard_map/pallas_call | solution.py:762
  801.8 24.1 %conditional.75 = (bf16[192,2048]{1,0:T(8,128)(2,1)}, bf16[192,2048]{1,0:T(8,128)(2,1)}, bf16[512,1024]{1,0:T(8,128)(2,1)}, f32[768]{0:T(1024)S(1)}, f32[1024]{0:T(1024)S(1)}) conditional(s32[]{:T(128)} %bitcast.63, () %tuple.839, (f32[768,2048]{1,0:T(8,128)}, bf16[768,2048]{1,0:T(8,128)(2,1)}, bf16[1536,2048]{1,0:T(8,128)(2,1)}, ...), branch_computations={%region_66.67_spmd, %region_67.70_spmd} | conditional | flops 7862528 | bytes 49552520 | solution.py:63
  813.0 12.9 %collective-permute-done.39 = bf16[192,2048]{1,0:T(8,128)(2,1)} collective-permute-done((bf16[192,2048]{1,0:T(8,128)(2,1)}, bf16[192,2048]{1,0:T(8,128)(2,1)}, u32[]{:S(2)}, u32[]{:S(2)}) %collective-permute-start.39) | collective-permute-done | bytes 786464 | tf_op jit(solution)/shard_map/cond/branch_1_fun/ppermute | solution.py:27
  833.0 32.7 %conditional.76 = (bf16[192,2048]{1,0:T(8,128)(2,1)}, bf16[192,2048]{1,0:T(8,128)(2,1)}, bf16[512,1024]{1,0:T(8,128)(2,1)}, bf16[1024,512]{1,0:T(8,128)(2,1)}, bf16[512,1024]{1,0:T(8,128)(2,1)}) conditional(s32[]{:T(128)} %bitcast.63, () %tuple.838, (f32[768,2048]{1,0:T(8,128)}, bf16[768,2048]{1,0:T(8,128)(2,1)}, bf16[192,2048]{1,0:T(8,128)(2,1)}, ...), branch_computations={%region_70.71_spmd, %region_71.72_spmd} | conditional | flops 1966080 | bytes 60555508 | solution.py:63
  853.0 12.7 %collective-permute-done.40 = bf16[192,2048]{1,0:T(8,128)(2,1)} collective-permute-done((bf16[192,2048]{1,0:T(8,128)(2,1)}, bf16[192,2048]{1,0:T(8,128)(2,1)}, u32[]{:S(2)}, u32[]{:S(2)}) %collective-permute-start.40) | collective-permute-done | bytes 786464 | tf_op jit(solution)/shard_map/cond/branch_1_fun/ppermute | solution.py:27
  932.2 13.0 %conditional.83 = (f32[6,1,2,1,64]{4,3,2,1,0:T(1,128)S(1)}, f32[3584]{0:T(1024)S(1)}) conditional(s32[]{:T(128)} %bitcast.63, () %tuple.889, (f32[6,2,2,1,64]{4,3,2,1,0:T(1,128)S(1)}, f32[3584]{0:T(1024)S(1)}) %conditional.80), branch_computations={%region_84.85_spmd, %region_85.86_spmd} | conditional | flops 8704 | bytes 181304 | solution.py:63
  (756 shorter events, 803.3 us)
Async XLA Ops:
  71.9 67.0 %collective-permute-start.56 = (bf16[1024,256]{1,0:T(8,128)(2,1)}, bf16[1024,256]{1,0:T(8,128)(2,1)}, u32[]{:S(2)}, u32[]{:S(2)}) collective-permute-start(bf16[1024,256]{1,0:T(8,128)(2,1)} %copy-done.86), channel_id=1, source_target_pairs={{0,8},{4,12},{8,0},{12,4},{16,24},{20,28},{24,16},{28,20},{1,9},{5... | collective-permute-start | bytes 1572872 | tf_op jit(solution)/shard_map/ppermute | solution.py:27
  102.5 48.9 %collective-permute-start.57 = (bf16[512,1024]{1,0:T(8,128)(2,1)}, bf16[512,1024]{1,0:T(8,128)(2,1)}, u32[]{:S(2)}, u32[]{:S(2)}) collective-permute-start(bf16[512,1024]{1,0:T(8,128)(2,1)} %copy-done.66), channel_id=1, source_target_pairs={{0,16},{4,20},{8,24},{12,28},{16,0},{20,4},{24,8},{28,12},{1,17},{... | collective-permute-start | bytes 3145736 | tf_op jit(solution)/shard_map/ppermute | solution.py:27
  102.5 50.1 %collective-permute-start.58 = (bf16[512,1024]{1,0:T(8,128)(2,1)}, bf16[512,1024]{1,0:T(8,128)(2,1)}, u32[]{:S(2)}, u32[]{:S(2)}) collective-permute-start(bf16[512,1024]{1,0:T(8,128)(2,1)} %copy-done.66), channel_id=1, source_target_pairs={{0,4},{4,0},{8,12},{12,8},{16,20},{20,16},{24,28},{28,24},{1,5},{5... | collective-permute-start | bytes 3145736 | tf_op jit(solution)/shard_map/ppermute | solution.py:27
  154.2 47.0 %collective-permute-start.60 = (bf16[1024,512]{1,0:T(8,128)(2,1)}, bf16[1024,512]{1,0:T(8,128)(2,1)}, u32[]{:S(2)}, u32[]{:S(2)}) collective-permute-start(bf16[1024,512]{1,0:T(8,128)(2,1)} %get-tuple-element.2681.refs_0_), channel_id=1, source_target_pairs={{0,16},{4,20},{8,24},{12,28},{16,0},{20,4},{24,8},{28,12},{1,17},{... | collective-permute-start | bytes 3145736 | tf_op jit(solution)/shard_map/ppermute | solution.py:27
  154.2 48.2 %collective-permute-start.61 = (bf16[1024,512]{1,0:T(8,128)(2,1)}, bf16[1024,512]{1,0:T(8,128)(2,1)}, u32[]{:S(2)}, u32[]{:S(2)}) collective-permute-start(bf16[1024,512]{1,0:T(8,128)(2,1)} %get-tuple-element.2681.refs_0_), channel_id=1, source_target_pairs={{0,4},{4,0},{8,12},{12,8},{16,20},{20,16},{24,28},{28,24},{1,5},{5... | collective-permute-start | bytes 3145736 | tf_op jit(solution)/shard_map/ppermute | solution.py:27
  233.4 63.7 %collective-permute-start.65 = (bf16[512,1024]{1,0:T(8,128)(2,1)}, bf16[512,1024]{1,0:T(8,128)(2,1)}, u32[]{:S(2)}, u32[]{:S(2)}) collective-permute-start(bf16[512,1024]{1,0:T(8,128)(2,1)} %copy.77), channel_id=1, source_target_pairs={{0,16},{4,20},{8,24},{12,28},{16,0},{20,4},{24,8},{28,12},{1,17},{... | collective-permute-start | bytes 3145736 | tf_op jit(solution)/shard_map/ppermute | solution.py:27
  241.2 57.1 %collective-permute-start.68 = (bf16[512,1024]{1,0:T(8,128)(2,1)}, bf16[512,1024]{1,0:T(8,128)(2,1)}, u32[]{:S(2)}, u32[]{:S(2)}) collective-permute-start(bf16[512,1024]{1,0:T(8,128)(2,1)} %copy.78), channel_id=1, source_target_pairs={{0,4},{4,0},{8,12},{12,8},{16,20},{20,16},{24,28},{28,24},{1,5},{5... | collective-permute-start | bytes 3145736 | tf_op jit(solution)/shard_map/ppermute | solution.py:27
  242.7 47.0 %collective-permute-start.67 = (bf16[192,2048]{1,0:T(8,128)(2,1)}, bf16[192,2048]{1,0:T(8,128)(2,1)S(1)}, u32[]{:S(2)}, u32[]{:S(2)}) collective-permute-start(bf16[192,2048]{1,0:T(8,128)(2,1)} %shard_map.220.grad_ref), channel_id=1, source_target_pairs={{0,8},{4,12},{8,0},{12,4},{16,24},{20,28},{24,16},{28,20},{1,9},{5... | collective-permute-start | bytes 2359304 | tf_op jit(solution)/shard_map/ppermute | solution.py:27
  318.1 47.6 %collective-permute-start.71 = (bf16[512,1024]{1,0:T(8,128)(2,1)}, bf16[512,1024]{1,0:T(8,128)(2,1)}, u32[]{:S(2)}, u32[]{:S(2)}) collective-permute-start(bf16[512,1024]{1,0:T(8,128)(2,1)} %collective-permute-done.65), channel_id=1, source_target_pairs={{0,4},{4,0},{8,12},{12,8},{16,20},{20,16},{24,28},{28,24},{1,5},{5... | collective-permute-start | bytes 3145736 | tf_op jit(solution)/shard_map/ppermute | solution.py:27
  320.3 45.4 %collective-permute-start.70 = (bf16[512,1024]{1,0:T(8,128)(2,1)}, bf16[512,1024]{1,0:T(8,128)(2,1)}, u32[]{:S(2)}, u32[]{:S(2)}) collective-permute-start(bf16[512,1024]{1,0:T(8,128)(2,1)} %get-tuple-element.2685.refs_0_), channel_id=1, source_target_pairs={{0,4},{4,0},{8,12},{12,8},{16,20},{20,16},{24,28},{28,24},{1,5},{5... | collective-permute-start | bytes 3145736 | tf_op jit(solution)/shard_map/ppermute | solution.py:27
  320.4 45.5 %collective-permute-start.69 = (bf16[512,1024]{1,0:T(8,128)(2,1)}, bf16[512,1024]{1,0:T(8,128)(2,1)}, u32[]{:S(2)}, u32[]{:S(2)}) collective-permute-start(bf16[512,1024]{1,0:T(8,128)(2,1)} %get-tuple-element.2685.refs_0_), channel_id=1, source_target_pairs={{0,16},{4,20},{8,24},{12,28},{16,0},{20,4},{24,8},{28,12},{1,17},{... | collective-permute-start | bytes 3145736 | tf_op jit(solution)/shard_map/ppermute | solution.py:27
  365.9 51.1 %collective-permute-start.73 = (bf16[1024,512]{1,0:T(8,128)(2,1)}, bf16[1024,512]{1,0:T(8,128)(2,1)}, u32[]{:S(2)}, u32[]{:S(2)}) collective-permute-start(bf16[1024,512]{1,0:T(8,128)(2,1)} %copy-done.68), channel_id=1, source_target_pairs={{0,4},{4,0},{8,12},{12,8},{16,20},{20,16},{24,28},{28,24},{1,5},{5... | collective-permute-start | bytes 3145736 | tf_op jit(solution)/shard_map/ppermute | solution.py:27
  367.6 49.4 %collective-permute-start.72 = (bf16[512,1024]{1,0:T(8,128)(2,1)}, bf16[512,1024]{1,0:T(8,128)(2,1)}, u32[]{:S(2)}, u32[]{:S(2)}) collective-permute-start(bf16[512,1024]{1,0:T(8,128)(2,1)} %collective-permute-done.69.refs_1_), channel_id=1, source_target_pairs={{0,4},{4,0},{8,12},{12,8},{16,20},{20,16},{24,28},{28,24},{1,5},{5... | collective-permute-start | bytes 3145736 | tf_op jit(solution)/shard_map/ppermute | solution.py:27
  367.9 80.7 %collective-permute-start.74 = (bf16[1024,512]{1,0:T(8,128)(2,1)}, bf16[1024,512]{1,0:T(8,128)(2,1)}, u32[]{:S(2)}, u32[]{:S(2)}) collective-permute-start(bf16[1024,512]{1,0:T(8,128)(2,1)} %copy-done.68), channel_id=1, source_target_pairs={{0,16},{4,20},{8,24},{12,28},{16,0},{20,4},{24,8},{28,12},{1,17},{... | collective-permute-start | bytes 3145736 | tf_op jit(solution)/shard_map/ppermute | solution.py:27
  455.2 65.9 %collective-permute-start.76 = (bf16[1024,512]{1,0:T(8,128)(2,1)}, bf16[1024,512]{1,0:T(8,128)(2,1)}, u32[]{:S(2)}, u32[]{:S(2)}) collective-permute-start(bf16[1024,512]{1,0:T(8,128)(2,1)} %shard_map.239), channel_id=1, source_target_pairs={{0,4},{4,0},{8,12},{12,8},{16,20},{20,16},{24,28},{28,24},{1,5},{5... | collective-permute-start | bytes 3145736 | tf_op jit(solution)/shard_map/ppermute | solution.py:27
  488.0 65.7 %collective-permute-start.78 = (bf16[1024,512]{1,0:T(8,128)(2,1)}, bf16[1024,512]{1,0:T(8,128)(2,1)}, u32[]{:S(2)}, u32[]{:S(2)}) collective-permute-start(bf16[1024,512]{1,0:T(8,128)(2,1)} %shard_map.243), channel_id=1, source_target_pairs={{0,4},{4,0},{8,12},{12,8},{16,20},{20,16},{24,28},{28,24},{1,5},{5... | collective-permute-start | bytes 3145736 | tf_op jit(solution)/shard_map/ppermute | solution.py:27
  591.3 46.2 %collective-permute-start.80 = (bf16[512,1024]{1,0:T(8,128)(2,1)}, bf16[512,1024]{1,0:T(8,128)(2,1)}, u32[]{:S(2)}, u32[]{:S(2)}) collective-permute-start(bf16[512,1024]{1,0:T(8,128)(2,1)} %get-tuple-element.1932), channel_id=1, source_target_pairs={{0,4},{4,0},{8,12},{12,8},{16,20},{20,16},{24,28},{28,24},{1,5},{5... | collective-permute-start | bytes 3145736 | tf_op jit(solution)/shard_map/ppermute | solution.py:27
  591.9 77.5 %collective-permute-start.81 = (bf16[1024,512]{1,0:T(8,128)(2,1)}, bf16[1024,512]{1,0:T(8,128)(2,1)}, u32[]{:S(2)}, u32[]{:S(2)}) collective-permute-start(bf16[1024,512]{1,0:T(8,128)(2,1)} %get-tuple-element.1947), channel_id=1, source_target_pairs={{0,16},{4,20},{8,24},{12,28},{16,0},{20,4},{24,8},{28,12},{1,17},{... | collective-permute-start | bytes 3145736 | tf_op jit(solution)/shard_map/ppermute | solution.py:27
  637.6 72.3 %collective-permute-start.85 = (bf16[512,1024]{1,0:T(8,128)(2,1)}, bf16[512,1024]{1,0:T(8,128)(2,1)}, u32[]{:S(2)}, u32[]{:S(2)}) collective-permute-start(bf16[512,1024]{1,0:T(8,128)(2,1)} %get-tuple-element.1973), channel_id=1, source_target_pairs={{0,16},{4,20},{8,24},{12,28},{16,0},{20,4},{24,8},{28,12},{1,17},{... | collective-permute-start | bytes 3145736 | tf_op jit(solution)/shard_map/ppermute | solution.py:27
  639.6 70.2 %collective-permute-start.86 = (bf16[512,1024]{1,0:T(8,128)(2,1)}, bf16[512,1024]{1,0:T(8,128)(2,1)}, u32[]{:S(2)}, u32[]{:S(2)}) collective-permute-start(bf16[512,1024]{1,0:T(8,128)(2,1)} %get-tuple-element.1981), channel_id=1, source_target_pairs={{0,4},{4,0},{8,12},{12,8},{16,20},{20,16},{24,28},{28,24},{1,5},{5... | collective-permute-start | bytes 3145736 | tf_op jit(solution)/shard_map/ppermute | solution.py:27
  668.5 72.4 %collective-permute-start.83 = (bf16[512,1024]{1,0:T(8,128)(2,1)}, bf16[512,1024]{1,0:T(8,128)(2,1)}, u32[]{:S(2)}, u32[]{:S(2)}) collective-permute-start(bf16[512,1024]{1,0:T(8,128)(2,1)} %copy-done.81), channel_id=1, source_target_pairs={{0,16},{4,20},{8,24},{12,28},{16,0},{20,4},{24,8},{28,12},{1,17},{... | collective-permute-start | bytes 3145736 | tf_op jit(solution)/shard_map/ppermute | solution.py:27
  675.9 66.2 %collective-permute-start.82 = (bf16[1024,512]{1,0:T(8,128)(2,1)}, bf16[1024,512]{1,0:T(8,128)(2,1)}, u32[]{:S(2)}, u32[]{:S(2)}) collective-permute-start(bf16[1024,512]{1,0:T(8,128)(2,1)} %shard_map.249), channel_id=1, source_target_pairs={{0,4},{4,0},{8,12},{12,8},{16,20},{20,16},{24,28},{28,24},{1,5},{5... | collective-permute-start | bytes 3145736 | tf_op jit(solution)/shard_map/ppermute | solution.py:27
  683.9 56.1 %collective-permute-start.84 = (bf16[192,2048]{1,0:T(8,128)(2,1)}, bf16[192,2048]{1,0:T(8,128)(2,1)S(1)}, u32[]{:S(2)}, u32[]{:S(2)}) collective-permute-start(bf16[192,2048]{1,0:T(8,128)(2,1)} %get-tuple-element.2688), channel_id=1, source_target_pairs={{0,8},{4,12},{8,0},{12,4},{16,24},{20,28},{24,16},{28,20},{1,9},{5... | collective-permute-start | bytes 2359304 | tf_op jit(solution)/shard_map/ppermute | solution.py:27
  747.4 49.1 %collective-permute-start.90 = (bf16[1024,512]{1,0:T(8,128)(2,1)}, bf16[1024,512]{1,0:T(8,128)(2,1)}, u32[]{:S(2)}, u32[]{:S(2)}) collective-permute-start(bf16[1024,512]{1,0:T(8,128)(2,1)} %shard_map.257), channel_id=1, source_target_pairs={{0,16},{4,20},{8,24},{12,28},{16,0},{20,4},{24,8},{28,12},{1,17},{... | collective-permute-start | bytes 3145736 | tf_op jit(solution)/shard_map/ppermute | solution.py:27
  751.1 45.4 %collective-permute-start.89 = (bf16[256,1024]{1,0:T(8,128)(2,1)}, bf16[256,1024]{1,0:T(8,128)(2,1)}, u32[]{:S(2)}, u32[]{:S(2)}) collective-permute-start(bf16[256,1024]{1,0:T(8,128)(2,1)} %get-tuple-element.2068), channel_id=1, source_target_pairs={{0,8},{4,12},{8,0},{12,4},{16,24},{20,28},{24,16},{28,20},{1,9},{5... | collective-permute-start | bytes 1572872 | tf_op jit(solution)/shard_map/ppermute | solution.py:27
  772.5 57.2 %collective-permute-start.92 = (bf16[1024,512]{1,0:T(8,128)(2,1)}, bf16[1024,512]{1,0:T(8,128)(2,1)}, u32[]{:S(2)}, u32[]{:S(2)}) collective-permute-start(bf16[1024,512]{1,0:T(8,128)(2,1)} %shard_map.260), channel_id=1, source_target_pairs={{0,4},{4,0},{8,12},{12,8},{16,20},{20,16},{24,28},{28,24},{1,5},{5... | collective-permute-start | bytes 3145736 | tf_op jit(solution)/shard_map/ppermute | solution.py:27
  777.5 48.4 %collective-permute-start.93 = (bf16[1024,256]{1,0:T(8,128)(2,1)}, bf16[1024,256]{1,0:T(8,128)(2,1)}, u32[]{:S(2)}, u32[]{:S(2)}) collective-permute-start(bf16[1024,256]{1,0:T(8,128)(2,1)} %get-tuple-element.2096), channel_id=1, source_target_pairs={{0,8},{4,12},{8,0},{12,4},{16,24},{20,28},{24,16},{28,20},{1,9},{5... | collective-permute-start | bytes 1572872 | tf_op jit(solution)/shard_map/ppermute | solution.py:27
  800.4 72.6 %collective-permute-start.94 = (bf16[512,1024]{1,0:T(8,128)(2,1)}, bf16[512,1024]{1,0:T(8,128)(2,1)}, u32[]{:S(2)}, u32[]{:S(2)}) collective-permute-start(bf16[512,1024]{1,0:T(8,128)(2,1)} %shard_map.261), channel_id=1, source_target_pairs={{0,16},{4,20},{8,24},{12,28},{16,0},{20,4},{24,8},{28,12},{1,17},{... | collective-permute-start | bytes 3145736 | tf_op jit(solution)/shard_map/ppermute | solution.py:27
  832.7 45.5 %collective-permute-start.96 = (bf16[512,1024]{1,0:T(8,128)(2,1)}, bf16[512,1024]{1,0:T(8,128)(2,1)}, u32[]{:S(2)}, u32[]{:S(2)}) collective-permute-start(bf16[512,1024]{1,0:T(8,128)(2,1)} %get-tuple-element.2152), channel_id=1, source_target_pairs={{0,4},{4,0},{8,12},{12,8},{16,20},{20,16},{24,28},{28,24},{1,5},{5... | collective-permute-start | bytes 3145736 | tf_op jit(solution)/shard_map/ppermute | solution.py:27
  878.2 46.5 %collective-permute-start.97 = (bf16[512,1024]{1,0:T(8,128)(2,1)}, bf16[512,1024]{1,0:T(8,128)(2,1)S(1)}, u32[]{:S(2)}, u32[]{:S(2)}) collective-permute-start(bf16[512,1024]{1,0:T(8,128)(2,1)} %get-tuple-element.2208), channel_id=1, source_target_pairs={{0,16},{4,20},{8,24},{12,28},{16,0},{20,4},{24,8},{28,12},{1,17},{... | collective-permute-start | bytes 3145736 | tf_op jit(solution)/shard_map/ppermute | solution.py:27
  887.0 58.2 %collective-permute-start.100 = (bf16[1024,256]{1,0:T(8,128)(2,1)}, bf16[1024,256]{1,0:T(8,128)(2,1)}, u32[]{:S(2)}, u32[]{:S(2)}) collective-permute-start(bf16[1024,256]{1,0:T(8,128)(2,1)} %get-tuple-element.2246), channel_id=1, source_target_pairs={{0,8},{4,12},{8,0},{12,4},{16,24},{20,28},{24,16},{28,20},{1,9},{5... | collective-permute-start | bytes 1572872 | tf_op jit(solution)/shard_map/ppermute | solution.py:27
  894.9 52.9 %collective-permute-start.99 = (bf16[256,1024]{1,0:T(8,128)(2,1)}, bf16[256,1024]{1,0:T(8,128)(2,1)}, u32[]{:S(2)}, u32[]{:S(2)}) collective-permute-start(bf16[256,1024]{1,0:T(8,128)(2,1)} %get-tuple-element.2244), channel_id=1, source_target_pairs={{0,8},{4,12},{8,0},{12,4},{16,24},{20,28},{24,16},{28,20},{1,9},{5... | collective-permute-start | bytes 1572872 | tf_op jit(solution)/shard_map/ppermute | solution.py:27
  (197 other events, 2510.2 us)
